TPU v7x, 128 devices: a whole 4x4x4 slice. The times are simulated.
128 devices in a mesh: gx: 16 (over y_hi, x, core), gy: 8 (over y_lo, z).
Axes of the slice: x: 4, y: 4 (y_hi: 2, y_lo: 2; y = y_hi * 2 + y_lo), z: 4, core: 2. Of those that a mesh axis runs over, the one named last changes fastest.
Arguments:
- right_side: float32 [3, 16, 128, 1024], P(None, None, 'gx', 'gy'), may hold values from -6 to 6
- density: int32 [16, 128, 1024], P(None, 'gx', 'gy'), may hold values from 0 to 15
- fixed_mask: int32 [16, 128, 1024], P(None, 'gx', 'gy'), may hold values 0 or 1
Outputs:
- correction: float32 [3, 16, 128, 1024], P(None, None, 'gx', 'gy')
All inputs are finite; a program needn't handle non-finite values. No bound on the sum of `fixed_mask` on one device may be relied on, other than what follows from the above.
Results may differ from a plain program's by a relative error of at most 0.0001.
Values sent between devices are 32-bit elements; how exact they have to be, the bound alone decides.
No kernel may reach another device: no remote copies, remote signals or barrier semaphores. Data moves between devices by JAX's collectives and lax.ppermute only.
A program may use at most 64 MiB of HBM per device.

v0:
```python
import math

import jax
import jax.numpy as jnp
import numpy as np
from jax import lax
from jax.sharding import PartitionSpec as P

LEVELS = 4
Q = 16


JACOBI_WEIGHT = 0.6
SOFT_FLOOR = 0.1


def with_halo(cells, sides, width):
    for axis, dim in sides:
        count = lax.axis_size(axis)
        ends = count - 1
        head = lax.slice_in_dim(cells, 0, width, axis=dim)
        tail = lax.slice_in_dim(cells, cells.shape[dim] - width, cells.shape[dim], axis=dim)
        cells = jnp.concatenate(
            [
                lax.ppermute(tail, axis, [(i, (i + 1) % count) for i in range(ends)]),
                cells,
                lax.ppermute(head, axis, [((i + 1) % count, i) for i in range(ends)]),
            ],
            axis=dim,
        )
    return cells


def corner_bits(corner):
    return (corner >> 2 & 1, corner >> 1 & 1, corner & 1)


def element_matrix():
    poisson = 0.3
    lame_first = poisson / ((1.0 + poisson) * (1.0 - 2.0 * poisson))
    shear_mod = 0.5 / (1.0 + poisson)
    elastic = np.zeros((6, 6))
    elastic[:3, :3] = lame_first
    for direction in range(3):
        elastic[direction, direction] = lame_first + 2.0 * shear_mod
        elastic[direction + 3, direction + 3] = shear_mod
    points = [0.5 - 0.5 / math.sqrt(3.0), 0.5 + 0.5 / math.sqrt(3.0)]
    matrix = np.zeros((24, 24))
    for point_z in points:
        for point_x in points:
            for point_y in points:
                coords = (point_z, point_x, point_y)
                strain = np.zeros((6, 24))
                for corner in range(8):
                    offsets = corner_bits(corner)
                    gradient = []
                    for direction in range(3):
                        product = 1.0
                        for second in range(3):
                            if second == direction:
                                factor = 1.0 if offsets[second] else -1.0
                            else:
                                factor = coords[second] if offsets[second] else 1.0 - coords[second]
                            product = product * factor
                        gradient.append(product)
                    column = 3 * corner
                    strain[0, column] = gradient[0]
                    strain[1, column + 1] = gradient[1]
                    strain[2, column + 2] = gradient[2]
                    strain[3, column] = gradient[1]
                    strain[3, column + 1] = gradient[0]
                    strain[4, column + 1] = gradient[2]
                    strain[4, column + 2] = gradient[1]
                    strain[5, column] = gradient[2]
                    strain[5, column + 2] = gradient[0]
                matrix = matrix + 0.125 * (strain.T @ elastic @ strain)
    return matrix.reshape(8, 3, 8, 3)


def young_modulus(density):
    return SOFT_FLOOR + (1.0 - SOFT_FLOOR) * (density.astype(jnp.float32) / (Q - 1)) ** 3


def level_coefficient(grown_scale, pad_low, spacing, anchor_x, anchor_y, total_x, total_y):
    layers, span_x, span_y = grown_scale.shape
    if spacing == 1:
        coarse = grown_scale[:, : span_x - 1, : span_y - 1]
    else:
        padded = jnp.pad(grown_scale, ((0, spacing), (0, 0), (0, 0)))
        coarse = 0.0
        for corner in range(8):
            offset_z, offset_x, offset_y = corner_bits(corner)
            coarse = (
                coarse
                + padded[
                    offset_z * spacing : offset_z * spacing + layers,
                    offset_x * spacing : offset_x * spacing + span_x - spacing,
                    offset_y * spacing : offset_y * spacing + span_y - spacing,
                ]
            )
        coarse = 0.125 * coarse
    cell_z = jnp.arange(layers, dtype=jnp.int32)
    cell_x = anchor_x - pad_low + jnp.arange(span_x - spacing, dtype=jnp.int32)
    cell_y = anchor_y - pad_low + jnp.arange(span_y - spacing, dtype=jnp.int32)
    inside = (
        (cell_z <= layers - 1 - spacing)[:, None, None]
        & ((cell_x >= 0) & (cell_x <= total_x - 1 - spacing))[None, :, None]
        & ((cell_y >= 0) & (cell_y <= total_y - 1 - spacing))[None, None, :]
    )
    return jnp.where(inside, coarse, 0.0)


def diagonal_terms(coefficient, pad_low, spacing, span_x, span_y, element_table):
    layers = coefficient.shape[0]
    scaled = jnp.pad(coefficient, ((spacing, 0), (0, 0), (0, 0)))
    totals = [0.0, 0.0, 0.0]
    for corner in range(8):
        offset_z, offset_x, offset_y = corner_bits(corner)
        weight = scaled[
            spacing - spacing * offset_z : spacing - spacing * offset_z + layers,
            pad_low - spacing * offset_x : pad_low - spacing * offset_x + span_x,
            pad_low - spacing * offset_y : pad_low - spacing * offset_y + span_y,
        ]
        for out_comp in range(3):
            totals[out_comp] = (
                totals[out_comp] + float(element_table[corner, out_comp, corner, out_comp]) * weight
            )
    return spacing * jnp.stack(totals)


def stiffness(values, pad_field, coefficient, pad_low, spacing, margin, element_table):
    layers = values.shape[1]
    span_x = values.shape[2] - 2 * pad_field + 2 * margin
    span_y = values.shape[3] - 2 * pad_field + 2 * margin
    lifted = jnp.pad(values, ((0, 0), (spacing, spacing), (0, 0), (0, 0)))
    scaled = jnp.pad(coefficient, ((spacing, 0), (0, 0), (0, 0)))
    totals = [0.0, 0.0, 0.0]
    for corner in range(8):
        offset_z, offset_x, offset_y = corner_bits(corner)
        low_x = pad_low - margin - spacing * offset_x
        low_y = pad_low - margin - spacing * offset_y
        weight = scaled[
            spacing - spacing * offset_z : spacing - spacing * offset_z + layers,
            low_x : low_x + span_x,
            low_y : low_y + span_y,
        ]
        partial_value = [0.0, 0.0, 0.0]
        for second in range(8):
            other_z, other_x, other_y = corner_bits(second)
            first_z = spacing + spacing * (other_z - offset_z)
            first_x = pad_field - margin + spacing * (other_x - offset_x)
            first_y = pad_field - margin + spacing * (other_y - offset_y)
            shifted = lifted[
                :,
                first_z : first_z + layers,
                first_x : first_x + span_x,
                first_y : first_y + span_y,
            ]
            for out_comp in range(3):
                for in_comp in range(3):
                    coupling = float(element_table[corner, out_comp, second, in_comp])
                    if abs(coupling) > 1e-12:
                        partial_value[out_comp] = (
                            partial_value[out_comp] + coupling * shifted[in_comp]
                        )
        for out_comp in range(3):
            totals[out_comp] = totals[out_comp] + weight * partial_value[out_comp]
    return spacing * jnp.stack(totals)


def spread(values, pad_field, spacing, side_weight, center, margin):
    layers = values.shape[1]
    span_x = values.shape[2] - 2 * pad_field + 2 * margin
    span_y = values.shape[3] - 2 * pad_field + 2 * margin
    lifted = jnp.pad(values, ((0, 0), (spacing, spacing), (0, 0), (0, 0)))
    along_z = center * lifted[:, spacing : spacing + layers] + side_weight * (
        lifted[:, 2 * spacing : 2 * spacing + layers] + lifted[:, :layers]
    )
    anchor = pad_field - margin
    along_x = center * along_z[:, :, anchor : anchor + span_x] + side_weight * (
        along_z[:, :, anchor + spacing : anchor + spacing + span_x]
        + along_z[:, :, anchor - spacing : anchor - spacing + span_x]
    )
    along_y = center * along_x[:, :, :, anchor : anchor + span_y] + side_weight * (
        along_x[:, :, :, anchor + spacing : anchor + spacing + span_y]
        + along_x[:, :, :, anchor - spacing : anchor - spacing + span_y]
    )
    return along_y


def smooth_rim(values, spacing):
    return with_halo(values, (("gx", 2), ("gy", 3)), spacing)


def on_device(right_side, density, fixed_mask):
    reach_max = 2 ** (LEVELS - 1)
    wide_x = right_side.shape[2]
    wide_y = right_side.shape[3]
    free_dofs = (1 - fixed_mask).astype(jnp.float32)
    element_table = element_matrix()
    grown_scale = with_halo(young_modulus(density), (("gx", 1), ("gy", 2)), reach_max)
    anchor_x = lax.axis_index("gx") * wide_x
    anchor_y = lax.axis_index("gy") * wide_y
    total_x = wide_x * lax.axis_size("gx")
    total_y = wide_y * lax.axis_size("gy")
    residuals, corrections, leftovers, coefficients, diagonals = ([], [], [], [], [])
    current = free_dofs * right_side
    for level_index in range(LEVELS):
        spacing = 2**level_index
        coefficient = level_coefficient(
            grown_scale, reach_max, spacing, anchor_x, anchor_y, total_x, total_y
        )
        diagonal_now = diagonal_terms(
            coefficient, reach_max, spacing, wide_x, wide_y, element_table
        )
        smoothed = free_dofs * JACOBI_WEIGHT * current / diagonal_now
        residuals.append(current)
        corrections.append(smoothed)
        coefficients.append(coefficient)
        diagonals.append(diagonal_now)
        if level_index < LEVELS - 1:
            wide_corr = with_halo(smoothed, (("gx", 2), ("gy", 3)), spacing)
            leftover = current - stiffness(
                wide_corr, spacing, coefficient, reach_max, spacing, 0, element_table
            )
            wide_left = with_halo(leftover, (("gx", 2), ("gy", 3)), spacing)
            following = spread(wide_left, spacing, spacing, 0.5, 1.0, 0)
            leftovers.append(leftover)
            current = following
    coarsest = LEVELS - 1
    spacing = 2**coarsest
    combined = corrections[coarsest]
    applied = stiffness(
        smooth_rim(combined, spacing),
        spacing,
        coefficients[coarsest],
        reach_max,
        spacing,
        0,
        element_table,
    )
    combined = (
        combined + free_dofs * JACOBI_WEIGHT * (residuals[coarsest] - applied) / diagonals[coarsest]
    )
    for level_index in range(LEVELS - 2, -1, -1):
        spacing = 2**level_index
        wide_coarse = with_halo(combined, (("gx", 2), ("gy", 3)), spacing)
        combined = corrections[level_index] + spread(wide_coarse, spacing, spacing, 0.25, 0.5, 0)
        applied = stiffness(
            smooth_rim(combined, spacing),
            spacing,
            coefficients[level_index],
            reach_max,
            spacing,
            0,
            element_table,
        )
        balance = residuals[level_index] - applied
        combined = combined + free_dofs * JACOBI_WEIGHT * balance / diagonals[level_index]
    return free_dofs * combined


def solution(mesh):
    in_specs = (P(None, None, "gx", "gy"), P(None, "gx", "gy"), P(None, "gx", "gy"))
    out_specs = P(None, None, "gx", "gy")
    return jax.shard_map(
        on_device, mesh=mesh, in_specs=in_specs, out_specs=out_specs, check_vma=False
    )
```

profile of v0, /device:TPU:103, one launch (start us, length us, event | category | flops | bytes accessed | tf_op | source)
XLA Modules:
  0.0 407.3 jit_solution(9964245867867355370)
XLA Ops:
  3.5 6.6 %collective-permute-start = (f32[16,8,128]{2,1,0:T(8,128)S(1)}, f32[16,8,128]{2,1,0:T(8,128)S(1)}, u32[]{:S(2)}, u32[]{:S(2)}) collective-permute-start(f32[16,8,128]{2,1,0:T(8,128)S(1)} %fusion.85), channel_id=1, source_target_pairs={{0,8},{8,16},{16,24},{24,32},{32,40},{40,48},{48,56},{56,64},{64,7... | collective-permute-start | bytes 196616 | tf_op jit(solution)/shard_map/ppermute | solution.py:25
  23.5 9.1 %collective-permute-start.4 = (f32[3,16,1,128]{3,1,2,0:T(8,128)S(1)}, f32[3,16,1,128]{3,1,2,0:T(8,128)S(1)}, u32[]{:S(2)}, u32[]{:S(2)}) collective-permute-start(f32[3,16,1,128]{3,1,2,0:T(8,128)S(1)} %get-tuple-element.168), channel_id=1, source_target_pairs={{0,8},{8,16},{16,24},{24,32},{32,40},{40,48},{48,56},{56,64},{64,7... | collective-permute-start | bytes 73736 | tf_op jit(solution)/shard_map/ppermute | solution.py:25
  34.6 6.7 %collective-permute-done.5 = f32[3,16,1,128]{3,1,2,0:T(8,128)S(1)} collective-permute-done((f32[3,16,1,128]{3,1,2,0:T(8,128)S(1)}, f32[3,16,1,128]{3,1,2,0:T(8,128)S(1)}, u32[]{:S(2)}, u32[]{:S(2)}) %collective-permute-start.5) | collective-permute-done | bytes 24608 | tf_op jit(solution)/shard_map/ppermute | solution.py:27
  48.4 4.0 collective-permute-done.6
  62.6 6.3 %collective-permute-done.9 = f32[3,16,1,128]{3,1,2,0:T(8,128)S(1)} collective-permute-done((f32[3,16,1,128]{3,1,2,0:T(8,128)S(1)}, f32[3,16,1,128]{3,1,2,0:T(8,128)S(1)}, u32[]{:S(2)}, u32[]{:S(2)}) %collective-permute-start.9) | collective-permute-done | bytes 24608 | tf_op jit(solution)/shard_map/ppermute | solution.py:27
  76.0 4.0 collective-permute-done.11
  85.7 7.1 %collective-permute-done.13 = f32[3,16,2,128]{3,1,2,0:T(8,128)S(1)} collective-permute-done((f32[3,16,2,128]{3,1,2,0:T(8,128)S(1)}, f32[3,16,2,128]{3,1,2,0:T(8,128)S(1)}, u32[]{:S(2)}, u32[]{:S(2)}) %collective-permute-start.13) | collective-permute-done | bytes 49184 | tf_op jit(solution)/shard_map/ppermute | solution.py:27
  94.9 3.9 collective-permute-start.14
  100.4 4.0 collective-permute-done.14
  115.2 6.6 %collective-permute-done.17 = f32[3,16,2,128]{3,1,2,0:T(8,128)S(1)} collective-permute-done((f32[3,16,2,128]{3,1,2,0:T(8,128)S(1)}, f32[3,16,2,128]{3,1,2,0:T(8,128)S(1)}, u32[]{:S(2)}, u32[]{:S(2)}) %collective-permute-start.17) | collective-permute-done | bytes 49184 | tf_op jit(solution)/shard_map/ppermute | solution.py:27
  129.5 4.0 collective-permute-done.19
  139.5 7.3 %collective-permute-done.21 = f32[3,16,4,128]{3,1,2,0:T(8,128)S(1)} collective-permute-done((f32[3,16,4,128]{3,1,2,0:T(8,128)S(1)}, f32[3,16,4,128]{3,1,2,0:T(8,128)S(1)}, u32[]{:S(2)}, u32[]{:S(2)}) %collective-permute-start.21) | collective-permute-done | bytes 98336 | tf_op jit(solution)/shard_map/ppermute | solution.py:27
  149.1 5.6 %collective-permute-start.23 = (f32[3,16,16,4]{3,2,1,0:T(8,128)S(1)}, f32[3,16,16,4]{3,2,1,0:T(8,128)S(1)}, u32[]{:S(2)}, u32[]{:S(2)}) collective-permute-start(f32[3,16,16,4]{3,2,1,0:T(8,128)S(1)} %get-tuple-element.115), channel_id=1, source_target_pairs={{0,1},{1,2},{2,3},{3,4},{4,5},{5,6},{6,7},{8,9},{9,10},{10,11},{11... | collective-permute-start | bytes 36872 | tf_op jit(solution)/shard_map/ppermute | solution.py:25
  172.0 6.8 %collective-permute-done.25 = f32[3,16,4,128]{3,1,2,0:T(8,128)S(1)} collective-permute-done((f32[3,16,4,128]{3,1,2,0:T(8,128)S(1)}, f32[3,16,4,128]{3,1,2,0:T(8,128)S(1)}, u32[]{:S(2)}, u32[]{:S(2)}) %collective-permute-start.25) | collective-permute-done | bytes 98336 | tf_op jit(solution)/shard_map/ppermute | solution.py:27
  179.1 5.6 %collective-permute-start.26 = (f32[3,16,16,4]{3,2,1,0:T(8,128)S(1)}, f32[3,16,16,4]{3,2,1,0:T(8,128)S(1)}, u32[]{:S(2)}, u32[]{:S(2)}) collective-permute-start(f32[3,16,16,4]{3,2,1,0:T(8,128)S(1)} %get-tuple-element.110), channel_id=1, source_target_pairs={{0,1},{1,2},{2,3},{3,4},{4,5},{5,6},{6,7},{8,9},{9,10},{10,11},{11... | collective-permute-start | bytes 36872 | tf_op jit(solution)/shard_map/ppermute | solution.py:25
  189.5 5.9 %collective-permute-done.27 = f32[3,16,16,4]{3,2,1,0:T(8,128)S(1)} collective-permute-done((f32[3,16,16,4]{3,2,1,0:T(8,128)S(1)}, f32[3,16,16,4]{3,2,1,0:T(8,128)S(1)}, u32[]{:S(2)}, u32[]{:S(2)}) %collective-permute-start.27) | collective-permute-done | bytes 12320 | tf_op jit(solution)/shard_map/ppermute | solution.py:27
  198.9 7.3 %collective-permute-start.28 = (f32[3,16,8,128]{3,2,1,0:T(8,128)S(1)}, f32[3,16,8,128]{3,2,1,0:T(8,128)S(1)}, u32[]{:S(2)}, u32[]{:S(2)}) collective-permute-start(f32[3,16,8,128]{3,2,1,0:T(8,128)S(1)} %copy.193), channel_id=1, source_target_pairs={{0,8},{8,16},{16,24},{24,32},{32,40},{40,48},{48,56},{56,64},{64,7... | collective-permute-start | bytes 589832 | tf_op jit(solution)/shard_map/ppermute | solution.py:25
  231.5 9.6 %collective-permute-start.32 = (f32[3,16,4,128]{3,1,2,0:T(8,128)S(1)}, f32[3,16,4,128]{3,1,2,0:T(8,128)S(1)}, u32[]{:S(2)}, u32[]{:S(2)}) collective-permute-start(f32[3,16,4,128]{3,1,2,0:T(8,128)S(1)} %get-tuple-element.154), channel_id=1, source_target_pairs={{0,8},{8,16},{16,24},{24,32},{32,40},{40,48},{48,56},{56,64},{64,7... | collective-permute-start | bytes 294920 | tf_op jit(solution)/shard_map/ppermute | solution.py:25
  243.1 7.6 %collective-permute-done.33 = f32[3,16,4,128]{3,1,2,0:T(8,128)S(1)} collective-permute-done((f32[3,16,4,128]{3,1,2,0:T(8,128)S(1)}, f32[3,16,4,128]{3,1,2,0:T(8,128)S(1)}, u32[]{:S(2)}, u32[]{:S(2)}) %collective-permute-start.33) | collective-permute-done | bytes 98336 | tf_op jit(solution)/shard_map/ppermute | solution.py:27
  259.5 4.0 collective-permute-done.35
  270.1 7.5 %collective-permute-done.37 = f32[3,16,4,128]{3,1,2,0:T(8,128)S(1)} collective-permute-done((f32[3,16,4,128]{3,1,2,0:T(8,128)S(1)}, f32[3,16,4,128]{3,1,2,0:T(8,128)S(1)}, u32[]{:S(2)}, u32[]{:S(2)}) %collective-permute-start.37) | collective-permute-done | bytes 98336 | tf_op jit(solution)/shard_map/ppermute | solution.py:27
  279.8 5.9 %collective-permute-start.39 = (f32[3,16,16,4]{3,2,1,0:T(8,128)S(1)}, f32[3,16,16,4]{3,2,1,0:T(8,128)S(1)}, u32[]{:S(2)}, u32[]{:S(2)}) collective-permute-start(f32[3,16,16,4]{3,2,1,0:T(8,128)S(1)} %get-tuple-element.107), channel_id=1, source_target_pairs={{0,1},{1,2},{2,3},{3,4},{4,5},{5,6},{6,7},{8,9},{9,10},{10,11},{11... | collective-permute-start | bytes 36872 | tf_op jit(solution)/shard_map/ppermute | solution.py:25
  302.0 7.1 %collective-permute-done.41 = f32[3,16,2,128]{3,1,2,0:T(8,128)S(1)} collective-permute-done((f32[3,16,2,128]{3,1,2,0:T(8,128)S(1)}, f32[3,16,2,128]{3,1,2,0:T(8,128)S(1)}, u32[]{:S(2)}, u32[]{:S(2)}) %collective-permute-start.41) | collective-permute-done | bytes 49184 | tf_op jit(solution)/shard_map/ppermute | solution.py:27
  309.3 5.6 %collective-permute-start.42 = (f32[3,16,12,2]{3,1,2,0:T(8,128)S(1)}, f32[3,16,12,2]{3,1,2,0:T(8,128)S(1)}, u32[]{:S(2)}, u32[]{:S(2)}) collective-permute-start(f32[3,16,12,2]{3,1,2,0:T(8,128)S(1)} %get-tuple-element.124), channel_id=1, source_target_pairs={{0,1},{1,2},{2,3},{3,4},{4,5},{5,6},{6,7},{8,9},{9,10},{10,11},{11... | collective-permute-start | bytes 13832 | tf_op jit(solution)/shard_map/ppermute | solution.py:25
  318.5 5.9 %collective-permute-done.43 = f32[3,16,12,2]{3,1,2,0:T(8,128)S(1)} collective-permute-done((f32[3,16,12,2]{3,1,2,0:T(8,128)S(1)}, f32[3,16,12,2]{3,1,2,0:T(8,128)S(1)}, u32[]{:S(2)}, u32[]{:S(2)}) %collective-permute-start.43) | collective-permute-done | bytes 4640 | tf_op jit(solution)/shard_map/ppermute | solution.py:27
  325.2 3.9 collective-permute-start.44
  331.1 7.1 %collective-permute-done.45 = f32[3,16,2,128]{3,1,2,0:T(8,128)S(1)} collective-permute-done((f32[3,16,2,128]{3,1,2,0:T(8,128)S(1)}, f32[3,16,2,128]{3,1,2,0:T(8,128)S(1)}, u32[]{:S(2)}, u32[]{:S(2)}) %collective-permute-start.45) | collective-permute-done | bytes 49184 | tf_op jit(solution)/shard_map/ppermute | solution.py:27
  345.8 4.0 collective-permute-done.46
  360.2 6.8 %collective-permute-done.49 = f32[3,16,1,128]{3,1,2,0:T(8,128)S(1)} collective-permute-done((f32[3,16,1,128]{3,1,2,0:T(8,128)S(1)}, f32[3,16,1,128]{3,1,2,0:T(8,128)S(1)}, u32[]{:S(2)}, u32[]{:S(2)}) %collective-permute-start.49) | collective-permute-done | bytes 24608 | tf_op jit(solution)/shard_map/ppermute | solution.py:27
  374.1 4.0 collective-permute-done.51
  383.8 6.8 %collective-permute-done.53 = f32[3,16,1,128]{3,1,2,0:T(8,128)S(1)} collective-permute-done((f32[3,16,1,128]{3,1,2,0:T(8,128)S(1)}, f32[3,16,1,128]{3,1,2,0:T(8,128)S(1)}, u32[]{:S(2)}, u32[]{:S(2)}) %collective-permute-start.53) | collective-permute-done | bytes 24608 | tf_op jit(solution)/shard_map/ppermute | solution.py:27
  397.8 4.0 collective-permute-done.54
  (282 shorter events, 214.4 us)
Async XLA Ops:
  0.9 11.2 %collective-permute-start.1 = (f32[16,8,128]{2,1,0:T(8,128)S(1)}, f32[16,8,128]{2,1,0:T(8,128)S(1)}, u32[]{:S(2)}, u32[]{:S(2)}) collective-permute-start(f32[16,8,128]{2,1,0:T(8,128)S(1)} %fusion.85), channel_id=1, source_target_pairs={{8,0},{16,8},{24,16},{32,24},{40,32},{48,40},{56,48},{64,56},{72,6... | collective-permute-start | bytes 196616 | tf_op jit(solution)/shard_map/ppermute | solution.py:27
  23.5 11.1 %collective-permute-start.4 = (f32[3,16,1,128]{3,1,2,0:T(8,128)S(1)}, f32[3,16,1,128]{3,1,2,0:T(8,128)S(1)}, u32[]{:S(2)}, u32[]{:S(2)}) collective-permute-start(f32[3,16,1,128]{3,1,2,0:T(8,128)S(1)} %get-tuple-element.168), channel_id=1, source_target_pairs={{0,8},{8,16},{16,24},{24,32},{32,40},{40,48},{48,56},{56,64},{64,7... | collective-permute-start | bytes 73736 | tf_op jit(solution)/shard_map/ppermute | solution.py:25
  32.6 8.8 %collective-permute-start.5 = (f32[3,16,1,128]{3,1,2,0:T(8,128)S(1)}, f32[3,16,1,128]{3,1,2,0:T(8,128)S(1)}, u32[]{:S(2)}, u32[]{:S(2)}) collective-permute-start(f32[3,16,1,128]{3,1,2,0:T(8,128)S(1)} %get-tuple-element.169), channel_id=1, source_target_pairs={{8,0},{16,8},{24,16},{32,24},{40,32},{48,40},{56,48},{64,56},{72,6... | collective-permute-start | bytes 73736 | tf_op jit(solution)/shard_map/ppermute | solution.py:27
  43.4 9.1 %collective-permute-start.6 = (f32[3,16,10,1]{3,1,2,0:T(8,128)S(1)}, f32[3,16,10,1]{3,1,2,0:T(8,128)S(1)}, u32[]{:S(2)}, u32[]{:S(2)}) collective-permute-start(f32[3,16,10,1]{3,1,2,0:T(8,128)S(1)} %get-tuple-element.143), channel_id=1, source_target_pairs={{1,0},{2,1},{3,2},{4,3},{5,4},{6,5},{7,6},{9,8},{10,9},{11,10},{12... | collective-permute-start | bytes 5768 | tf_op jit(solution)/shard_map/ppermute | solution.py:27
  60.1 8.8 %collective-permute-start.9 = (f32[3,16,1,128]{3,1,2,0:T(8,128)S(1)}, f32[3,16,1,128]{3,1,2,0:T(8,128)S(1)}, u32[]{:S(2)}, u32[]{:S(2)}) collective-permute-start(f32[3,16,1,128]{3,1,2,0:T(8,128)S(1)} %get-tuple-element.167), channel_id=1, source_target_pairs={{8,0},{16,8},{24,16},{32,24},{40,32},{48,40},{56,48},{64,56},{72,6... | collective-permute-start | bytes 73736 | tf_op jit(solution)/shard_map/ppermute | solution.py:27
  71.0 9.1 %collective-permute-start.11 = (f32[3,16,10,1]{3,1,2,0:T(8,128)S(1)}, f32[3,16,10,1]{3,1,2,0:T(8,128)S(1)}, u32[]{:S(2)}, u32[]{:S(2)}) collective-permute-start(f32[3,16,10,1]{3,1,2,0:T(8,128)S(1)} %get-tuple-element.139), channel_id=1, source_target_pairs={{1,0},{2,1},{3,2},{4,3},{5,4},{6,5},{7,6},{9,8},{10,9},{11,10},{12... | collective-permute-start | bytes 5768 | tf_op jit(solution)/shard_map/ppermute | solution.py:27
  83.8 9.0 %collective-permute-start.13 = (f32[3,16,2,128]{3,1,2,0:T(8,128)S(1)}, f32[3,16,2,128]{3,1,2,0:T(8,128)S(1)}, u32[]{:S(2)}, u32[]{:S(2)}) collective-permute-start(f32[3,16,2,128]{3,1,2,0:T(8,128)S(1)} %get-tuple-element.165), channel_id=1, source_target_pairs={{8,0},{16,8},{24,16},{32,24},{40,32},{48,40},{56,48},{64,56},{72,6... | collective-permute-start | bytes 147464 | tf_op jit(solution)/shard_map/ppermute | solution.py:27
  94.9 9.6 %collective-permute-start.14 = (f32[3,16,12,2]{3,1,2,0:T(8,128)S(1)}, f32[3,16,12,2]{3,1,2,0:T(8,128)S(1)}, u32[]{:S(2)}, u32[]{:S(2)}) collective-permute-start(f32[3,16,12,2]{3,1,2,0:T(8,128)S(1)} %get-tuple-element.131), channel_id=1, source_target_pairs={{1,0},{2,1},{3,2},{4,3},{5,4},{6,5},{7,6},{9,8},{10,9},{11,10},{12... | collective-permute-start | bytes 13832 | tf_op jit(solution)/shard_map/ppermute | solution.py:27
  112.8 9.0 %collective-permute-start.17 = (f32[3,16,2,128]{3,1,2,0:T(8,128)S(1)}, f32[3,16,2,128]{3,1,2,0:T(8,128)S(1)}, u32[]{:S(2)}, u32[]{:S(2)}) collective-permute-start(f32[3,16,2,128]{3,1,2,0:T(8,128)S(1)} %get-tuple-element.163), channel_id=1, source_target_pairs={{8,0},{16,8},{24,16},{32,24},{40,32},{48,40},{56,48},{64,56},{72,6... | collective-permute-start | bytes 147464 | tf_op jit(solution)/shard_map/ppermute | solution.py:27
  123.9 9.6 %collective-permute-start.19 = (f32[3,16,12,2]{3,1,2,0:T(8,128)S(1)}, f32[3,16,12,2]{3,1,2,0:T(8,128)S(1)}, u32[]{:S(2)}, u32[]{:S(2)}) collective-permute-start(f32[3,16,12,2]{3,1,2,0:T(8,128)S(1)} %get-tuple-element.127), channel_id=1, source_target_pairs={{1,0},{2,1},{3,2},{4,3},{5,4},{6,5},{7,6},{9,8},{10,9},{11,10},{12... | collective-permute-start | bytes 13832 | tf_op jit(solution)/shard_map/ppermute | solution.py:27
  137.3 9.5 %collective-permute-start.21 = (f32[3,16,4,128]{3,1,2,0:T(8,128)S(1)}, f32[3,16,4,128]{3,1,2,0:T(8,128)S(1)}, u32[]{:S(2)}, u32[]{:S(2)}) collective-permute-start(f32[3,16,4,128]{3,1,2,0:T(8,128)S(1)} %get-tuple-element.159), channel_id=1, source_target_pairs={{8,0},{16,8},{24,16},{32,24},{40,32},{48,40},{56,48},{64,56},{72,6... | collective-permute-start | bytes 294920 | tf_op jit(solution)/shard_map/ppermute | solution.py:27
  147.2 10.6 %collective-permute-start.22 = (f32[3,16,16,4]{3,2,1,0:T(8,128)S(1)}, f32[3,16,16,4]{3,2,1,0:T(8,128)S(1)}, u32[]{:S(2)}, u32[]{:S(2)}) collective-permute-start(f32[3,16,16,4]{3,2,1,0:T(8,128)S(1)} %get-tuple-element.114), channel_id=1, source_target_pairs={{1,0},{2,1},{3,2},{4,3},{5,4},{6,5},{7,6},{9,8},{10,9},{11,10},{12... | collective-permute-start | bytes 36872 | tf_op jit(solution)/shard_map/ppermute | solution.py:27
  149.1 10.2 %collective-permute-start.23 = (f32[3,16,16,4]{3,2,1,0:T(8,128)S(1)}, f32[3,16,16,4]{3,2,1,0:T(8,128)S(1)}, u32[]{:S(2)}, u32[]{:S(2)}) collective-permute-start(f32[3,16,16,4]{3,2,1,0:T(8,128)S(1)} %get-tuple-element.115), channel_id=1, source_target_pairs={{0,1},{1,2},{2,3},{3,4},{4,5},{5,6},{6,7},{8,9},{9,10},{10,11},{11... | collective-permute-start | bytes 36872 | tf_op jit(solution)/shard_map/ppermute | solution.py:25
  169.3 9.5 %collective-permute-start.25 = (f32[3,16,4,128]{3,1,2,0:T(8,128)S(1)}, f32[3,16,4,128]{3,1,2,0:T(8,128)S(1)}, u32[]{:S(2)}, u32[]{:S(2)}) collective-permute-start(f32[3,16,4,128]{3,1,2,0:T(8,128)S(1)} %get-tuple-element.157), channel_id=1, source_target_pairs={{8,0},{16,8},{24,16},{32,24},{40,32},{48,40},{56,48},{64,56},{72,6... | collective-permute-start | bytes 294920 | tf_op jit(solution)/shard_map/ppermute | solution.py:27
  179.1 10.3 %collective-permute-start.26 = (f32[3,16,16,4]{3,2,1,0:T(8,128)S(1)}, f32[3,16,16,4]{3,2,1,0:T(8,128)S(1)}, u32[]{:S(2)}, u32[]{:S(2)}) collective-permute-start(f32[3,16,16,4]{3,2,1,0:T(8,128)S(1)} %get-tuple-element.110), channel_id=1, source_target_pairs={{0,1},{1,2},{2,3},{3,4},{4,5},{5,6},{6,7},{8,9},{9,10},{10,11},{11... | collective-permute-start | bytes 36872 | tf_op jit(solution)/shard_map/ppermute | solution.py:25
  184.8 10.6 %collective-permute-start.27 = (f32[3,16,16,4]{3,2,1,0:T(8,128)S(1)}, f32[3,16,16,4]{3,2,1,0:T(8,128)S(1)}, u32[]{:S(2)}, u32[]{:S(2)}) collective-permute-start(f32[3,16,16,4]{3,2,1,0:T(8,128)S(1)} %get-tuple-element.111), channel_id=1, source_target_pairs={{1,0},{2,1},{3,2},{4,3},{5,4},{6,5},{7,6},{9,8},{10,9},{11,10},{12... | collective-permute-start | bytes 36872 | tf_op jit(solution)/shard_map/ppermute | solution.py:27
  197.0 10.6 %collective-permute-start.29 = (f32[3,16,8,128]{3,2,1,0:T(8,128)S(1)}, f32[3,16,8,128]{3,2,1,0:T(8,128)S(1)}, u32[]{:S(2)}, u32[]{:S(2)}) collective-permute-start(f32[3,16,8,128]{3,2,1,0:T(8,128)S(1)} %copy.193), channel_id=1, source_target_pairs={{8,0},{16,8},{24,16},{32,24},{40,32},{48,40},{56,48},{64,56},{72,6... | collective-permute-start | bytes 589832 | tf_op jit(solution)/shard_map/ppermute | solution.py:27
  198.9 9.9 %collective-permute-start.28 = (f32[3,16,8,128]{3,2,1,0:T(8,128)S(1)}, f32[3,16,8,128]{3,2,1,0:T(8,128)S(1)}, u32[]{:S(2)}, u32[]{:S(2)}) collective-permute-start(f32[3,16,8,128]{3,2,1,0:T(8,128)S(1)} %copy.193), channel_id=1, source_target_pairs={{0,8},{8,16},{16,24},{24,32},{32,40},{40,48},{48,56},{56,64},{64,7... | collective-permute-start | bytes 589832 | tf_op jit(solution)/shard_map/ppermute | solution.py:25
  214.8 8.8 %collective-permute-start.30 = (f32[3,16,24,8]{2,3,1,0:T(8,128)}, f32[3,16,24,8]{2,3,1,0:T(8,128)}, u32[]{:S(2)}, u32[]{:S(2)}) collective-permute-start(f32[3,16,24,8]{2,3,1,0:T(8,128)} %copy.197), channel_id=1, source_target_pairs={{1,0},{2,1},{3,2},{4,3},{5,4},{6,5},{7,6},{9,8},{10,9},{11,10},{12... | collective-permute-start | bytes 110600 | tf_op jit(solution)/shard_map/ppermute | solution.py:27
  231.5 11.6 %collective-permute-start.32 = (f32[3,16,4,128]{3,1,2,0:T(8,128)S(1)}, f32[3,16,4,128]{3,1,2,0:T(8,128)S(1)}, u32[]{:S(2)}, u32[]{:S(2)}) collective-permute-start(f32[3,16,4,128]{3,1,2,0:T(8,128)S(1)} %get-tuple-element.154), channel_id=1, source_target_pairs={{0,8},{8,16},{16,24},{24,32},{32,40},{40,48},{48,56},{56,64},{64,7... | collective-permute-start | bytes 294920 | tf_op jit(solution)/shard_map/ppermute | solution.py:25
  241.1 9.7 %collective-permute-start.33 = (f32[3,16,4,128]{3,1,2,0:T(8,128)S(1)}, f32[3,16,4,128]{3,1,2,0:T(8,128)S(1)}, u32[]{:S(2)}, u32[]{:S(2)}) collective-permute-start(f32[3,16,4,128]{3,1,2,0:T(8,128)S(1)} %get-tuple-element.155), channel_id=1, source_target_pairs={{8,0},{16,8},{24,16},{32,24},{40,32},{48,40},{56,48},{64,56},{72,6... | collective-permute-start | bytes 294920 | tf_op jit(solution)/shard_map/ppermute | solution.py:27
  252.9 10.6 %collective-permute-start.35 = (f32[3,16,16,4]{3,2,1,0:T(8,128)S(1)}, f32[3,16,16,4]{3,2,1,0:T(8,128)S(1)}, u32[]{:S(2)}, u32[]{:S(2)}) collective-permute-start(f32[3,16,16,4]{3,2,1,0:T(8,128)S(1)} %get-tuple-element.109), channel_id=1, source_target_pairs={{1,0},{2,1},{3,2},{4,3},{5,4},{6,5},{7,6},{9,8},{10,9},{11,10},{12... | collective-permute-start | bytes 36872 | tf_op jit(solution)/shard_map/ppermute | solution.py:27
  268.0 9.5 %collective-permute-start.37 = (f32[3,16,4,128]{3,1,2,0:T(8,128)S(1)}, f32[3,16,4,128]{3,1,2,0:T(8,128)S(1)}, u32[]{:S(2)}, u32[]{:S(2)}) collective-permute-start(f32[3,16,4,128]{3,1,2,0:T(8,128)S(1)} %get-tuple-element.153), channel_id=1, source_target_pairs={{8,0},{16,8},{24,16},{32,24},{40,32},{48,40},{56,48},{64,56},{72,6... | collective-permute-start | bytes 294920 | tf_op jit(solution)/shard_map/ppermute | solution.py:27
  277.9 10.6 %collective-permute-start.38 = (f32[3,16,16,4]{3,2,1,0:T(8,128)S(1)}, f32[3,16,16,4]{3,2,1,0:T(8,128)S(1)}, u32[]{:S(2)}, u32[]{:S(2)}) collective-permute-start(f32[3,16,16,4]{3,2,1,0:T(8,128)S(1)} %get-tuple-element.106), channel_id=1, source_target_pairs={{1,0},{2,1},{3,2},{4,3},{5,4},{6,5},{7,6},{9,8},{10,9},{11,10},{12... | collective-permute-start | bytes 36872 | tf_op jit(solution)/shard_map/ppermute | solution.py:27
  279.8 10.2 %collective-permute-start.39 = (f32[3,16,16,4]{3,2,1,0:T(8,128)S(1)}, f32[3,16,16,4]{3,2,1,0:T(8,128)S(1)}, u32[]{:S(2)}, u32[]{:S(2)}) collective-permute-start(f32[3,16,16,4]{3,2,1,0:T(8,128)S(1)} %get-tuple-element.107), channel_id=1, source_target_pairs={{0,1},{1,2},{2,3},{3,4},{4,5},{5,6},{6,7},{8,9},{9,10},{10,11},{11... | collective-permute-start | bytes 36872 | tf_op jit(solution)/shard_map/ppermute | solution.py:25
  300.1 9.0 %collective-permute-start.41 = (f32[3,16,2,128]{3,1,2,0:T(8,128)S(1)}, f32[3,16,2,128]{3,1,2,0:T(8,128)S(1)}, u32[]{:S(2)}, u32[]{:S(2)}) collective-permute-start(f32[3,16,2,128]{3,1,2,0:T(8,128)S(1)} %get-tuple-element.151), channel_id=1, source_target_pairs={{8,0},{16,8},{24,16},{32,24},{40,32},{48,40},{56,48},{64,56},{72,6... | collective-permute-start | bytes 147464 | tf_op jit(solution)/shard_map/ppermute | solution.py:27
  309.3 9.3 %collective-permute-start.42 = (f32[3,16,12,2]{3,1,2,0:T(8,128)S(1)}, f32[3,16,12,2]{3,1,2,0:T(8,128)S(1)}, u32[]{:S(2)}, u32[]{:S(2)}) collective-permute-start(f32[3,16,12,2]{3,1,2,0:T(8,128)S(1)} %get-tuple-element.124), channel_id=1, source_target_pairs={{0,1},{1,2},{2,3},{3,4},{4,5},{5,6},{6,7},{8,9},{9,10},{10,11},{11... | collective-permute-start | bytes 13832 | tf_op jit(solution)/shard_map/ppermute | solution.py:25
  314.9 9.6 %collective-permute-start.43 = (f32[3,16,12,2]{3,1,2,0:T(8,128)S(1)}, f32[3,16,12,2]{3,1,2,0:T(8,128)S(1)}, u32[]{:S(2)}, u32[]{:S(2)}) collective-permute-start(f32[3,16,12,2]{3,1,2,0:T(8,128)S(1)} %get-tuple-element.125), channel_id=1, source_target_pairs={{1,0},{2,1},{3,2},{4,3},{5,4},{6,5},{7,6},{9,8},{10,9},{11,10},{12... | collective-permute-start | bytes 13832 | tf_op jit(solution)/shard_map/ppermute | solution.py:27
  329.1 9.0 %collective-permute-start.45 = (f32[3,16,2,128]{3,1,2,0:T(8,128)S(1)}, f32[3,16,2,128]{3,1,2,0:T(8,128)S(1)}, u32[]{:S(2)}, u32[]{:S(2)}) collective-permute-start(f32[3,16,2,128]{3,1,2,0:T(8,128)S(1)} %get-tuple-element.149), channel_id=1, source_target_pairs={{8,0},{16,8},{24,16},{32,24},{40,32},{48,40},{56,48},{64,56},{72,6... | collective-permute-start | bytes 147464 | tf_op jit(solution)/shard_map/ppermute | solution.py:27
  340.2 9.6 %collective-permute-start.46 = (f32[3,16,12,2]{3,1,2,0:T(8,128)S(1)}, f32[3,16,12,2]{3,1,2,0:T(8,128)S(1)}, u32[]{:S(2)}, u32[]{:S(2)}) collective-permute-start(f32[3,16,12,2]{3,1,2,0:T(8,128)S(1)} %get-tuple-element.123), channel_id=1, source_target_pairs={{1,0},{2,1},{3,2},{4,3},{5,4},{6,5},{7,6},{9,8},{10,9},{11,10},{12... | collective-permute-start | bytes 13832 | tf_op jit(solution)/shard_map/ppermute | solution.py:27
  369.1 9.1 %collective-permute-start.51 = (f32[3,16,10,1]{3,1,2,0:T(8,128)S(1)}, f32[3,16,10,1]{3,1,2,0:T(8,128)S(1)}, u32[]{:S(2)}, u32[]{:S(2)}) collective-permute-start(f32[3,16,10,1]{3,1,2,0:T(8,128)S(1)} %get-tuple-element.137), channel_id=1, source_target_pairs={{1,0},{2,1},{3,2},{4,3},{5,4},{6,5},{7,6},{9,8},{10,9},{11,10},{12... | collective-permute-start | bytes 5768 | tf_op jit(solution)/shard_map/ppermute | solution.py:27
  392.7 9.1 %collective-permute-start.54 = (f32[3,16,10,1]{3,1,2,0:T(8,128)S(1)}, f32[3,16,10,1]{3,1,2,0:T(8,128)S(1)}, u32[]{:S(2)}, u32[]{:S(2)}) collective-permute-start(f32[3,16,10,1]{3,1,2,0:T(8,128)S(1)} %get-tuple-element.135), channel_id=1, source_target_pairs={{1,0},{2,1},{3,2},{4,3},{5,4},{6,5},{7,6},{9,8},{10,9},{11,10},{12... | collective-permute-start | bytes 5768 | tf_op jit(solution)/shard_map/ppermute | solution.py:27
  (40 other events, 337.9 us)
where the time goes:
time: 415 us; the launch traced here: 407 us
  starting transfers between devices  175 us (42%)
  waiting for transfers between devices  168 us (40%)
  other arithmetic  49.4 us (12%)
  local copies, waits for them, and re-layouts  12.9 us (3%)
    ppermute x28, waiting for transfers between devices, with_halo(): lax.ppermute(head, axis, [((i + 1) % count, i) for i in range(ends)])  143 us
    ppermute x28, starting transfers between devices, with_halo(): lax.ppermute(tail, axis, [(i, (i + 1) % count) for i in range(ends)])  106 us
    ppermute x28, starting transfers between devices, with_halo(): lax.ppermute(head, axis, [((i + 1) % count, i) for i in range(ends)])  69.8 us
    another operation x21, other arithmetic, stiffness(): return spacing * jnp.stack(totals)  30.3 us
    ppermute x28, waiting for transfers between devices, with_halo(): lax.ppermute(tail, axis, [(i, (i + 1) % count) for i in range(ends)])  25.3 us
    concatenate x35, other arithmetic, with_halo(): jnp.concatenate([lax.ppermute(tail, axis, [(i, (i + 1) % count) for i in...  8.85 us
  transfers between devices with their start and end apart: 56, of which 42 were waited for; matrix products, arithmetic and copies ran while one was open for 2% of the time, Pallas kernels for 0%

commit v1 on v0

v1 whole, which is shorter than its diff:
```python
import jax
import jax.numpy as jnp
from jax import lax
from jax.experimental import pallas as pl
from jax.experimental.pallas import tpu as pltpu
from jax.sharding import PartitionSpec as P

LEVELS = 4
Q = 16
JACOBI_WEIGHT = 0.6
SOFT_FLOOR = 0.1
LAME_FIRST = 0.3 / (1.3 * 0.4)
SHEAR_MOD = 0.5 / 1.3
RATIO = LAME_FIRST / SHEAR_MOD
UNIT = SHEAR_MOD / 16.0
GAIN = JACOBI_WEIGHT / ((RATIO + 4.0) * 16.0 / 9.0)
TINY = 1e-30

SLAB = 8
LANES = 128
EDGE = 40
QUARTER = 32
REACH = 36
KEYS = [(i, az, ay) for i in range(3) for az in range(2) for ay in range(2)]
VMEM_BYTES = 50 * 1024 * 1024
F32 = jnp.float32


def roll(value, shift, axis):
    shift %= value.shape[axis]
    return value if shift == 0 else pltpu.roll(value, shift, axis)


def z_up(planes, step):
    if len(planes) == 1:
        return [roll(planes[0], -step, 0)]
    return [planes[1], roll(planes[0], -1, 0)]


def z_down(planes, step):
    if len(planes) == 1:
        return [roll(planes[0], step, 0)]
    return [roll(planes[1], 1, 0), planes[0]]


def rows_of(shape):
    return lax.broadcasted_iota(jnp.int32, shape, 0)


def lanes_of(shape):
    return lax.broadcasted_iota(jnp.int32, shape, 1)


def to_modes(fields, step, spacing):
    modes = {}
    for i, planes in enumerate(fields):
        ahead = [roll(p, -spacing, 1) for p in planes]
        for ay, along in ((0, [b + a for a, b in zip(planes, ahead)]), (1, [b - a for a, b in zip(planes, ahead)])):
            above = z_up(along, step)
            modes[i, 0, ay] = [b + a for a, b in zip(along, above)]
            modes[i, 1, ay] = [b - a for a, b in zip(along, above)]
    return modes


def from_modes(modes, step, spacing):
    fields = []
    for i in range(3):
        along = []
        for ay in range(2):
            low = [s - d for s, d in zip(modes[i, 0, ay], modes[i, 1, ay])]
            high = z_down([s + d for s, d in zip(modes[i, 0, ay], modes[i, 1, ay])], step)
            along.append([a + b for a, b in zip(low, high)])
        fields.append([(s - d) + roll(s + d, spacing, 1) for s, d in zip(along[0], along[1])])
    return fields


def cell(low, high, scale):
    full = {}
    for i, az, ay in KEYS:
        if az or ay:
            full[i, az, 0, ay] = high[i, az, ay] + low[i, az, ay]
        full[i, az, 1, ay] = high[i, az, ay] - low[i, az, ay]

    def mode(i, *dims):
        return full[i, int(0 in dims), int(1 in dims), int(2 in dims)]

    out = {}

    def put(value, i, *dims):
        out[i, int(0 in dims), int(1 in dims), int(2 in dims)] = value

    twice = 2.0 * scale
    half = 0.5 * scale * (RATIO / 1.5)
    third = scale * (1.0 / 3.0)
    trace = (RATIO * scale) * (mode(0, 0) + mode(1, 1) + mode(2, 2))
    for i in range(3):
        put(trace + twice * mode(i, i), i, i)
    for i, j in ((0, 1), (0, 2), (1, 2)):
        shear = scale * (mode(i, j) + mode(j, i))
        put(shear, i, j)
        put(shear, j, i)
    for q in range(3):
        p, r = [d for d in range(3) if d != q]
        first, second = mode(p, p, q), mode(r, r, q)
        both = half * (first + second)
        put(both + scale * first, p, p, q)
        put(both + scale * second, r, r, q)
    others = [[d for d in range(3) if d != i] for i in range(3)]
    total = mode(0, *others[0]) + mode(1, *others[1]) + mode(2, *others[2])
    for i in range(3):
        put(third * (total + mode(i, *others[i])), i, *others[i])
    ninth = scale * ((RATIO + 4.0) / 9.0)
    for i in range(3):
        put(ninth * mode(i, 0, 1, 2), i, 0, 1, 2)

    to_low, to_high = {}, {}
    for i, az, ay in KEYS:
        difference = out[i, az, 1, ay]
        if az or ay:
            to_low[i, az, ay] = out[i, az, 0, ay] - difference
            to_high[i, az, ay] = out[i, az, 0, ay] + difference
        else:
            to_low[i, az, ay] = -difference
            to_high[i, az, ay] = difference
    return to_low, to_high


def spread_plane(planes, step, spacing):
    rows = rows_of(planes[0].shape)
    above, below = z_up(planes, step), z_down(planes, step)
    if len(planes) == 1:
        above = [jnp.where(rows < 8 - step, above[0], 0.0)]
        below = [jnp.where(rows >= step, below[0], 0.0)]
    else:
        above = [above[0], jnp.where(rows < 7, above[1], 0.0)]
        below = [jnp.where(rows >= 1, below[0], 0.0), below[1]]
    along = [p + 0.5 * (a + b) for p, a, b in zip(planes, above, below)]
    return [p + 0.5 * (roll(p, spacing, 1) + roll(p, -spacing, 1)) for p in along]


def edges_kernel(right_ref, density_ref, mask_ref, own_ref, first_ref, last_ref):
    lanes = lanes_of((8, LANES))
    for x in range(SLAB):
        for e in range(2):
            rows = pl.ds(e * 8 + x, 8, stride=16)
            free = 1.0 - mask_ref[rows, :].astype(F32)
            level = density_ref[rows, :].astype(F32) / (Q - 1)
            young = SOFT_FLOOR + (1.0 - SOFT_FLOOR) * (level * level * level)
            fields = [free * right_ref[i, rows, :] for i in range(3)] + [UNIT * young, free]
            for f, value in enumerate(fields):
                own_ref[x, f, e] = value
            for group in range(2):
                members = fields[3 * group : 3 * group + 3]
                first = last = None
                for n, value in enumerate(members):
                    begin = roll(value, EDGE * n, 1)
                    end = roll(value, EDGE * n - (LANES - EDGE), 1)
                    first = begin if n == 0 else jnp.where(lanes < EDGE * n, first, begin)
                    last = end if n == 0 else jnp.where(lanes < EDGE * n, last, end)
                first_ref[x, group, e] = first
                last_ref[x, group, e] = last


WIDE = 2 * LANES


def fine_kernel(
    meta_ref, own_ref, after_ref, before_ref, pair_ref, far_ref,
    out_ref, value_ref, scale_out_ref, gain_ref,
    res, scale, mode, ahead, node, left,
):
    slab, line, core = meta_ref[0], meta_ref[1], meta_ref[2]
    lanes = lanes_of((8, LANES))
    wide = lanes_of((8, WIDE))
    rows = rows_of((8, WIDE))
    local = jnp.where(wide < 192, wide, wide - WIDE)
    place = local + LANES * line
    node_in = (place >= 0) & (place < 8 * LANES) & (local >= -EDGE) & (local < LANES + EDGE)
    cell_in = (place >= 0) & (place < 8 * LANES - 1)
    first_slab, last_slab = slab == 0, slab == 15

    def field(x, f, e):
        group, n = f // 3, f % 3
        if 0 <= x < SLAB:
            mid, hi, lo = own_ref[x, f, e], after_ref[x, group, e], before_ref[x, group, e]
        else:
            p = x + 3 if x < 0 else x - SLAB
            is_pair = (core == 1) if x < 0 else (core == 0)
            mid, hi, lo = (
                jnp.where(is_pair, pair_ref[p, s, e], far_ref[p, s, e])
                for s in (f, 5 + group, 7 + group)
            )
        hi = roll(hi, -EDGE * n, 1)
        lo = roll(lo, (LANES - EDGE) - EDGE * n, 1)
        return jnp.concatenate([mid, jnp.where(lanes < 64, hi, lo)], axis=1)

    def inside(mask, x, top):
        if x < 0:
            return mask & jnp.logical_not(first_slab)
        if x >= top:
            return mask & jnp.logical_not(last_slab)
        return mask

    for x in range(-3, SLAB + 2):
        for e in range(2):
            cells = inside(cell_in, x, SLAB - 1)
            if e == 1:
                cells = cells & (rows < 7)
            scale[x + 3, e] = jnp.where(cells, field(x, 3, e), 0.0)

    for x in range(-2, SLAB + 2):
        total = []
        for e in range(2):
            total.append(scale[x + 3, e] + scale[x + 2, e])
        total = [a + b for a, b in zip(total, z_down(total, 1))]
        total = [a + roll(a, 1, 1) for a in total]
        nodes = inside(node_in, x, SLAB)
        gains = []
        for e in range(2):
            free = jnp.where(nodes, field(x, 4, e), 0.0)
            gains.append(GAIN * free / jnp.maximum(total[e], TINY))
            if 0 <= x < SLAB:
                gain_ref[x, e] = gains[e][:, :LANES]
                left[x, 3, e] = free
        values = []
        for i in range(3):
            planes = []
            for e in range(2):
                now = jnp.where(nodes, field(x, i, e), 0.0)
                res[x + 2, i, e] = now
                planes.append(gains[e] * now)
                if -1 <= x < SLAB + 1:
                    value_ref[x + 1, i, e] = planes[e]
            values.append(planes)
        for k, key in enumerate(KEYS):
            pass
        modes = to_modes(values, 1, 1)
        for k, key in enumerate(KEYS):
            for e in range(2):
                mode[x + 2, k, e] = modes[key][e]
    for x in range(-1, SLAB):
        for e in range(2):
            scale_out_ref[x + 1, e] = scale[x + 3, e]

    for k in range(12):
        for e in range(2):
            ahead[k, e] = jnp.zeros((8, WIDE), F32)

    def sweep(n, carry):
        for e in range(2):
            for t in range(2):
                part = slice(t * LANES, (t + 1) * LANES)
                low = {key: mode[n, k, e, :, part] for k, key in enumerate(KEYS)}
                high = {key: mode[n + 1, k, e, :, part] for k, key in enumerate(KEYS)}
                to_low, to_high = cell(low, high, scale[n + 1, e, :, part])
                for k, key in enumerate(KEYS):
                    node[k, e, :, part] = to_low[key] + ahead[k, e, :, part]
                    ahead[k, e, :, part] = to_high[key]
        modes = {key: [node[k, e] for e in range(2)] for k, key in enumerate(KEYS)}
        applied = from_modes(modes, 1, 1)
        x = n - 2
        keep = node_in & jnp.logical_not((x < 0) & first_slab) & jnp.logical_not((x >= SLAB) & last_slab)
        for i in range(3):
            rest = [jnp.where(keep, res[n, i, e] - applied[i][e], 0.0) for e in range(2)]
            rest = spread_plane(rest, 1, 1)
            for e in range(2):
                res[n, i, e] = rest[e]
        return carry

    lax.fori_loop(0, SLAB + 3, sweep, 0)

    for x in range(SLAB):
        for e in range(2):
            fields = []
            for i in range(3):
                fields.append(res[x + 2, i, e] + 0.5 * (res[x + 1, i, e] + res[x + 3, i, e]))
            fields.append(left[x, 3, e])
            young = field(x, 3, e)
            for quarter in range(4):
                start = REACH - QUARTER * quarter
                window = roll(young, start, 1)[:, :LANES]
                target = e * 8 + (x % 2) * 4 + quarter
                for f in range(4):
                    main = roll(fields[f], start, 1)[:, :LANES]
                    piece = roll(window, 102 - 26 * f, 1)
                    out_ref[target, x // 2, f] = jnp.where(lanes < 102, main, piece)


COUNT = 64
PAD = 4


def coarse_kernel(meta_ref, in_ref, out_ref, young, free, res, value, gain, scale, spread, mode, ahead):
    start = meta_ref[3]
    shape = (8, LANES)
    lanes = lanes_of(shape)
    rows = rows_of(shape)
    place = lanes + start
    node_in = (place >= 0) & (place < 8 * LANES)
    first_in = node_in & (lanes >= 2) & (lanes < 102)
    zero = jnp.zeros(shape, F32)
    unroll = 4

    def loop(body):
        def step(i, carry):
            for u in range(unroll):
                body(unroll * i + u, i, u)
            return carry

        lax.fori_loop(0, COUNT // unroll, step, 0)

    for p in range(PAD):
        for i in range(3):
            spread[p, i] = zero
            spread[PAD + COUNT + p, i] = zero
        for k in range(12):
            mode[COUNT + p, k] = zero
        young[COUNT + p] = zero

    def unpack(x, i, u):
        total = zero
        tiles = [in_ref[x, f] for f in range(4)]
        for f in range(4):
            total = jnp.where(lanes >= 26 * f, roll(tiles[f], 26 * f - 102, 1), total)
        young[x] = total
        for f in range(3):
            res[0, x, f] = jnp.where(first_in, tiles[f], 0.0)
        free[x] = jnp.where(first_in, tiles[3], 0.0)

    loop(unpack)

    for level in range(1, LEVELS):
        step, spacing = 2 ** (level - 1), 2**level
        cells = (place >= 0) & (place <= 8 * LANES - 1 - spacing) & (rows < 8 - step)
        for p in range(step):
            scale[level - 1, p] = zero

        def fill_scale(x, i, u):
            total = young[x] + young[x + step]
            total = total + roll(total, -step, 0)
            total = total + roll(total, -spacing, 1)
            inside = cells & (x < COUNT - step)
            scale[level - 1, x + PAD] = jnp.where(inside, (0.125 * spacing) * total, 0.0)

        def fill_gain(x, i, u):
            total = scale[level - 1, x + PAD] + scale[level - 1, x + PAD - step]
            total = total + roll(total, step, 0)
            total = total + roll(total, spacing, 1)
            gain[level - 1, x] = GAIN * free[x] / jnp.maximum(total, TINY)

        for p in range(PAD):
            scale[level - 1, p] = zero
        loop(fill_scale)
        loop(fill_gain)

    def put_modes(x, fields, step, spacing):
        modes = to_modes([[f] for f in fields], step, spacing)
        for k, key in enumerate(KEYS):
            mode[x, k] = modes[key][0]

    def sweep(level, finish):
        step, spacing = 2 ** (level - 1), 2**level
        for p in range(step):
            for k in range(12):
                ahead[p, k] = zero

        def body(x, i, u):
            low = {key: mode[x, k] for k, key in enumerate(KEYS)}
            high = {key: mode[x + step, k] for k, key in enumerate(KEYS)}
            to_low, to_high = cell(low, high, scale[level - 1, x + PAD])
            modes = {key: [to_low[key] + ahead[x, k]] for k, key in enumerate(KEYS)}
            for k, key in enumerate(KEYS):
                ahead[x + step, k] = to_high[key]
            applied = from_modes(modes, step, spacing)
            finish(x, i, u, [a[0] for a in applied])

        loop(body)

    for level in range(1, LEVELS):
        step, spacing = 2 ** (level - 1), 2**level

        def smooth(x, i, u):
            fields = []
            for f in range(3):
                if level == 1:
                    now = res[0, x, f]
                else:
                    reach = step // 2
                    sides = spread[PAD + x - reach, f] + spread[PAD + x + reach, f]
                    now = jnp.where(node_in, spread[PAD + x, f] + 0.5 * sides, 0.0)
                    res[level - 1, x, f] = now
                fields.append(gain[level - 1, x] * now)
                value[level - 1, x, f] = fields[f]
            put_modes(x, fields, step, spacing)

        def restrict(x, i, u, applied):
            for f in range(3):
                rest = res[level - 1, x, f] - applied[f]
                spread[PAD + x, f] = spread_plane([rest], step, spacing)[0]

        def correct(x, i, u, applied):
            for f in range(3):
                rest = res[level - 1, x, f] - applied[f]
                spread[PAD + x, f] = value[level - 1, x, f] + gain[level - 1, x] * rest

        loop(smooth)
        sweep(level, restrict if level < LEVELS - 1 else correct)

    for level in range(LEVELS - 2, 0, -1):
        step, spacing = 2 ** (level - 1), 2**level

        def prolong(x, i, u):
            fields = []
            for f in range(3):
                sides = spread[PAD + x - step, f] + spread[PAD + x + step, f]
                along = spread[PAD + x, f] + 0.5 * sides
                along = spread_plane([along], step, spacing)[0]
                fields.append(jnp.where(node_in, value[level - 1, x, f] + 0.125 * along, 0.0))
                value[level - 1, x, f] = fields[f]
            put_modes(x, fields, step, spacing)

        def correct(x, i, u, applied):
            fields = []
            for f in range(3):
                rest = res[level - 1, x, f] - applied[f]
                fields.append(value[level - 1, x, f] + gain[level - 1, x] * rest)
            if level > 1:
                for f in range(3):
                    spread[PAD + x, f] = fields[f]
                return
            packed = roll(fields[0], -34, 1)
            for f in range(1, 3):
                packed = jnp.where(lanes < EDGE * f, packed, roll(fields[f], EDGE * f - 34, 1))
            out_ref[i, u + 1] = packed
            if u == 0:

                @pl.when(i > 0)
                def _():
                    out_ref[i - 1, 5] = packed

            if u == 3:

                @pl.when(i < COUNT // unroll - 1)
                def _():
                    out_ref[i + 1, 0] = packed

        loop(prolong)
        sweep(level, correct)
    out_ref[0, 0] = zero
    out_ref[COUNT // unroll - 1, 5] = zero


def last_kernel(own_ref, value_ref, scale_ref, gain_ref, in_ref, out_ref, coarse, mode, ahead, node, field):
    lanes = lanes_of((8, LANES))
    for n in range(SLAB + 4):
        slot, parity = n // 2, n % 2
        for i in range(3):
            planes = []
            for e in range(2):
                parts = [
                    roll(in_ref[e * 8 + parity * 4 + q, slot], QUARTER * q - 2 - EDGE * i, 1)
                    for q in range(4)
                ]
                main = parts[0]
                for q in range(1, 4):
                    main = jnp.where(lanes < QUARTER * q, main, parts[q])
                side = jnp.where(lanes < 64, parts[3], parts[0])
                planes.append(jnp.concatenate([main, side], axis=1))
            planes = spread_plane(planes, 1, 1)
            for e in range(2):
                coarse[n, i, e] = planes[e]

    def prolong(n, carry):
        fields = []
        for i in range(3):
            planes = []
            for e in range(2):
                along = coarse[n + 1, i, e] + 0.5 * (coarse[n, i, e] + coarse[n + 2, i, e])
                planes.append(value_ref[n, i, e] + 0.125 * along)
                field[n, i, e] = planes[e][:, :LANES]
            fields.append(planes)
        modes = to_modes(fields, 1, 1)
        for k, key in enumerate(KEYS):
            for e in range(2):
                mode[n, k, e] = modes[key][e]
        return carry

    lax.fori_loop(0, SLAB + 2, prolong, 0)

    for k in range(12):
        for e in range(2):
            ahead[k, e] = jnp.zeros((8, WIDE), F32)

    for n in range(SLAB + 1):
        x = n - 1
        for e in range(2):
            for t in range(2):
                part = slice(t * LANES, (t + 1) * LANES)
                low = {key: mode[n, k, e, :, part] for k, key in enumerate(KEYS)}
                high = {key: mode[n + 1, k, e, :, part] for k, key in enumerate(KEYS)}
                to_low, to_high = cell(low, high, scale_ref[n, e, :, part])
                for k, key in enumerate(KEYS):
                    if x >= 0:
                        node[k, e, :, part] = to_low[key] + ahead[k, e, :, part]
                    ahead[k, e, :, part] = to_high[key]
        if x < 0:
            continue
        modes = {key: [node[k, e] for e in range(2)] for k, key in enumerate(KEYS)}
        applied = from_modes(modes, 1, 1)
        for i in range(3):
            for e in range(2):
                rest = own_ref[x, i, e] - applied[i][e][:, :LANES]
                total = field[n, i, e] + gain_ref[x, e] * rest
                out_ref[i, pl.ds(e * 8 + x, 8, stride=16), :] = own_ref[x, 4, e] * total


def shapes(*sizes):
    return [jax.ShapeDtypeStruct(size, F32) for size in sizes]


def scratch(*sizes):
    return [pltpu.VMEM(size, F32) for size in sizes]


def call(kernel, name, out, scratches, scalars, arrays):
    specs = [pl.BlockSpec(memory_space=pltpu.SMEM)] * len(scalars)
    specs += [pl.BlockSpec(memory_space=pltpu.VMEM)] * len(arrays)
    return pl.pallas_call(
        kernel,
        out_shape=out,
        in_specs=specs,
        out_specs=[pl.BlockSpec(memory_space=pltpu.VMEM)] * len(out),
        scratch_shapes=scratches,
        compiler_params=pltpu.CompilerParams(vmem_limit_bytes=VMEM_BYTES),
        name=name,
    )(*scalars, *arrays)


def on_device(right_side, density, fixed_mask):
    slab, line = lax.axis_index("gx"), lax.axis_index("gy")
    slabs, lines = lax.axis_size("gx"), lax.axis_size("gy")
    core = slab % 2
    start = LANES * line + QUARTER * (slab % 4) - REACH
    meta = jnp.stack([slab, line, core, start]).astype(jnp.int32)
    rows = 16 * SLAB

    own, first, last = call(
        edges_kernel,
        "edges",
        shapes((SLAB, 5, 2, 8, LANES), (SLAB, 2, 2, 8, LANES), (SLAB, 2, 2, 8, LANES)),
        [],
        [],
        [right_side.reshape(3, rows, LANES), density.reshape(rows, LANES), fixed_mask.reshape(rows, LANES)],
    )
    after = lax.ppermute(first, "gy", [((j + 1) % lines, j) for j in range(lines)])
    before = lax.ppermute(last, "gy", [(j, (j + 1) % lines) for j in range(lines)])

    def columns(begin):
        parts = [lax.dynamic_slice_in_dim(a, begin, 3, axis=0) for a in (own, after, before)]
        return jnp.concatenate(parts, axis=1)

    pair = lax.ppermute(columns(5 * (1 - core)), "gx", [(i, i ^ 1) for i in range(slabs)])
    swaps = [(i, (i + 1) % slabs) for i in range(1, slabs, 2)]
    far = lax.ppermute(columns(5 * core), "gx", swaps + [(b, a) for a, b in swaps])

    packed, value, scale, gain = call(
        fine_kernel,
        "fine",
        shapes(
            (slabs, 4, 4, 8, LANES),
            (SLAB + 2, 3, 2, 8, WIDE),
            (SLAB + 1, 2, 8, WIDE),
            (SLAB, 2, 8, LANES),
        ),
        scratch(
            (SLAB + 4, 3, 2, 8, WIDE),
            (SLAB + 5, 2, 8, WIDE),
            (SLAB + 4, 12, 2, 8, WIDE),
            (12, 2, 8, WIDE),
            (12, 2, 8, WIDE),
            (SLAB, 4, 2, 8, WIDE),
        ),
        [meta],
        [own, after, before, pair, far],
    )
    packed = lax.all_to_all(packed, "gx", 0, 0)
    (result,) = call(
        coarse_kernel,
        "coarse",
        shapes((slabs, 6, 8, LANES)),
        scratch(
            (COUNT + PAD, 8, LANES),
            (COUNT, 8, LANES),
            (3, COUNT, 3, 8, LANES),
            (3, COUNT, 3, 8, LANES),
            (3, COUNT, 8, LANES),
            (3, PAD + COUNT, 8, LANES),
            (2 * PAD + COUNT, 3, 8, LANES),
            (COUNT + PAD, 12, 8, LANES),
            (COUNT + PAD, 12, 8, LANES),
        ),
        [meta],
        [packed.reshape(COUNT, 4, 8, LANES)],
    )
    result = lax.all_to_all(result, "gx", 0, 0)
    (correction,) = call(
        last_kernel,
        "last",
        shapes((3, rows, LANES)),
        scratch(
            (SLAB + 4, 3, 2, 8, WIDE),
            (SLAB + 2, 12, 2, 8, WIDE),
            (12, 2, 8, WIDE),
            (12, 2, 8, WIDE),
            (SLAB + 2, 3, 2, 8, LANES),
        ),
        [],
        [own, value, scale, gain, result],
    )
    return correction.reshape(right_side.shape)


def solution(mesh):
    in_specs = (P(None, None, "gx", "gy"), P(None, "gx", "gy"), P(None, "gx", "gy"))
    out_specs = P(None, None, "gx", "gy")
    return jax.shard_map(
        on_device, mesh=mesh, in_specs=in_specs, out_specs=out_specs, check_vma=False
    )
```

time: 415 us -> 115 us (0.28)
  the two profiles are of different devices: /device:TPU:103 before, /device:TPU:1 now
where the time goes in v1:
time: 115 us; the launch traced here: 114 us
  Pallas kernels  52.2 us (45%)
  blocking collectives  40.3 us (35%)
  waiting for transfers between devices  10.1 us (9%)
  starting transfers between devices  9.05 us (8%)
  local copies, waits for them, and re-layouts  2.64 us (2%)
    pallas_call x4, Pallas kernels, call(): pl.pallas_call(kernel, out_shape=out, in_specs=specs, out_specs=[pl.Block...  52.2 us
    all_to_all x1, blocking collectives, on_device(): packed = lax.all_to_all(packed, 'gx', 0, 0)  26.9 us
    all_to_all x1, blocking collectives, on_device(): result = lax.all_to_all(result, 'gx', 0, 0)  13.4 us
    ppermute x1, starting transfers between devices, on_device(): lax.ppermute(first, 'gy', [((j + 1) % lines, j) for j in range(lines)])  5.67 us
    ppermute x1, waiting for transfers between devices, on_device(): lax.ppermute(columns(5 * core), 'gx', swaps + [(b, a) for a, b in swaps])  4.16 us
    ppermute x1, waiting for transfers between devices, on_device(): lax.ppermute(last, 'gy', [(j, (j + 1) % lines) for j in range(lines)])  3.75 us
    unnamed x6, local copies, waits for them, and re-layouts  2.6 us
  transfers between devices with their start and end apart: 4, of which 3 were waited for; matrix products, arithmetic and copies ran while one was open for 0% of the time, Pallas kernels for 0%

profile of v1, /device:TPU:1, one launch (start us, length us, event | category | flops | bytes accessed | tf_op | source)
XLA Modules:
  0.0 114.4 jit_solution(9715531348649074931)
XLA Ops:
  0.0 0.0 copy-start
  0.0 0.9 copy-done
  0.9 0.0 copy-start.1
  0.9 0.8 copy-done.1
  1.8 0.0 copy-start.2
  1.8 0.8 copy-done.2
  2.6 0.2 edges.1
  2.8 5.7 %collective-permute-start = (f32[8,2,2,8,128]{4,3,2,1,0:T(8,128)S(1)}, f32[8,2,2,8,128]{4,3,2,1,0:T(8,128)S(1)}, u32[]{:S(2)}, u32[]{:S(2)}) collective-permute-start(f32[8,2,2,8,128]{4,3,2,1,0:T(8,128)S(1)} %get-tuple-element.13), channel_id=1, source_target_pairs={{1,0},{2,1},{3,2},{4,3},{5,4},{6,5},{7,6},{0,7},{9,8},{10,9},{11,1... | collective-permute-start | bytes 393224 | tf_op jit(solution)/shard_map/ppermute | solution.py:555
  8.5 0.0 collective-permute-start.1
  8.5 2.1 %collective-permute-done.after_ref = f32[8,2,2,8,128]{4,3,2,1,0:T(8,128)S(1)} collective-permute-done((f32[8,2,2,8,128]{4,3,2,1,0:T(8,128)S(1)}, f32[8,2,2,8,128]{4,3,2,1,0:T(8,128)S(1)}, u32[]{:S(2)}, u32[]{:S(2)}) %collective-permute-start) | collective-permute-done | bytes 131104 | tf_op jit(solution)/shard_map/ppermute | solution.py:555
  10.7 3.8 %collective-permute-done.1.before_ref = f32[8,2,2,8,128]{4,3,2,1,0:T(8,128)S(1)} collective-permute-done((f32[8,2,2,8,128]{4,3,2,1,0:T(8,128)S(1)}, f32[8,2,2,8,128]{4,3,2,1,0:T(8,128)S(1)}, u32[]{:S(2)}, u32[]{:S(2)}) %collective-permute-start.1) | collective-permute-done | bytes 131104 | tf_op jit(solution)/shard_map/ppermute | solution.py:556
  14.5 2.2 %collective-permute-start.2 = (f32[3,9,2,8,128]{4,3,2,1,0:T(8,128)S(1)}, f32[3,9,2,8,128]{4,3,2,1,0:T(8,128)S(1)}, u32[]{:S(2)}, u32[]{:S(2)}) collective-permute-start(f32[3,9,2,8,128]{4,3,2,1,0:T(8,128)S(1)} %pad_maximum_fusion), channel_id=1, source_target_pairs={{0,8},{8,0},{16,24},{24,16},{32,40},{40,32},{48,56},{56,48},{64,72... | collective-permute-start | bytes 663560 | tf_op jit(solution)/shard_map/ppermute | solution.py:562
  16.7 1.2 %collective-permute-start.3 = (f32[3,9,2,8,128]{4,3,2,1,0:T(8,128)S(1)}, f32[3,9,2,8,128]{4,3,2,1,0:T(8,128)S(1)}, u32[]{:S(2)}, u32[]{:S(2)}) collective-permute-start(f32[3,9,2,8,128]{4,3,2,1,0:T(8,128)S(1)} %pad_maximum_fusion.1), channel_id=1, source_target_pairs={{8,16},{24,32},{40,48},{56,64},{72,80},{88,96},{104,112},{120,0},{... | collective-permute-start | bytes 663560 | tf_op jit(solution)/shard_map/ppermute | solution.py:564
  17.9 0.1 pad_add_fusion.meta_ref
  17.9 0.0 collective-permute-done.2.pair_ref
  17.9 4.2 %collective-permute-done.3.far_ref = f32[3,9,2,8,128]{4,3,2,1,0:T(8,128)S(1)} collective-permute-done((f32[3,9,2,8,128]{4,3,2,1,0:T(8,128)S(1)}, f32[3,9,2,8,128]{4,3,2,1,0:T(8,128)S(1)}, u32[]{:S(2)}, u32[]{:S(2)}) %collective-permute-start.3) | collective-permute-done | bytes 221216 | tf_op jit(solution)/shard_map/ppermute | solution.py:564
  22.1 9.4 %fine.1 = (f32[16,4,4,8,128]{4,3,2,1,0:T(8,128)S(1)}, f32[10,3,2,8,256]{4,3,2,1,0:T(8,128)S(1)}, f32[9,2,8,256]{3,2,1,0:T(8,128)S(1)}, f32[8,2,8,128]{3,2,1,0:T(8,128)S(1)}) custom-call(s32[4]{0:T(128)S(1)} %pad_add_fusion.meta_ref, f32[8,5,2,8,128]{4,3,2,1,0:T(8,128)S(1)} %get-tuple-element.12.own_ref, ...), custom_call_target="tpu_custom_call" | custom-call | tf_op jit(solution)/shard_map/fine/pallas_call | solution.py:528
  31.5 26.9 %all_to_all.10 = f32[16,4,4,8,128]{4,3,2,1,0:T(8,128)S(1)} all-to-all(f32[16,4,4,8,128]{4,3,2,1,0:T(8,128)S(1)} %get-tuple-element.18), channel_id=1, replica_groups=mesh['gx'=16,'gy'=8] {'gx'}, dimensions={0} | all-to-all | bytes 2097152 | tf_op jit(solution)/shard_map/all_to_all | solution.py:586
  58.4 37.4 %coarse.1 = f32[16,6,8,128]{3,2,1,0:T(8,128)S(1)} custom-call(s32[4]{0:T(128)S(1)} %pad_add_fusion.meta_ref, f32[64,4,8,128]{3,2,1,0:T(8,128)S(1)} %bitcast.9), custom_call_target="tpu_custom_call" | custom-call | tf_op jit(solution)/shard_map/coarse/pallas_call | solution.py:528
  95.8 13.4 %all_to_all.11.in_ref = f32[16,6,8,128]{3,2,1,0:T(8,128)S(1)} all-to-all(f32[16,6,8,128]{3,2,1,0:T(8,128)S(1)} %coarse.1), channel_id=1, replica_groups=mesh['gx'=16,'gy'=8] {'gx'}, dimensions={0} | all-to-all | bytes 786432 | tf_op jit(solution)/shard_map/all_to_all | solution.py:605
  109.2 5.2 %last.1 = f32[3,128,128]{2,1,0:T(8,128)} custom-call(f32[8,5,2,8,128]{4,3,2,1,0:T(8,128)S(1)} %get-tuple-element.12.own_ref, f32[10,3,2,8,256]{4,3,2,1,0:T(8,128)S(1)} %get-tuple-element.15.value_ref, f32[9,2,8,256]{3,2,1,0:T(8,128)S(1)} %get-tuple-element.16.scale_ref, f32[8,2,8,128]{3,2,1,0:T(8,128)S(1)} %get-tuple-element.17.gain_ref, ...), custom_call_target="tpu_custom_call" | custom-call | tf_op jit(solution)/shard_map/last/pallas_call | solution.py:528
  (5 shorter events, 0.1 us)
Async XLA Ops:
  0.0 0.9 copy-start
  0.9 0.8 copy-start.1
  1.8 0.8 copy-start.2
  2.8 7.8 %collective-permute-start = (f32[8,2,2,8,128]{4,3,2,1,0:T(8,128)S(1)}, f32[8,2,2,8,128]{4,3,2,1,0:T(8,128)S(1)}, u32[]{:S(2)}, u32[]{:S(2)}) collective-permute-start(f32[8,2,2,8,128]{4,3,2,1,0:T(8,128)S(1)} %get-tuple-element.13), channel_id=1, source_target_pairs={{1,0},{2,1},{3,2},{4,3},{5,4},{6,5},{7,6},{0,7},{9,8},{10,9},{11,1... | collective-permute-start | bytes 393224 | tf_op jit(solution)/shard_map/ppermute | solution.py:555
  8.5 5.9 %collective-permute-start.1 = (f32[8,2,2,8,128]{4,3,2,1,0:T(8,128)S(1)}, f32[8,2,2,8,128]{4,3,2,1,0:T(8,128)S(1)}, u32[]{:S(2)}, u32[]{:S(2)}) collective-permute-start(f32[8,2,2,8,128]{4,3,2,1,0:T(8,128)S(1)} %get-tuple-element.14), channel_id=1, source_target_pairs={{0,1},{1,2},{2,3},{3,4},{4,5},{5,6},{6,7},{7,0},{8,9},{9,10},{10,1... | collective-permute-start | bytes 393224 | tf_op jit(solution)/shard_map/ppermute | solution.py:556
  14.5 3.5 %collective-permute-start.2 = (f32[3,9,2,8,128]{4,3,2,1,0:T(8,128)S(1)}, f32[3,9,2,8,128]{4,3,2,1,0:T(8,128)S(1)}, u32[]{:S(2)}, u32[]{:S(2)}) collective-permute-start(f32[3,9,2,8,128]{4,3,2,1,0:T(8,128)S(1)} %pad_maximum_fusion), channel_id=1, source_target_pairs={{0,8},{8,0},{16,24},{24,16},{32,40},{40,32},{48,56},{56,48},{64,72... | collective-permute-start | bytes 663560 | tf_op jit(solution)/shard_map/ppermute | solution.py:562
  16.7 5.4 %collective-permute-start.3 = (f32[3,9,2,8,128]{4,3,2,1,0:T(8,128)S(1)}, f32[3,9,2,8,128]{4,3,2,1,0:T(8,128)S(1)}, u32[]{:S(2)}, u32[]{:S(2)}) collective-permute-start(f32[3,9,2,8,128]{4,3,2,1,0:T(8,128)S(1)} %pad_maximum_fusion.1), channel_id=1, source_target_pairs={{8,16},{24,32},{40,48},{56,64},{72,80},{88,96},{104,112},{120,0},{... | collective-permute-start | bytes 663560 | tf_op jit(solution)/shard_map/ppermute | solution.py:564

commit v2 on v1

--- a/solution.py
+++ b/solution.py
@@ -18,6 +18,8 @@
 
 SLAB = 8
 LANES = 128
+FINE_UNROLL = 11
+LAST_UNROLL = 10
 EDGE = 40
 QUARTER = 32
 REACH = 36
@@ -41,6 +43,14 @@
     if len(planes) == 1:
         return [roll(planes[0], step, 0)]
     return [roll(planes[1], 1, 0), planes[0]]
+
+
+def fori(count, body, unroll):
+    if unroll == count:
+        for n in range(count):
+            body(n, 0)
+    else:
+        lax.fori_loop(0, count, body, 0)
 
 
 def rows_of(shape):
@@ -163,6 +173,15 @@
 
 WIDE = 2 * LANES
 
+FINE_SCRATCH = (
+    (SLAB + 4, 3, 2, 8, WIDE),
+    (SLAB + 5, 2, 8, WIDE),
+    (SLAB + 4, 12, 2, 8, WIDE),
+    (12, 2, 8, WIDE),
+    (12, 2, 8, WIDE),
+    (SLAB, 4, 2, 8, WIDE),
+)
+
 
 def fine_kernel(
     meta_ref, own_ref, after_ref, before_ref, pair_ref, far_ref,
@@ -267,7 +286,7 @@
                 res[n, i, e] = rest[e]
         return carry
 
-    lax.fori_loop(0, SLAB + 3, sweep, 0)
+    fori(SLAB + 3, sweep, FINE_UNROLL)
 
     for x in range(SLAB):
         for e in range(2):
@@ -287,7 +306,21 @@
 
 
 COUNT = 64
+UNROLL = 16
+UNROLL_SWEEP = 16
 PAD = 4
+
+COARSE_SCRATCH = (
+    (COUNT + PAD, 8, LANES),
+    (COUNT, 8, LANES),
+    (3, COUNT, 3, 8, LANES),
+    (3, COUNT, 3, 8, LANES),
+    (3, COUNT, 8, LANES),
+    (3, PAD + COUNT, 8, LANES),
+    (2 * PAD + COUNT, 3, 8, LANES),
+    (COUNT + PAD, 12, 8, LANES),
+    (COUNT + PAD, 12, 8, LANES),
+)
 
 
 def coarse_kernel(meta_ref, in_ref, out_ref, young, free, res, value, gain, scale, spread, mode, ahead):
@@ -299,12 +332,11 @@
     node_in = (place >= 0) & (place < 8 * LANES)
     first_in = node_in & (lanes >= 2) & (lanes < 102)
     zero = jnp.zeros(shape, F32)
-    unroll = 4
-
-    def loop(body):
+
+    def loop(body, unroll):
         def step(i, carry):
             for u in range(unroll):
-                body(unroll * i + u, i, u)
+                body(unroll * i + u, i * (unroll // 4) + u // 4, u % 4)
             return carry
 
         lax.fori_loop(0, COUNT // unroll, step, 0)
@@ -327,7 +359,7 @@
             res[0, x, f] = jnp.where(first_in, tiles[f], 0.0)
         free[x] = jnp.where(first_in, tiles[3], 0.0)
 
-    loop(unpack)
+    loop(unpack, UNROLL)
 
     for level in range(1, LEVELS):
         step, spacing = 2 ** (level - 1), 2**level
@@ -350,8 +382,8 @@
 
         for p in range(PAD):
             scale[level - 1, p] = zero
-        loop(fill_scale)
-        loop(fill_gain)
+        loop(fill_scale, UNROLL)
+        loop(fill_gain, UNROLL)
 
     def put_modes(x, fields, step, spacing):
         modes = to_modes([[f] for f in fields], step, spacing)
@@ -374,7 +406,7 @@
             applied = from_modes(modes, step, spacing)
             finish(x, i, u, [a[0] for a in applied])
 
-        loop(body)
+        loop(body, UNROLL_SWEEP)
 
     for level in range(1, LEVELS):
         step, spacing = 2 ** (level - 1), 2**level
@@ -403,7 +435,7 @@
                 rest = res[level - 1, x, f] - applied[f]
                 spread[PAD + x, f] = value[level - 1, x, f] + gain[level - 1, x] * rest
 
-        loop(smooth)
+        loop(smooth, UNROLL)
         sweep(level, restrict if level < LEVELS - 1 else correct)
 
     for level in range(LEVELS - 2, 0, -1):
@@ -440,14 +472,23 @@
 
             if u == 3:
 
-                @pl.when(i < COUNT // unroll - 1)
+                @pl.when(i < COUNT // 4 - 1)
                 def _():
                     out_ref[i + 1, 0] = packed
 
-        loop(prolong)
+        loop(prolong, UNROLL)
         sweep(level, correct)
     out_ref[0, 0] = zero
-    out_ref[COUNT // unroll - 1, 5] = zero
+    out_ref[COUNT // 4 - 1, 5] = zero
+
+
+LAST_SCRATCH = (
+    (SLAB + 4, 3, 2, 8, WIDE),
+    (SLAB + 2, 12, 2, 8, WIDE),
+    (12, 2, 8, WIDE),
+    (12, 2, 8, WIDE),
+    (SLAB + 2, 3, 2, 8, LANES),
+)
 
 
 def last_kernel(own_ref, value_ref, scale_ref, gain_ref, in_ref, out_ref, coarse, mode, ahead, node, field):
@@ -485,7 +526,7 @@
                 mode[n, k, e] = modes[key][e]
         return carry
 
-    lax.fori_loop(0, SLAB + 2, prolong, 0)
+    fori(SLAB + 2, prolong, LAST_UNROLL)
 
     for k in range(12):
         for e in range(2):
@@ -572,14 +613,7 @@
             (SLAB + 1, 2, 8, WIDE),
             (SLAB, 2, 8, LANES),
         ),
-        scratch(
-            (SLAB + 4, 3, 2, 8, WIDE),
-            (SLAB + 5, 2, 8, WIDE),
-            (SLAB + 4, 12, 2, 8, WIDE),
-            (12, 2, 8, WIDE),
-            (12, 2, 8, WIDE),
-            (SLAB, 4, 2, 8, WIDE),
-        ),
+        scratch(*FINE_SCRATCH),
         [meta],
         [own, after, before, pair, far],
     )
@@ -588,17 +622,7 @@
         coarse_kernel,
         "coarse",
         shapes((slabs, 6, 8, LANES)),
-        scratch(
-            (COUNT + PAD, 8, LANES),
-            (COUNT, 8, LANES),
-            (3, COUNT, 3, 8, LANES),
-            (3, COUNT, 3, 8, LANES),
-            (3, COUNT, 8, LANES),
-            (3, PAD + COUNT, 8, LANES),
-            (2 * PAD + COUNT, 3, 8, LANES),
-            (COUNT + PAD, 12, 8, LANES),
-            (COUNT + PAD, 12, 8, LANES),
-        ),
+        scratch(*COARSE_SCRATCH),
         [meta],
         [packed.reshape(COUNT, 4, 8, LANES)],
     )
@@ -607,13 +631,7 @@
         last_kernel,
         "last",
         shapes((3, rows, LANES)),
-        scratch(
-            (SLAB + 4, 3, 2, 8, WIDE),
-            (SLAB + 2, 12, 2, 8, WIDE),
-            (12, 2, 8, WIDE),
-            (12, 2, 8, WIDE),
-            (SLAB + 2, 3, 2, 8, LANES),
-        ),
+        scratch(*LAST_SCRATCH),
         [],
         [own, value, scale, gain, result],
     )

time: 115 us -> 96 us (0.83)
  Pallas kernels: 52.2 us -> 33.6 us
    pallas_call x4, Pallas kernels: 52.2 us -> 33.6 us  [call(): pl.pallas_call(kernel, out_shape=out, in_specs=specs, out_specs=[pl.Block...]
where the time goes in v2:
time: 96 us; the launch traced here: 95.8 us
  blocking collectives  40.3 us (42%)
  Pallas kernels  33.6 us (35%)
  waiting for transfers between devices  10.1 us (11%)
  starting transfers between devices  9.05 us (9%)
  local copies, waits for them, and re-layouts  2.64 us (3%)
    pallas_call x4, Pallas kernels, call(): pl.pallas_call(kernel, out_shape=out, in_specs=specs, out_specs=[pl.Block...  33.6 us
    all_to_all x1, blocking collectives, on_device(): packed = lax.all_to_all(packed, 'gx', 0, 0)  26.9 us
    all_to_all x1, blocking collectives, on_device(): result = lax.all_to_all(result, 'gx', 0, 0)  13.4 us
    ppermute x1, starting transfers between devices, on_device(): lax.ppermute(first, 'gy', [((j + 1) % lines, j) for j in range(lines)])  5.67 us
    ppermute x1, waiting for transfers between devices, on_device(): lax.ppermute(columns(5 * core), 'gx', swaps + [(b, a) for a, b in swaps])  4.16 us
    ppermute x1, waiting for transfers between devices, on_device(): lax.ppermute(last, 'gy', [(j, (j + 1) % lines) for j in range(lines)])  3.75 us
    unnamed x6, local copies, waits for them, and re-layouts  2.6 us
    ppermute x1, starting transfers between devices, on_device(): lax.ppermute(columns(5 * (1 - core)), 'gx', [(i, i ^ 1) for i in range(sl...  2.18 us
  transfers between devices with their start and end apart: 4, of which 3 were waited for; matrix products, arithmetic and copies ran while one was open for 0% of the time, Pallas kernels for 0%

profile of v2, /device:TPU:1, one launch (start us, length us, event | category | flops | bytes accessed | tf_op | source)
XLA Modules:
  0.0 95.8 jit_solution(3501851795702160999)
XLA Ops:
  0.0 0.0 copy-start
  0.0 0.9 copy-done
  0.9 0.0 copy-start.1
  0.9 0.8 copy-done.1
  1.8 0.0 copy-start.2
  1.8 0.8 copy-done.2
  2.6 0.2 edges.1
  2.8 5.7 %collective-permute-start = (f32[8,2,2,8,128]{4,3,2,1,0:T(8,128)S(1)}, f32[8,2,2,8,128]{4,3,2,1,0:T(8,128)S(1)}, u32[]{:S(2)}, u32[]{:S(2)}) collective-permute-start(f32[8,2,2,8,128]{4,3,2,1,0:T(8,128)S(1)} %get-tuple-element.13), channel_id=1, source_target_pairs={{1,0},{2,1},{3,2},{4,3},{5,4},{6,5},{7,6},{0,7},{9,8},{10,9},{11,1... | collective-permute-start | bytes 393224 | tf_op jit(solution)/shard_map/ppermute | solution.py:596
  8.5 0.0 collective-permute-start.1
  8.5 2.1 %collective-permute-done.after_ref = f32[8,2,2,8,128]{4,3,2,1,0:T(8,128)S(1)} collective-permute-done((f32[8,2,2,8,128]{4,3,2,1,0:T(8,128)S(1)}, f32[8,2,2,8,128]{4,3,2,1,0:T(8,128)S(1)}, u32[]{:S(2)}, u32[]{:S(2)}) %collective-permute-start) | collective-permute-done | bytes 131104 | tf_op jit(solution)/shard_map/ppermute | solution.py:596
  10.7 3.8 %collective-permute-done.1.before_ref = f32[8,2,2,8,128]{4,3,2,1,0:T(8,128)S(1)} collective-permute-done((f32[8,2,2,8,128]{4,3,2,1,0:T(8,128)S(1)}, f32[8,2,2,8,128]{4,3,2,1,0:T(8,128)S(1)}, u32[]{:S(2)}, u32[]{:S(2)}) %collective-permute-start.1) | collective-permute-done | bytes 131104 | tf_op jit(solution)/shard_map/ppermute | solution.py:597
  14.5 2.2 %collective-permute-start.2 = (f32[3,9,2,8,128]{4,3,2,1,0:T(8,128)S(1)}, f32[3,9,2,8,128]{4,3,2,1,0:T(8,128)S(1)}, u32[]{:S(2)}, u32[]{:S(2)}) collective-permute-start(f32[3,9,2,8,128]{4,3,2,1,0:T(8,128)S(1)} %pad_maximum_fusion), channel_id=1, source_target_pairs={{0,8},{8,0},{16,24},{24,16},{32,40},{40,32},{48,56},{56,48},{64,72... | collective-permute-start | bytes 663560 | tf_op jit(solution)/shard_map/ppermute | solution.py:603
  16.7 1.2 %collective-permute-start.3 = (f32[3,9,2,8,128]{4,3,2,1,0:T(8,128)S(1)}, f32[3,9,2,8,128]{4,3,2,1,0:T(8,128)S(1)}, u32[]{:S(2)}, u32[]{:S(2)}) collective-permute-start(f32[3,9,2,8,128]{4,3,2,1,0:T(8,128)S(1)} %pad_maximum_fusion.1), channel_id=1, source_target_pairs={{8,16},{24,32},{40,48},{56,64},{72,80},{88,96},{104,112},{120,0},{... | collective-permute-start | bytes 663560 | tf_op jit(solution)/shard_map/ppermute | solution.py:605
  17.9 0.1 pad_add_fusion.meta_ref
  17.9 0.0 collective-permute-done.2.pair_ref
  17.9 4.2 %collective-permute-done.3.far_ref = f32[3,9,2,8,128]{4,3,2,1,0:T(8,128)S(1)} collective-permute-done((f32[3,9,2,8,128]{4,3,2,1,0:T(8,128)S(1)}, f32[3,9,2,8,128]{4,3,2,1,0:T(8,128)S(1)}, u32[]{:S(2)}, u32[]{:S(2)}) %collective-permute-start.3) | collective-permute-done | bytes 221216 | tf_op jit(solution)/shard_map/ppermute | solution.py:605
  22.1 8.7 %fine.1 = (f32[16,4,4,8,128]{4,3,2,1,0:T(8,128)S(1)}, f32[10,3,2,8,256]{4,3,2,1,0:T(8,128)S(1)}, f32[9,2,8,256]{3,2,1,0:T(8,128)S(1)}, f32[8,2,8,128]{3,2,1,0:T(8,128)S(1)}) custom-call(s32[4]{0:T(128)S(1)} %pad_add_fusion.meta_ref, f32[8,5,2,8,128]{4,3,2,1,0:T(8,128)S(1)} %get-tuple-element.12.own_ref, ...), custom_call_target="tpu_custom_call" | custom-call | tf_op jit(solution)/shard_map/fine/pallas_call | solution.py:569
  30.8 26.9 %all_to_all.10 = f32[16,4,4,8,128]{4,3,2,1,0:T(8,128)S(1)} all-to-all(f32[16,4,4,8,128]{4,3,2,1,0:T(8,128)S(1)} %get-tuple-element.18), channel_id=1, replica_groups=mesh['gx'=16,'gy'=8] {'gx'}, dimensions={0} | all-to-all | bytes 2097152 | tf_op jit(solution)/shard_map/all_to_all | solution.py:620
  57.7 20.1 %coarse.1 = f32[16,6,8,128]{3,2,1,0:T(8,128)S(1)} custom-call(s32[4]{0:T(128)S(1)} %pad_add_fusion.meta_ref, f32[64,4,8,128]{3,2,1,0:T(8,128)S(1)} %bitcast.9), custom_call_target="tpu_custom_call" | custom-call | tf_op jit(solution)/shard_map/coarse/pallas_call | solution.py:569
  77.8 13.4 %all_to_all.11.in_ref = f32[16,6,8,128]{3,2,1,0:T(8,128)S(1)} all-to-all(f32[16,6,8,128]{3,2,1,0:T(8,128)S(1)} %coarse.1), channel_id=1, replica_groups=mesh['gx'=16,'gy'=8] {'gx'}, dimensions={0} | all-to-all | bytes 786432 | tf_op jit(solution)/shard_map/all_to_all | solution.py:629
  91.1 4.6 %last.1 = f32[3,128,128]{2,1,0:T(8,128)} custom-call(f32[8,5,2,8,128]{4,3,2,1,0:T(8,128)S(1)} %get-tuple-element.12.own_ref, f32[10,3,2,8,256]{4,3,2,1,0:T(8,128)S(1)} %get-tuple-element.15.value_ref, f32[9,2,8,256]{3,2,1,0:T(8,128)S(1)} %get-tuple-element.16.scale_ref, f32[8,2,8,128]{3,2,1,0:T(8,128)S(1)} %get-tuple-element.17.gain_ref, ...), custom_call_target="tpu_custom_call" | custom-call | tf_op jit(solution)/shard_map/last/pallas_call | solution.py:569
  (5 shorter events, 0.1 us)
Async XLA Ops:
  0.0 0.9 copy-start
  0.9 0.8 copy-start.1
  1.8 0.8 copy-start.2
  2.8 7.8 %collective-permute-start = (f32[8,2,2,8,128]{4,3,2,1,0:T(8,128)S(1)}, f32[8,2,2,8,128]{4,3,2,1,0:T(8,128)S(1)}, u32[]{:S(2)}, u32[]{:S(2)}) collective-permute-start(f32[8,2,2,8,128]{4,3,2,1,0:T(8,128)S(1)} %get-tuple-element.13), channel_id=1, source_target_pairs={{1,0},{2,1},{3,2},{4,3},{5,4},{6,5},{7,6},{0,7},{9,8},{10,9},{11,1... | collective-permute-start | bytes 393224 | tf_op jit(solution)/shard_map/ppermute | solution.py:596
  8.5 5.9 %collective-permute-start.1 = (f32[8,2,2,8,128]{4,3,2,1,0:T(8,128)S(1)}, f32[8,2,2,8,128]{4,3,2,1,0:T(8,128)S(1)}, u32[]{:S(2)}, u32[]{:S(2)}) collective-permute-start(f32[8,2,2,8,128]{4,3,2,1,0:T(8,128)S(1)} %get-tuple-element.14), channel_id=1, source_target_pairs={{0,1},{1,2},{2,3},{3,4},{4,5},{5,6},{6,7},{7,0},{8,9},{9,10},{10,1... | collective-permute-start | bytes 393224 | tf_op jit(solution)/shard_map/ppermute | solution.py:597
  14.5 3.5 %collective-permute-start.2 = (f32[3,9,2,8,128]{4,3,2,1,0:T(8,128)S(1)}, f32[3,9,2,8,128]{4,3,2,1,0:T(8,128)S(1)}, u32[]{:S(2)}, u32[]{:S(2)}) collective-permute-start(f32[3,9,2,8,128]{4,3,2,1,0:T(8,128)S(1)} %pad_maximum_fusion), channel_id=1, source_target_pairs={{0,8},{8,0},{16,24},{24,16},{32,40},{40,32},{48,56},{56,48},{64,72... | collective-permute-start | bytes 663560 | tf_op jit(solution)/shard_map/ppermute | solution.py:603
  16.7 5.4 %collective-permute-start.3 = (f32[3,9,2,8,128]{4,3,2,1,0:T(8,128)S(1)}, f32[3,9,2,8,128]{4,3,2,1,0:T(8,128)S(1)}, u32[]{:S(2)}, u32[]{:S(2)}) collective-permute-start(f32[3,9,2,8,128]{4,3,2,1,0:T(8,128)S(1)} %pad_maximum_fusion.1), channel_id=1, source_target_pairs={{8,16},{24,32},{40,48},{56,64},{72,80},{88,96},{104,112},{120,0},{... | collective-permute-start | bytes 663560 | tf_op jit(solution)/shard_map/ppermute | solution.py:605

commit v3 on v2

--- a/solution.py
+++ b/solution.py
@@ -21,8 +21,10 @@
 FINE_UNROLL = 11
 LAST_UNROLL = 10
 EDGE = 40
-QUARTER = 32
 REACH = 36
+WINDOW = 100
+PIECE = WINDOW // 4
+BACK = 66
 KEYS = [(i, az, ay) for i in range(3) for az in range(2) for ay in range(2)]
 VMEM_BYTES = 50 * 1024 * 1024
 F32 = jnp.float32
@@ -179,14 +181,14 @@
     (SLAB + 4, 12, 2, 8, WIDE),
     (12, 2, 8, WIDE),
     (12, 2, 8, WIDE),
-    (SLAB, 4, 2, 8, WIDE),
+    (5, SLAB, 2, 8, WIDE),
 )
 
 
 def fine_kernel(
     meta_ref, own_ref, after_ref, before_ref, pair_ref, far_ref,
     out_ref, value_ref, scale_out_ref, gain_ref,
-    res, scale, mode, ahead, node, left,
+    res, scale, mode, ahead, node, gather,
 ):
     slab, line, core = meta_ref[0], meta_ref[1], meta_ref[2]
     lanes = lanes_of((8, LANES))
@@ -240,7 +242,7 @@
             gains.append(GAIN * free / jnp.maximum(total[e], TINY))
             if 0 <= x < SLAB:
                 gain_ref[x, e] = gains[e][:, :LANES]
-                left[x, 3, e] = free
+                gather[3, x, e] = free
         values = []
         for i in range(3):
             planes = []
@@ -251,8 +253,6 @@
                 if -1 <= x < SLAB + 1:
                     value_ref[x + 1, i, e] = planes[e]
             values.append(planes)
-        for k, key in enumerate(KEYS):
-            pass
         modes = to_modes(values, 1, 1)
         for k, key in enumerate(KEYS):
             for e in range(2):
@@ -290,26 +290,34 @@
 
     for x in range(SLAB):
         for e in range(2):
-            fields = []
             for i in range(3):
-                fields.append(res[x + 2, i, e] + 0.5 * (res[x + 1, i, e] + res[x + 3, i, e]))
-            fields.append(left[x, 3, e])
-            young = field(x, 3, e)
-            for quarter in range(4):
-                start = REACH - QUARTER * quarter
-                window = roll(young, start, 1)[:, :LANES]
-                target = e * 8 + (x % 2) * 4 + quarter
+                gather[i, x, e] = res[x + 2, i, e] + 0.5 * (res[x + 1, i, e] + res[x + 3, i, e])
+            gather[4, x, e] = field(x, 3, e)
+    source = rows_of((WIDE, WIDE))
+    target = lanes_of((WIDE, WIDE))
+    y = 2 * (target % LANES) - REACH + target // LANES
+    choose = ((target % LANES) < WINDOW) & (source == (y + WIDE) % WIDE)
+    rows_in = gather[...].reshape(5 * SLAB * 16, WIDE)
+    parts = jnp.dot(
+        rows_in, choose.astype(F32), preferred_element_type=F32, precision=lax.Precision.HIGHEST
+    )
+    parts = parts.reshape(5, SLAB, 2, 8, WIDE)
+    for x in range(SLAB):
+        for e in range(2):
+            for parity in range(2):
+                part = slice(parity * LANES, (parity + 1) * LANES)
+                young = parts[4, x, e, :, part]
                 for f in range(4):
-                    main = roll(fields[f], start, 1)[:, :LANES]
-                    piece = roll(window, 102 - 26 * f, 1)
-                    out_ref[target, x // 2, f] = jnp.where(lanes < 102, main, piece)
-
-
-COUNT = 64
-UNROLL = 16
-UNROLL_SWEEP = 16
+                    piece = roll(young, WINDOW - PIECE * f, 1)
+                    out_ref[e * 4 + (x % 2) * 2 + parity, x // 2, f] = jnp.where(
+                        lanes < WINDOW, parts[f, x, e, :, part], piece
+                    )
+
+
+OWN = 32
+HALO = 18
+COUNT = OWN + HALO
 PAD = 4
-
 COARSE_SCRATCH = (
     (COUNT + PAD, 8, LANES),
     (COUNT, 8, LANES),
@@ -320,166 +328,168 @@
     (2 * PAD + COUNT, 3, 8, LANES),
     (COUNT + PAD, 12, 8, LANES),
     (COUNT + PAD, 12, 8, LANES),
+    (OWN + 8, 2, 8, LANES),
 )
-
-
-def coarse_kernel(meta_ref, in_ref, out_ref, young, free, res, value, gain, scale, spread, mode, ahead):
-    start = meta_ref[3]
+POINTS = {1: (50, 10), 2: (48, 12), 3: (44, 11)}
+SWEEPS = {1: (50, 10), 2: (48, 12), 3: (44, 11)}
+POINTS_UP = {2: (39, 13), 1: (36, 12)}
+SWEEPS_UP = {2: (39, 13), 1: (36, 12)}
+
+
+def coarse_kernel(meta_ref, own_ref, side_ref, out_ref, young, free, res, value, gain, scale, spread, mode, ahead, last):
+    half, origin = meta_ref[3], meta_ref[4]
     shape = (8, LANES)
     lanes = lanes_of(shape)
     rows = rows_of(shape)
-    place = lanes + start
+    place = 2 * lanes + origin
     node_in = (place >= 0) & (place < 8 * LANES)
-    first_in = node_in & (lanes >= 2) & (lanes < 102)
+    first_in = node_in & (lanes >= 1) & (lanes < WINDOW - 1)
     zero = jnp.zeros(shape, F32)
 
-    def loop(body, unroll):
-        def step(i, carry):
+    def loop(body, planes):
+        count, unroll = planes
+        begin = (COUNT - count) * half
+
+        def step(n, carry):
             for u in range(unroll):
-                body(unroll * i + u, i * (unroll // 4) + u // 4, u % 4)
+                body(begin + unroll * n + u)
             return carry
 
-        lax.fori_loop(0, COUNT // unroll, step, 0)
-
+        lax.fori_loop(0, count // unroll, step, 0)
+
+    for p in range(2 * PAD + COUNT):
+        for f in range(3):
+            spread[p, f] = zero
     for p in range(PAD):
-        for i in range(3):
-            spread[p, i] = zero
-            spread[PAD + COUNT + p, i] = zero
+        young[COUNT + p] = zero
         for k in range(12):
             mode[COUNT + p, k] = zero
-        young[COUNT + p] = zero
-
-    def unpack(x, i, u):
-        total = zero
-        tiles = [in_ref[x, f] for f in range(4)]
-        for f in range(4):
-            total = jnp.where(lanes >= 26 * f, roll(tiles[f], 26 * f - 102, 1), total)
-        young[x] = total
+        for level in range(3):
+            scale[level, p] = zero
+
+    def unpack(tiles, p):
+        total = roll(tiles[0], -WINDOW, 1)
+        for f in range(1, 4):
+            total = jnp.where(lanes >= PIECE * f, roll(tiles[f], PIECE * f - WINDOW, 1), total)
+        young[p] = total
         for f in range(3):
-            res[0, x, f] = jnp.where(first_in, tiles[f], 0.0)
-        free[x] = jnp.where(first_in, tiles[3], 0.0)
-
-    loop(unpack, UNROLL)
+            res[0, p, f] = jnp.where(first_in, tiles[f], 0.0)
+        free[p] = jnp.where(first_in, tiles[3], 0.0)
+
+    for p in range(OWN):
+        unpack([own_ref[p, f] for f in range(4)], p + HALO * half)
+    for p in range(HALO):
+        unpack([side_ref[p, f] for f in range(4)], p + OWN * (1 - half))
 
     for level in range(1, LEVELS):
         step, spacing = 2 ** (level - 1), 2**level
         cells = (place >= 0) & (place <= 8 * LANES - 1 - spacing) & (rows < 8 - step)
-        for p in range(step):
-            scale[level - 1, p] = zero
-
-        def fill_scale(x, i, u):
-            total = young[x] + young[x + step]
+
+        def fill_scale(p):
+            total = young[p] + young[p + step]
             total = total + roll(total, -step, 0)
-            total = total + roll(total, -spacing, 1)
-            inside = cells & (x < COUNT - step)
-            scale[level - 1, x + PAD] = jnp.where(inside, (0.125 * spacing) * total, 0.0)
-
-        def fill_gain(x, i, u):
-            total = scale[level - 1, x + PAD] + scale[level - 1, x + PAD - step]
+            total = total + roll(total, -step, 1)
+            inside = cells & (p + (2 * OWN - COUNT) * half < 2 * OWN - step)
+            scale[level - 1, p + PAD] = jnp.where(inside, (0.125 * spacing) * total, 0.0)
+
+        def fill_gain(p):
+            total = scale[level - 1, p + PAD] + scale[level - 1, p + PAD - step]
             total = total + roll(total, step, 0)
-            total = total + roll(total, spacing, 1)
-            gain[level - 1, x] = GAIN * free[x] / jnp.maximum(total, TINY)
-
-        for p in range(PAD):
-            scale[level - 1, p] = zero
-        loop(fill_scale, UNROLL)
-        loop(fill_gain, UNROLL)
-
-    def put_modes(x, fields, step, spacing):
-        modes = to_modes([[f] for f in fields], step, spacing)
+            total = total + roll(total, step, 1)
+            gain[level - 1, p] = GAIN * free[p] / jnp.maximum(total, TINY)
+
+        loop(fill_scale, (COUNT, 25))
+        loop(fill_gain, (COUNT, 25))
+
+    def put_modes(p, fields, step):
+        modes = to_modes([[f] for f in fields], step, step)
         for k, key in enumerate(KEYS):
-            mode[x, k] = modes[key][0]
-
-    def sweep(level, finish):
-        step, spacing = 2 ** (level - 1), 2**level
+            mode[p, k] = modes[key][0]
+
+    def sweep(level, planes, finish):
+        step = 2 ** (level - 1)
+        begin = (COUNT - planes[0]) * half
         for p in range(step):
             for k in range(12):
-                ahead[p, k] = zero
-
-        def body(x, i, u):
-            low = {key: mode[x, k] for k, key in enumerate(KEYS)}
-            high = {key: mode[x + step, k] for k, key in enumerate(KEYS)}
-            to_low, to_high = cell(low, high, scale[level - 1, x + PAD])
-            modes = {key: [to_low[key] + ahead[x, k]] for k, key in enumerate(KEYS)}
+                ahead[begin + p, k] = zero
+
+        def body(p):
+            low = {key: mode[p, k] for k, key in enumerate(KEYS)}
+            high = {key: mode[p + step, k] for k, key in enumerate(KEYS)}
+            to_low, to_high = cell(low, high, scale[level - 1, p + PAD])
+            modes = {key: [to_low[key] + ahead[p, k]] for k, key in enumerate(KEYS)}
             for k, key in enumerate(KEYS):
-                ahead[x + step, k] = to_high[key]
-            applied = from_modes(modes, step, spacing)
-            finish(x, i, u, [a[0] for a in applied])
-
-        loop(body, UNROLL_SWEEP)
+                ahead[p + step, k] = to_high[key]
+            applied = from_modes(modes, step, step)
+            finish(p, [a[0] for a in applied])
+
+        loop(body, planes)
 
     for level in range(1, LEVELS):
-        step, spacing = 2 ** (level - 1), 2**level
-
-        def smooth(x, i, u):
+        step = 2 ** (level - 1)
+
+        def smooth(p):
             fields = []
             for f in range(3):
                 if level == 1:
-                    now = res[0, x, f]
+                    now = res[0, p, f]
                 else:
                     reach = step // 2
-                    sides = spread[PAD + x - reach, f] + spread[PAD + x + reach, f]
-                    now = jnp.where(node_in, spread[PAD + x, f] + 0.5 * sides, 0.0)
-                    res[level - 1, x, f] = now
-                fields.append(gain[level - 1, x] * now)
-                value[level - 1, x, f] = fields[f]
-            put_modes(x, fields, step, spacing)
-
-        def restrict(x, i, u, applied):
+                    sides = spread[PAD + p - reach, f] + spread[PAD + p + reach, f]
+                    now = jnp.where(node_in, spread[PAD + p, f] + 0.5 * sides, 0.0)
+                    res[level - 1, p, f] = now
+                fields.append(gain[level - 1, p] * now)
+                value[level - 1, p, f] = fields[f]
+            put_modes(p, fields, step)
+
+        def restrict(p, applied):
             for f in range(3):
-                rest = res[level - 1, x, f] - applied[f]
-                spread[PAD + x, f] = spread_plane([rest], step, spacing)[0]
-
-        def correct(x, i, u, applied):
+                rest = res[level - 1, p, f] - applied[f]
+                spread[PAD + p, f] = spread_plane([rest], step, step)[0]
+
+        def correct(p, applied):
             for f in range(3):
-                rest = res[level - 1, x, f] - applied[f]
-                spread[PAD + x, f] = value[level - 1, x, f] + gain[level - 1, x] * rest
-
-        loop(smooth, UNROLL)
-        sweep(level, restrict if level < LEVELS - 1 else correct)
-
+                rest = res[level - 1, p, f] - applied[f]
+                spread[PAD + p, f] = value[level - 1, p, f] + gain[level - 1, p] * rest
+
+        loop(smooth, POINTS[level])
+        sweep(level, SWEEPS[level], restrict if level < LEVELS - 1 else correct)
+
+    last[3, 0] = last[3, 1] = zero
+    last[OWN + 4, 0] = last[OWN + 4, 1] = zero
     for level in range(LEVELS - 2, 0, -1):
-        step, spacing = 2 ** (level - 1), 2**level
-
-        def prolong(x, i, u):
+        step = 2 ** (level - 1)
+
+        def prolong(p):
             fields = []
             for f in range(3):
-                sides = spread[PAD + x - step, f] + spread[PAD + x + step, f]
-                along = spread[PAD + x, f] + 0.5 * sides
-                along = spread_plane([along], step, spacing)[0]
-                fields.append(jnp.where(node_in, value[level - 1, x, f] + 0.125 * along, 0.0))
-                value[level - 1, x, f] = fields[f]
-            put_modes(x, fields, step, spacing)
-
-        def correct(x, i, u, applied):
+                sides = spread[PAD + p - step, f] + spread[PAD + p + step, f]
+                along = spread[PAD + p, f] + 0.5 * sides
+                along = spread_plane([along], step, step)[0]
+                fields.append(jnp.where(node_in, value[level - 1, p, f] + 0.125 * along, 0.0))
+                value[level - 1, p, f] = fields[f]
+            put_modes(p, fields, step)
+
+        def correct(p, applied):
             fields = []
             for f in range(3):
-                rest = res[level - 1, x, f] - applied[f]
-                fields.append(value[level - 1, x, f] + gain[level - 1, x] * rest)
+                rest = res[level - 1, p, f] - applied[f]
+                fields.append(value[level - 1, p, f] + gain[level - 1, p] * rest)
             if level > 1:
                 for f in range(3):
-                    spread[PAD + x, f] = fields[f]
+                    spread[PAD + p, f] = fields[f]
                 return
-            packed = roll(fields[0], -34, 1)
-            for f in range(1, 3):
-                packed = jnp.where(lanes < EDGE * f, packed, roll(fields[f], EDGE * f - 34, 1))
-            out_ref[i, u + 1] = packed
-            if u == 0:
-
-                @pl.when(i > 0)
-                def _():
-                    out_ref[i - 1, 5] = packed
-
-            if u == 3:
-
-                @pl.when(i < COUNT // 4 - 1)
-                def _():
-                    out_ref[i + 1, 0] = packed
-
-        loop(prolong, UNROLL)
-        sweep(level, correct)
-    out_ref[0, 0] = zero
-    out_ref[COUNT // 4 - 1, 5] = zero
+            place = p + 4 - HALO * half
+            for t in range(2):
+                third = roll(fields[2], BACK - 17 - (BACK // 2) * t, 1)
+                last[place, t] = jnp.where(lanes < BACK, roll(fields[t], -17, 1), third)
+
+        loop(prolong, POINTS_UP[level])
+        sweep(level, SWEEPS_UP[level], correct)
+    for d in range(8):
+        for p in range(6):
+            for t in range(2):
+                out_ref[d, p, t] = last[4 * d + p + 3, t]
 
 
 LAST_SCRATCH = (
@@ -488,26 +498,39 @@
     (12, 2, 8, WIDE),
     (12, 2, 8, WIDE),
     (SLAB + 2, 3, 2, 8, LANES),
+    (SLAB + 4, 3, 2, 8, WIDE),
 )
 
 
-def last_kernel(own_ref, value_ref, scale_ref, gain_ref, in_ref, out_ref, coarse, mode, ahead, node, field):
+def last_kernel(own_ref, value_ref, scale_ref, gain_ref, in_ref, out_ref, coarse, mode, ahead, node, field, gather):
     lanes = lanes_of((8, LANES))
     for n in range(SLAB + 4):
         slot, parity = n // 2, n % 2
+        for e in range(2):
+            tiles = [[in_ref[e * 4 + parity * 2 + w, slot, t] for t in range(2)] for w in range(2)]
+            for w in range(2):
+                part = slice(w * LANES, (w + 1) * LANES)
+                first, second = tiles[w]
+                third = jnp.where(
+                    lanes < BACK // 2, roll(first, -BACK, 1), roll(second, BACK // 2 - BACK, 1)
+                )
+                gather[n, 0, e, :, part] = first
+                gather[n, 1, e, :, part] = second
+                gather[n, 2, e, :, part] = third
+    source = rows_of((WIDE, WIDE))
+    target = lanes_of((WIDE, WIDE))
+    y = 2 * (source % LANES) - 2 + source // LANES
+    choose = ((source % LANES) < BACK) & (target == (y + WIDE) % WIDE)
+    full = jnp.dot(
+        gather[...].reshape((SLAB + 4) * 48, WIDE),
+        choose.astype(F32),
+        preferred_element_type=F32,
+        precision=lax.Precision.HIGHEST,
+    )
+    full = full.reshape(SLAB + 4, 3, 2, 8, WIDE)
+    for n in range(SLAB + 4):
         for i in range(3):
-            planes = []
-            for e in range(2):
-                parts = [
-                    roll(in_ref[e * 8 + parity * 4 + q, slot], QUARTER * q - 2 - EDGE * i, 1)
-                    for q in range(4)
-                ]
-                main = parts[0]
-                for q in range(1, 4):
-                    main = jnp.where(lanes < QUARTER * q, main, parts[q])
-                side = jnp.where(lanes < 64, parts[3], parts[0])
-                planes.append(jnp.concatenate([main, side], axis=1))
-            planes = spread_plane(planes, 1, 1)
+            planes = spread_plane([full[n, i, e] for e in range(2)], 1, 1)
             for e in range(2):
                 coarse[n, i, e] = planes[e]
 
@@ -581,8 +604,10 @@
     slab, line = lax.axis_index("gx"), lax.axis_index("gy")
     slabs, lines = lax.axis_size("gx"), lax.axis_size("gy")
     core = slab % 2
-    start = LANES * line + QUARTER * (slab % 4) - REACH
-    meta = jnp.stack([slab, line, core, start]).astype(jnp.int32)
+    half = slab // 8
+    origin = LANES * line - REACH + core
+    meta = jnp.stack([slab, line, core, half, origin]).astype(jnp.int32)
+    groups = [list(range(8)), list(range(8, 16))]
     rows = 16 * SLAB
 
     own, first, last = call(
@@ -608,7 +633,7 @@
         fine_kernel,
         "fine",
         shapes(
-            (slabs, 4, 4, 8, LANES),
+            (8, 4, 4, 8, LANES),
             (SLAB + 2, 3, 2, 8, WIDE),
             (SLAB + 1, 2, 8, WIDE),
             (SLAB, 2, 8, LANES),
@@ -617,16 +642,19 @@
         [meta],
         [own, after, before, pair, far],
     )
-    packed = lax.all_to_all(packed, "gx", 0, 0)
+    packed = lax.all_to_all(packed, "gx", 0, 0, axis_index_groups=groups)
+    packed = packed.reshape(OWN, 4, 8, LANES)
+    side = lax.dynamic_slice_in_dim(packed, (OWN - HALO) * (1 - half), HALO, axis=0)
+    side = lax.ppermute(side, "gx", [(i, i ^ 8) for i in range(slabs)])
     (result,) = call(
         coarse_kernel,
         "coarse",
-        shapes((slabs, 6, 8, LANES)),
+        shapes((8, 6, 2, 8, LANES)),
         scratch(*COARSE_SCRATCH),
         [meta],
-        [packed.reshape(COUNT, 4, 8, LANES)],
+        [packed, side],
     )
-    result = lax.all_to_all(result, "gx", 0, 0)
+    result = lax.all_to_all(result, "gx", 0, 0, axis_index_groups=groups)
     (correction,) = call(
         last_kernel,
         "last",

time: 96 us -> 79.2 us (0.83)
  blocking collectives: 40.3 us -> 12.2 us
  waiting for transfers between devices: 10.1 us -> 26.1 us
  Pallas kernels: 33.6 us -> 18.2 us
  starting transfers between devices: 9.05 us -> 19.5 us
    all_to_all x2 -> x1, blocking collectives: 40.3 us -> 12.2 us  [on_device(): result = lax.all_to_all(result, 'gx', 0, 0, axis_index_groups=groups)]
    pallas_call x4, Pallas kernels: 33.6 us -> 18.2 us  [call(): pl.pallas_call(kernel, out_shape=out, in_specs=specs, out_specs=[pl.Block...]
    all_to_all x0 -> x1, waiting for transfers between devices: none -> 9.48 us  [on_device(): packed = lax.all_to_all(packed, 'gx', 0, 0, axis_index_groups=groups)]
    all_to_all x0 -> x1, starting transfers between devices: none -> 7.76 us  [on_device(): packed = lax.all_to_all(packed, 'gx', 0, 0, axis_index_groups=groups)]
    ppermute x0 -> x1, waiting for transfers between devices: none -> 6.53 us  [on_device(): side = lax.ppermute(side, 'gx', [(i, i ^ 8) for i in range(slabs)])]
    ppermute x0 -> x1, starting transfers between devices: none -> 2.7 us  [on_device(): side = lax.ppermute(side, 'gx', [(i, i ^ 8) for i in range(slabs)])]
  transfers between devices with their start and end apart: 4 -> 6, of which waited for: 3 -> 5; matrix products, arithmetic and copies ran while one was open for 0% -> 0% of each run, Pallas kernels for 0% -> 0%
where the time goes in v3:
time: 79.2 us; the launch traced here: 78.8 us
  waiting for transfers between devices  26.1 us (33%)
  starting transfers between devices  19.5 us (25%)
  Pallas kernels  18.2 us (23%)
  blocking collectives  12.2 us (15%)
  local copies, waits for them, and re-layouts  2.75 us (3%)
    pallas_call x4, Pallas kernels, call(): pl.pallas_call(kernel, out_shape=out, in_specs=specs, out_specs=[pl.Block...  18.2 us
    all_to_all x1, blocking collectives, on_device(): result = lax.all_to_all(result, 'gx', 0, 0, axis_index_groups=groups)  12.2 us
    all_to_all x1, waiting for transfers between devices, on_device(): packed = lax.all_to_all(packed, 'gx', 0, 0, axis_index_groups=groups)  9.48 us
    all_to_all x1, starting transfers between devices, on_device(): packed = lax.all_to_all(packed, 'gx', 0, 0, axis_index_groups=groups)  7.76 us
    ppermute x1, waiting for transfers between devices, on_device(): side = lax.ppermute(side, 'gx', [(i, i ^ 8) for i in range(slabs)])  6.53 us
    ppermute x1, starting transfers between devices, on_device(): lax.ppermute(first, 'gy', [((j + 1) % lines, j) for j in range(lines)])  5.67 us
    ppermute x1, waiting for transfers between devices, on_device(): lax.ppermute(columns(5 * core), 'gx', swaps + [(b, a) for a, b in swaps])  4.16 us
    ppermute x1, waiting for transfers between devices, on_device(): lax.ppermute(last, 'gy', [(j, (j + 1) % lines) for j in range(lines)])  3.75 us
  transfers between devices with their start and end apart: 6, of which 5 were waited for; matrix products, arithmetic and copies ran while one was open for 0% of the time, Pallas kernels for 0%

profile of v3, /device:TPU:1, one launch (start us, length us, event | category | flops | bytes accessed | tf_op | source)
XLA Modules:
  0.0 78.8 jit_solution(17321459384652540819)
XLA Ops:
  0.0 0.0 copy-start
  0.0 0.9 %copy-done = f32[3,16,8,128]{3,2,1,0:T(8,128)S(1)} copy-done((f32[3,16,8,128]{3,2,1,0:T(8,128)S(1)}, f32[3,16,8,128]{3,2,1,0:T(8,128)}, u32[]{:S(2)}) %copy-start) | copy-done | bytes 196632
  0.9 0.0 copy-start.1
  0.9 0.8 %copy-done.1 = s32[16,8,128]{2,1,0:T(8,128)S(1)} copy-done((s32[16,8,128]{2,1,0:T(8,128)S(1)}, s32[16,8,128]{2,1,0:T(8,128)}, u32[]{:S(2)}) %copy-start.1) | copy-done | bytes 65560
  1.8 0.0 copy-start.2
  1.8 0.8 %copy-done.2 = s32[16,8,128]{2,1,0:T(8,128)S(1)} copy-done((s32[16,8,128]{2,1,0:T(8,128)S(1)}, s32[16,8,128]{2,1,0:T(8,128)}, u32[]{:S(2)}) %copy-start.2) | copy-done | bytes 65560
  2.6 0.2 edges.1
  2.8 5.7 %collective-permute-start = (f32[8,2,2,8,128]{4,3,2,1,0:T(8,128)S(1)}, f32[8,2,2,8,128]{4,3,2,1,0:T(8,128)S(1)}, u32[]{:S(2)}, u32[]{:S(2)}) collective-permute-start(f32[8,2,2,8,128]{4,3,2,1,0:T(8,128)S(1)} %get-tuple-element.13), channel_id=1, source_target_pairs={{1,0},{2,1},{3,2},{4,3},{5,4},{6,5},{7,6},{0,7},{9,8},{10,9},{11,1... | collective-permute-start | bytes 393224 | tf_op jit(solution)/shard_map/ppermute | solution.py:621
  8.5 0.0 collective-permute-start.1
  8.5 2.1 %collective-permute-done.after_ref = f32[8,2,2,8,128]{4,3,2,1,0:T(8,128)S(1)} collective-permute-done((f32[8,2,2,8,128]{4,3,2,1,0:T(8,128)S(1)}, f32[8,2,2,8,128]{4,3,2,1,0:T(8,128)S(1)}, u32[]{:S(2)}, u32[]{:S(2)}) %collective-permute-start) | collective-permute-done | bytes 131104 | tf_op jit(solution)/shard_map/ppermute | solution.py:621
  10.7 3.8 %collective-permute-done.1.before_ref = f32[8,2,2,8,128]{4,3,2,1,0:T(8,128)S(1)} collective-permute-done((f32[8,2,2,8,128]{4,3,2,1,0:T(8,128)S(1)}, f32[8,2,2,8,128]{4,3,2,1,0:T(8,128)S(1)}, u32[]{:S(2)}, u32[]{:S(2)}) %collective-permute-start.1) | collective-permute-done | bytes 131104 | tf_op jit(solution)/shard_map/ppermute | solution.py:622
  14.5 2.2 %collective-permute-start.2 = (f32[3,9,2,8,128]{4,3,2,1,0:T(8,128)S(1)}, f32[3,9,2,8,128]{4,3,2,1,0:T(8,128)S(1)}, u32[]{:S(2)}, u32[]{:S(2)}) collective-permute-start(f32[3,9,2,8,128]{4,3,2,1,0:T(8,128)S(1)} %pad_maximum_fusion), channel_id=1, source_target_pairs={{0,8},{8,0},{16,24},{24,16},{32,40},{40,32},{48,56},{56,48},{64,72... | collective-permute-start | bytes 663560 | tf_op jit(solution)/shard_map/ppermute | solution.py:628
  16.7 1.2 %collective-permute-start.3 = (f32[3,9,2,8,128]{4,3,2,1,0:T(8,128)S(1)}, f32[3,9,2,8,128]{4,3,2,1,0:T(8,128)S(1)}, u32[]{:S(2)}, u32[]{:S(2)}) collective-permute-start(f32[3,9,2,8,128]{4,3,2,1,0:T(8,128)S(1)} %pad_maximum_fusion.1), channel_id=1, source_target_pairs={{8,16},{24,32},{40,48},{56,64},{72,80},{88,96},{104,112},{120,0},{... | collective-permute-start | bytes 663560 | tf_op jit(solution)/shard_map/ppermute | solution.py:630
  17.9 0.1 stack.23.meta_ref
  17.9 0.0 collective-permute-done.2.pair_ref
  17.9 4.2 %collective-permute-done.3.far_ref = f32[3,9,2,8,128]{4,3,2,1,0:T(8,128)S(1)} collective-permute-done((f32[3,9,2,8,128]{4,3,2,1,0:T(8,128)S(1)}, f32[3,9,2,8,128]{4,3,2,1,0:T(8,128)S(1)}, u32[]{:S(2)}, u32[]{:S(2)}) %collective-permute-start.3) | collective-permute-done | bytes 221216 | tf_op jit(solution)/shard_map/ppermute | solution.py:630
  22.1 3.9 %fine.1 = (f32[8,4,4,8,128]{4,3,2,1,0:T(8,128)}, f32[10,3,2,8,256]{4,3,2,1,0:T(8,128)S(1)}, f32[9,2,8,256]{3,2,1,0:T(8,128)S(1)}, f32[8,2,8,128]{3,2,1,0:T(8,128)S(1)}) custom-call(s32[5]{0:T(128)S(1)} %stack.23.meta_ref, f32[8,5,2,8,128]{4,3,2,1,0:T(8,128)S(1)} %get-tuple-element.12.own_ref, f32[8,2,2,8,128]{4,3,2,1,0:T(8,128)S(1)} %collective-permute-done.after_ref, ...), custom_call_target="tpu_custom_call" | custom-call | tf_op jit(solution)/shard_map/fine/pallas_call | solution.py:592
  26.0 7.8 %all-to-all-start = ((f32[8,4,4,8,128]{4,3,2,1,0:T(8,128)}), f32[8,4,4,8,128]{4,3,2,1,0:T(8,128)S(1)}, u32[]{:S(2)}, u32[]{:S(2)}) async-start(f32[8,4,4,8,128]{4,3,2,1,0:T(8,128)} %get-tuple-element.18), calls=%async_computation | async-start | bytes 1048576 | tf_op jit(solution)/shard_map/all_to_all | solution.py:645
  33.7 9.5 %all-to-all-done = f32[8,4,4,8,128]{4,3,2,1,0:T(8,128)S(1)} async-done(((f32[8,4,4,8,128]{4,3,2,1,0:T(8,128)}), f32[8,4,4,8,128]{4,3,2,1,0:T(8,128)S(1)}, u32[]{:S(2)}, u32[]{:S(2)}) %all-to-all-start) | async-done | bytes 524320 | tf_op jit(solution)/shard_map/all_to_all | solution.py:645
  43.2 2.7 %collective-permute-start.4 = (f32[18,4,8,128]{3,2,1,0:T(8,128)S(1)}, f32[18,4,8,128]{3,2,1,0:T(8,128)S(1)}, u32[]{:S(2)}, u32[]{:S(2)}) collective-permute-start(f32[18,4,8,128]{3,2,1,0:T(8,128)S(1)} %constant_dynamic-slice_fusion), channel_id=1, source_target_pairs={{0,64},{8,72},{16,80},{24,88},{32,96},{40,104},{48,112},{56,120},{... | collective-permute-start | bytes 884744 | tf_op jit(solution)/shard_map/ppermute | solution.py:648
  45.9 6.5 %collective-permute-done.4.side_ref = f32[18,4,8,128]{3,2,1,0:T(8,128)S(1)} collective-permute-done((f32[18,4,8,128]{3,2,1,0:T(8,128)S(1)}, f32[18,4,8,128]{3,2,1,0:T(8,128)S(1)}, u32[]{:S(2)}, u32[]{:S(2)}) %collective-permute-start.4) | collective-permute-done | bytes 294944 | tf_op jit(solution)/shard_map/ppermute | solution.py:648
  52.5 11.5 %coarse.1 = f32[8,6,2,8,128]{4,3,2,1,0:T(8,128)S(1)} custom-call(s32[5]{0:T(128)S(1)} %stack.23.meta_ref, f32[32,4,8,128]{3,2,1,0:T(8,128)S(1)} %bitcast.11, f32[18,4,8,128]{3,2,1,0:T(8,128)S(1)} %collective-permute-done.4.side_ref), custom_call_target="tpu_custom_call" | custom-call | tf_op jit(solution)/shard_map/coarse/pallas_call | solution.py:592
  64.0 12.2 %all_to_all.10.in_ref = f32[8,6,2,8,128]{4,3,2,1,0:T(8,128)S(1)} all-to-all(f32[8,6,2,8,128]{4,3,2,1,0:T(8,128)S(1)} %coarse.1), channel_id=1, replica_groups={{0,8,16,24,32,40,48,56},{64,72,80,88,96,104,112,120},{1,9,17,25,33,41,4..., dimensions={0} | all-to-all | bytes 786432 | tf_op jit(solution)/shard_map/all_to_all | solution.py:657
  76.3 2.6 %last.1 = f32[3,128,128]{2,1,0:T(8,128)} custom-call(f32[8,5,2,8,128]{4,3,2,1,0:T(8,128)S(1)} %get-tuple-element.12.own_ref, f32[10,3,2,8,256]{4,3,2,1,0:T(8,128)S(1)} %get-tuple-element.15.value_ref, f32[9,2,8,256]{3,2,1,0:T(8,128)S(1)} %get-tuple-element.16.scale_ref, f32[8,2,8,128]{3,2,1,0:T(8,128)S(1)} %get-tuple-element.17.gain_ref, ...), custom_call_target="tpu_custom_call" | custom-call | tf_op jit(solution)/shard_map/last/pallas_call | solution.py:592
  (6 shorter events, 0.1 us)
Async XLA Ops:
  0.0 0.9 %copy-start = (f32[3,16,8,128]{3,2,1,0:T(8,128)S(1)}, f32[3,16,8,128]{3,2,1,0:T(8,128)}, u32[]{:S(2)}) copy-start(f32[3,16,8,128]{3,2,1,0:T(8,128)} %param.3) | copy-start | bytes 589828
  0.9 0.8 %copy-start.1 = (s32[16,8,128]{2,1,0:T(8,128)S(1)}, s32[16,8,128]{2,1,0:T(8,128)}, u32[]{:S(2)}) copy-start(s32[16,8,128]{2,1,0:T(8,128)} %param.4) | copy-start | bytes 196612
  1.8 0.8 %copy-start.2 = (s32[16,8,128]{2,1,0:T(8,128)S(1)}, s32[16,8,128]{2,1,0:T(8,128)}, u32[]{:S(2)}) copy-start(s32[16,8,128]{2,1,0:T(8,128)} %param.5) | copy-start | bytes 196612
  2.8 7.8 %collective-permute-start = (f32[8,2,2,8,128]{4,3,2,1,0:T(8,128)S(1)}, f32[8,2,2,8,128]{4,3,2,1,0:T(8,128)S(1)}, u32[]{:S(2)}, u32[]{:S(2)}) collective-permute-start(f32[8,2,2,8,128]{4,3,2,1,0:T(8,128)S(1)} %get-tuple-element.13), channel_id=1, source_target_pairs={{1,0},{2,1},{3,2},{4,3},{5,4},{6,5},{7,6},{0,7},{9,8},{10,9},{11,1... | collective-permute-start | bytes 393224 | tf_op jit(solution)/shard_map/ppermute | solution.py:621
  8.5 5.9 %collective-permute-start.1 = (f32[8,2,2,8,128]{4,3,2,1,0:T(8,128)S(1)}, f32[8,2,2,8,128]{4,3,2,1,0:T(8,128)S(1)}, u32[]{:S(2)}, u32[]{:S(2)}) collective-permute-start(f32[8,2,2,8,128]{4,3,2,1,0:T(8,128)S(1)} %get-tuple-element.14), channel_id=1, source_target_pairs={{0,1},{1,2},{2,3},{3,4},{4,5},{5,6},{6,7},{7,0},{8,9},{9,10},{10,1... | collective-permute-start | bytes 393224 | tf_op jit(solution)/shard_map/ppermute | solution.py:622
  14.5 3.5 %collective-permute-start.2 = (f32[3,9,2,8,128]{4,3,2,1,0:T(8,128)S(1)}, f32[3,9,2,8,128]{4,3,2,1,0:T(8,128)S(1)}, u32[]{:S(2)}, u32[]{:S(2)}) collective-permute-start(f32[3,9,2,8,128]{4,3,2,1,0:T(8,128)S(1)} %pad_maximum_fusion), channel_id=1, source_target_pairs={{0,8},{8,0},{16,24},{24,16},{32,40},{40,32},{48,56},{56,48},{64,72... | collective-permute-start | bytes 663560 | tf_op jit(solution)/shard_map/ppermute | solution.py:628
  16.7 5.4 %collective-permute-start.3 = (f32[3,9,2,8,128]{4,3,2,1,0:T(8,128)S(1)}, f32[3,9,2,8,128]{4,3,2,1,0:T(8,128)S(1)}, u32[]{:S(2)}, u32[]{:S(2)}) collective-permute-start(f32[3,9,2,8,128]{4,3,2,1,0:T(8,128)S(1)} %pad_maximum_fusion.1), channel_id=1, source_target_pairs={{8,16},{24,32},{40,48},{56,64},{72,80},{88,96},{104,112},{120,0},{... | collective-permute-start | bytes 663560 | tf_op jit(solution)/shard_map/ppermute | solution.py:630
  26.0 17.2 %all-to-all-start = ((f32[8,4,4,8,128]{4,3,2,1,0:T(8,128)}), f32[8,4,4,8,128]{4,3,2,1,0:T(8,128)S(1)}, u32[]{:S(2)}, u32[]{:S(2)}) async-start(f32[8,4,4,8,128]{4,3,2,1,0:T(8,128)} %get-tuple-element.18), calls=%async_computation | async-start | bytes 1048576 | tf_op jit(solution)/shard_map/all_to_all | solution.py:645
  43.2 9.2 %collective-permute-start.4 = (f32[18,4,8,128]{3,2,1,0:T(8,128)S(1)}, f32[18,4,8,128]{3,2,1,0:T(8,128)S(1)}, u32[]{:S(2)}, u32[]{:S(2)}) collective-permute-start(f32[18,4,8,128]{3,2,1,0:T(8,128)S(1)} %constant_dynamic-slice_fusion), channel_id=1, source_target_pairs={{0,64},{8,72},{16,80},{24,88},{32,96},{40,104},{48,112},{56,120},{... | collective-permute-start | bytes 884744 | tf_op jit(solution)/shard_map/ppermute | solution.py:648

commit v4 on v3

v4 whole, which is shorter than its diff:
```python
import jax
import jax.numpy as jnp
from jax import lax
from jax.experimental import pallas as pl
from jax.experimental.pallas import tpu as pltpu
from jax.sharding import PartitionSpec as P

LEVELS = 4
Q = 16
JACOBI_WEIGHT = 0.6
SOFT_FLOOR = 0.1
LAME_FIRST = 0.3 / (1.3 * 0.4)
SHEAR_MOD = 0.5 / 1.3
RATIO = LAME_FIRST / SHEAR_MOD
UNIT = SHEAR_MOD / 16.0
GAIN = JACOBI_WEIGHT / ((RATIO + 4.0) * 16.0 / 9.0)
TINY = 1e-30

SLAB = 8
LANES = 128
LAST_UNROLL = 10
EDGE = 40
REACH = 36
WINDOW = 100
PIECE = WINDOW // 4
BACK = 66
KEYS = [(i, az, ay) for i in range(3) for az in range(2) for ay in range(2)]
VMEM_BYTES = 32 * 1024 * 1024
EDGES_BYTES = 62 * 1024 * 1024
F32 = jnp.float32


def roll(value, shift, axis):
    shift %= value.shape[axis]
    return value if shift == 0 else pltpu.roll(value, shift, axis)


def z_up(planes, step):
    if len(planes) == 1:
        return [roll(planes[0], -step, 0)]
    return [planes[1], roll(planes[0], -1, 0)]


def z_down(planes, step):
    if len(planes) == 1:
        return [roll(planes[0], step, 0)]
    return [roll(planes[1], 1, 0), planes[0]]


def fori(count, body, unroll):
    if unroll == count:
        for n in range(count):
            body(n, 0)
    else:
        lax.fori_loop(0, count, body, 0)


def rows_of(shape):
    return lax.broadcasted_iota(jnp.int32, shape, 0)


def lanes_of(shape):
    return lax.broadcasted_iota(jnp.int32, shape, 1)


def to_modes(fields, step, spacing):
    modes = {}
    for i, planes in enumerate(fields):
        ahead = [roll(p, -spacing, 1) for p in planes]
        for ay, along in ((0, [b + a for a, b in zip(planes, ahead)]), (1, [b - a for a, b in zip(planes, ahead)])):
            above = z_up(along, step)
            modes[i, 0, ay] = [b + a for a, b in zip(along, above)]
            modes[i, 1, ay] = [b - a for a, b in zip(along, above)]
    return modes


def from_modes(modes, step, spacing):
    fields = []
    for i in range(3):
        along = []
        for ay in range(2):
            low = [s - d for s, d in zip(modes[i, 0, ay], modes[i, 1, ay])]
            high = z_down([s + d for s, d in zip(modes[i, 0, ay], modes[i, 1, ay])], step)
            along.append([a + b for a, b in zip(low, high)])
        fields.append([(s - d) + roll(s + d, spacing, 1) for s, d in zip(along[0], along[1])])
    return fields


def cell(low, high, scale):
    full = {}
    for i, az, ay in KEYS:
        if az or ay:
            full[i, az, 0, ay] = high[i, az, ay] + low[i, az, ay]
        full[i, az, 1, ay] = high[i, az, ay] - low[i, az, ay]

    def mode(i, *dims):
        return full[i, int(0 in dims), int(1 in dims), int(2 in dims)]

    out = {}

    def put(value, i, *dims):
        out[i, int(0 in dims), int(1 in dims), int(2 in dims)] = value

    twice = 2.0 * scale
    half = 0.5 * scale * (RATIO / 1.5)
    third = scale * (1.0 / 3.0)
    trace = (RATIO * scale) * (mode(0, 0) + mode(1, 1) + mode(2, 2))
    for i in range(3):
        put(trace + twice * mode(i, i), i, i)
    for i, j in ((0, 1), (0, 2), (1, 2)):
        shear = scale * (mode(i, j) + mode(j, i))
        put(shear, i, j)
        put(shear, j, i)
    for q in range(3):
        p, r = [d for d in range(3) if d != q]
        first, second = mode(p, p, q), mode(r, r, q)
        both = half * (first + second)
        put(both + scale * first, p, p, q)
        put(both + scale * second, r, r, q)
    others = [[d for d in range(3) if d != i] for i in range(3)]
    total = mode(0, *others[0]) + mode(1, *others[1]) + mode(2, *others[2])
    for i in range(3):
        put(third * (total + mode(i, *others[i])), i, *others[i])
    ninth = scale * ((RATIO + 4.0) / 9.0)
    for i in range(3):
        put(ninth * mode(i, 0, 1, 2), i, 0, 1, 2)

    to_low, to_high = {}, {}
    for i, az, ay in KEYS:
        difference = out[i, az, 1, ay]
        if az or ay:
            to_low[i, az, ay] = out[i, az, 0, ay] - difference
            to_high[i, az, ay] = out[i, az, 0, ay] + difference
        else:
            to_low[i, az, ay] = -difference
            to_high[i, az, ay] = difference
    return to_low, to_high


def spread_plane(planes, step, spacing):
    rows = rows_of(planes[0].shape)
    above, below = z_up(planes, step), z_down(planes, step)
    if len(planes) == 1:
        above = [jnp.where(rows < 8 - step, above[0], 0.0)]
        below = [jnp.where(rows >= step, below[0], 0.0)]
    else:
        above = [above[0], jnp.where(rows < 7, above[1], 0.0)]
        below = [jnp.where(rows >= 1, below[0], 0.0), below[1]]
    along = [p + 0.5 * (a + b) for p, a, b in zip(planes, above, below)]
    return [p + 0.5 * (roll(p, spacing, 1) + roll(p, -spacing, 1)) for p in along]


def edges_kernel(right_hbm, density_hbm, mask_hbm, own_ref, first_ref, last_ref, right_ref, density_ref, mask_ref, sems):
    copies = [
        pltpu.make_async_copy(source, target, sems.at[n])
        for n, (source, target) in enumerate(
            ((right_hbm, right_ref), (density_hbm, density_ref), (mask_hbm, mask_ref))
        )
    ]
    for copy in copies:
        copy.start()
    for copy in copies:
        copy.wait()
    lanes = lanes_of((8, LANES))
    for x in range(SLAB):
        for e in range(2):
            rows = pl.ds(e * 8 + x, 8, stride=16)
            free = 1.0 - mask_ref[rows, :].astype(F32)
            level = density_ref[rows, :].astype(F32) / (Q - 1)
            young = SOFT_FLOOR + (1.0 - SOFT_FLOOR) * (level * level * level)
            fields = [free * right_ref[i, rows, :] for i in range(3)] + [UNIT * young, free]
            for f, value in enumerate(fields):
                own_ref[x, f, e] = value
            for group in range(2):
                members = fields[3 * group : 3 * group + 3]
                first = last = None
                for n, value in enumerate(members):
                    begin = roll(value, EDGE * n, 1)
                    end = roll(value, EDGE * n - (LANES - EDGE), 1)
                    first = begin if n == 0 else jnp.where(lanes < EDGE * n, first, begin)
                    last = end if n == 0 else jnp.where(lanes < EDGE * n, last, end)
                first_ref[x, group, e] = first
                last_ref[x, group, e] = last


WIDE = 2 * LANES

FINE_SCRATCH = (
    (5, 3, 2, 8, WIDE),
    (5, 2, 8, WIDE),
    (5, 12, 2, 8, WIDE),
    (12, 2, 8, WIDE),
    (12, 2, 8, WIDE),
    (SLAB + 2, 3, 2, 8, WIDE),
)


class Fine:
    def __init__(self, meta_ref):
        slab, line, core = meta_ref[0], meta_ref[1], meta_ref[2]
        self.core = core
        self.lanes = lanes_of((8, LANES))
        wide = lanes_of((8, WIDE))
        self.rows = rows_of((8, WIDE))
        local = jnp.where(wide < 192, wide, wide - WIDE)
        place = local + LANES * line
        self.node_in = (
            (place >= 0) & (place < 8 * LANES) & (local >= -EDGE) & (local < LANES + EDGE)
        )
        self.cell_in = (place >= 0) & (place < 8 * LANES - 1)
        self.first_slab, self.last_slab = slab == 0, slab == 15

    def inside(self, mask, x, top):
        if x < 0:
            return mask & jnp.logical_not(self.first_slab)
        if x >= top:
            return mask & jnp.logical_not(self.last_slab)
        return mask

    def widen(self, n, mid, hi, lo):
        hi = roll(hi, -EDGE * n, 1)
        lo = roll(lo, (LANES - EDGE) - EDGE * n, 1)
        return jnp.concatenate([mid, jnp.where(self.lanes < 64, hi, lo)], axis=1)

    def cells(self, x, e, young):
        mask = self.inside(self.cell_in, x, SLAB - 1)
        if e == 1:
            mask = mask & (self.rows < 7)
        return jnp.where(mask, young, 0.0)

    def smooth(self, x, scales, fields):
        total = [a + b for a, b in zip(*scales)]
        total = [a + b for a, b in zip(total, z_down(total, 1))]
        total = [a + roll(a, 1, 1) for a in total]
        nodes = self.inside(self.node_in, x, SLAB)
        free = [jnp.where(nodes, f, 0.0) for f in fields[4]]
        gains = [GAIN * f / jnp.maximum(t, TINY) for f, t in zip(free, total)]
        res = [[jnp.where(nodes, r, 0.0) for r in fields[i]] for i in range(3)]
        values = [[g * r for g, r in zip(gains, planes)] for planes in res]
        return gains, res, values


def choose_class():
    source = rows_of((WIDE, WIDE))
    target = lanes_of((WIDE, WIDE))
    y = 2 * (target % LANES) - REACH + target // LANES
    return (((target % LANES) < WINDOW) & (source == (y + WIDE) % WIDE)).astype(F32)


def split_classes(rows_in):
    return jnp.dot(
        rows_in, choose_class(), preferred_element_type=F32, precision=lax.Precision.HIGHEST
    )


def put_smoothed(x, found, res_ref, mode_ref, gain_ref, value_ref, n_res, n_mode, n_gain, n_value):
    gains, res, values = found
    modes = to_modes(values, 1, 1)
    for e in range(2):
        for i in range(3):
            res_ref[n_res, i, e] = res[i][e]
            if n_value is not None:
                value_ref[n_value, i, e] = values[i][e]
        for k, key in enumerate(KEYS):
            mode_ref[n_mode, k, e] = modes[key][e]
        if n_gain is not None:
            gain_ref[n_gain, e] = gains[e][:, :LANES]


FINE_STATE = (
    (SLAB, 2, 8, WIDE),
    (SLAB, 3, 2, 8, WIDE),
    (SLAB, 12, 2, 8, WIDE),
    (SLAB, 3, 2, 8, WIDE),
    (SLAB, 2, 8, LANES),
    (4, 2, 8, WIDE),
    (2, SLAB, 2, 8, WIDE),
)


def fine_head_kernel(
    meta_ref, own_ref, after_ref, before_ref,
    scale, res, mode, value, gain, edge, split, gather,
):
    at = Fine(meta_ref)

    def field(x, f, e):
        group, n = f // 3, f % 3
        return at.widen(n, own_ref[x, f, e], after_ref[x, group, e], before_ref[x, group, e])

    for x in range(SLAB):
        for e in range(2):
            young = field(x, 3, e)
            gather[1, x, e] = young
            scale[x, e] = at.cells(x, e, young)
            free = jnp.where(at.node_in, field(x, 4, e), 0.0)
            gather[0, x, e] = free
            if x == 0:
                for i in range(3):
                    edge[i, e] = field(0, i, e)
                edge[3, e] = free
        if x == 0:
            continue
        fields = [[field(x, i, e) for e in range(2)] for i in range(3)]
        fields += [None, [gather[0, x, e] for e in range(2)]]
        scales = [[scale[x - d, e] for e in range(2)] for d in range(2)]
        put_smoothed(x, at.smooth(x, scales, fields), res, mode, gain, value, x, x, x, x)
    parts = split_classes(gather[...].reshape(2 * SLAB * 16, WIDE))
    split[...] = parts.reshape(2, SLAB, 2, 8, WIDE)


def fine_kernel(
    meta_ref, own_scale, own_res, own_mode, own_value, own_gain, edge, split, pair_ref, far_ref,
    out_ref, value_ref, scale_ref, gain_ref,
    res, scale, mode, ahead, node, gather,
):
    at = Fine(meta_ref)

    def field(x, f, e):
        group, n = f // 3, f % 3
        p = x + 3 if x < 0 else x - SLAB
        is_pair = (at.core == 1) if x < 0 else (at.core == 0)
        parts = [
            jnp.where(is_pair, pair_ref[p, s, e], far_ref[p, s, e]) for s in (f, 5 + group, 7 + group)
        ]
        return at.widen(n, *parts)

    def scale_at(x, e):
        return own_scale[x, e] if 0 <= x < SLAB else scale[x + 3 if x < 0 else x - SLAB + 3, e]

    def mode_at(x, k, e, part):
        if 1 <= x < SLAB:
            return own_mode[x, k, e, :, part]
        return mode[x + 2 if x < 1 else x - SLAB + 3, k, e, :, part]

    def res_at(x, i, e):
        return own_res[x, i, e] if 1 <= x < SLAB else res[x + 2 if x < 1 else x - SLAB + 3, i, e]

    for x in (-3, -2, -1, 8, 9):
        for e in range(2):
            scale[x + 3 if x < 0 else x - SLAB + 3, e] = at.cells(x, e, field(x, 3, e))
    for x in (-2, -1, 0, 8, 9):
        n = x + 2 if x < 1 else x - SLAB + 3
        if x == 0:
            fields = [[edge[i, e] for e in range(2)] for i in range(3)]
            fields += [None, [edge[3, e] for e in range(2)]]
        else:
            fields = [[field(x, i, e) if i != 3 else None for e in range(2)] for i in range(5)]
        scales = [[scale_at(x - d, e) for e in range(2)] for d in range(2)]
        found = at.smooth(x, scales, fields)
        inner = -1 <= x <= SLAB
        put_smoothed(
            x, found, res, mode, gain_ref, value_ref, n, n, 0 if x == 0 else None, x + 1 if inner else None
        )
    for x in range(1, SLAB):
        for e in range(2):
            gain_ref[x, e] = own_gain[x, e]
            for i in range(3):
                value_ref[x + 1, i, e] = own_value[x, i, e]
    for x in range(-1, SLAB):
        for e in range(2):
            scale_ref[x + 1, e] = scale_at(x, e)

    for x in range(-2, SLAB + 1):
        for e in range(2):
            for t in range(2):
                part = slice(t * LANES, (t + 1) * LANES)
                low = {key: mode_at(x, k, e, part) for k, key in enumerate(KEYS)}
                high = {key: mode_at(x + 1, k, e, part) for k, key in enumerate(KEYS)}
                to_low, to_high = cell(low, high, scale_at(x, e)[:, part])
                for k, key in enumerate(KEYS):
                    if x > -2:
                        node[k, e, :, part] = to_low[key] + ahead[k, e, :, part]
                    ahead[k, e, :, part] = to_high[key]
        if x == -2:
            continue
        applied = from_modes({key: [node[k, e] for e in range(2)] for k, key in enumerate(KEYS)}, 1, 1)
        keep = at.inside(at.node_in, x, SLAB)
        for i in range(3):
            planes = [jnp.where(keep, res_at(x, i, e) - applied[i][e], 0.0) for e in range(2)]
            planes = spread_plane(planes, 1, 1)
            for e in range(2):
                gather[x + 1, i, e] = planes[e]
    rows_in = [
        gather[x + 1, i, e] + 0.5 * (gather[x, i, e] + gather[x + 2, i, e])
        for x in range(SLAB)
        for i in range(3)
        for e in range(2)
    ]
    parts = split_classes(jnp.concatenate(rows_in, axis=0)).reshape(SLAB, 3, 2, 8, WIDE)
    for x in range(SLAB):
        for e in range(2):
            for parity in range(2):
                part = slice(parity * LANES, (parity + 1) * LANES)
                young = split[1, x, e, :, part]
                mains = [parts[x, i, e, :, part] for i in range(3)] + [split[0, x, e, :, part]]
                for f in range(4):
                    piece = roll(young, WINDOW - PIECE * f, 1)
                    out_ref[e * 4 + (x % 2) * 2 + parity, x // 2, f] = jnp.where(
                        at.lanes < WINDOW, mains[f], piece
                    )


OWN = 32
HALO = 18
COUNT = OWN + HALO
PAD = 4
RES = (COUNT, 3, 8, LANES)
GAINS = (3, COUNT, 8, LANES)
SCALES = (3, PAD + COUNT, 8, LANES)
SPREAD = (2 * PAD + COUNT, 3, 8, LANES)
YOUNG = (COUNT + PAD, 8, LANES)
FREE = (COUNT, 8, LANES)
MODES = (2 * PAD + COUNT, 12, 8, LANES)
STATE = (RES, RES, GAINS, SCALES, SPREAD, SPREAD, SPREAD)
HEAD_SCRATCH = (YOUNG, FREE, RES, MODES, MODES)
TAIL_SCRATCH = (YOUNG, FREE, RES, MODES, MODES, *STATE, RES, (OWN + 8, 2, 8, LANES))
HEAD_POINTS = {1: (0, 18, 32, 16), 2: (0, 20, 30, 15), 3: (0, 22, 28, 14)}
HEAD_SWEEPS = {1: (0, 18, 32, 8), 2: (0, 20, 30, 10), 3: (0, 22, 28, 14)}
TAIL_POINTS = {1: (28, 0, 22, 11), 2: (24, 0, 26, 13), 3: (16, 2, 32, 16)}
TAIL_SWEEPS = {1: (30, 0, 20, 10), 2: (26, 2, 22, 11), 3: (20, 6, 24, 12)}
POINTS_UP = {2: (0, 11, 39, 13), 1: (0, 14, 36, 12)}
SWEEPS_UP = {2: (0, 11, 39, 13), 1: (0, 14, 36, 12)}


class Passes:
    def __init__(self, meta_ref, young, free, first, mode, ahead, state):
        self.half, origin = meta_ref[3], meta_ref[4]
        self.young, self.free, self.mode, self.ahead = young, free, mode, ahead
        self.res = {1: first, 2: state[0], 3: state[1]}
        self.gain, self.scale = state[2], state[3]
        self.spread = {1: state[4], 2: state[5], 3: state[6]}
        shape = (8, LANES)
        self.lanes, self.rows = lanes_of(shape), rows_of(shape)
        self.place = 2 * self.lanes + origin
        self.node_in = (self.place >= 0) & (self.place < 8 * LANES)
        self.first_in = self.node_in & (self.lanes >= 1) & (self.lanes < WINDOW - 1)
        self.zero = jnp.zeros(shape, F32)

    def loop(self, body, planes):
        low, high, count, unroll = planes
        begin = low + (high - low) * self.half

        def step(n, carry):
            for u in range(unroll):
                body(begin + unroll * n + u)
            return carry

        lax.fori_loop(0, count // unroll, step, 0)

    def clear(self):
        for p in range(PAD):
            self.young[COUNT + p] = self.zero
            for level in range(3):
                self.scale[level, p] = self.zero
            for spread in self.spread.values():
                for f in range(3):
                    spread[p, f] = self.zero
                    spread[PAD + COUNT + p, f] = self.zero
            for k in range(12):
                self.mode[p, k] = self.zero
                self.mode[PAD + COUNT + p, k] = self.zero

    def unpack(self, tiles, p):
        total = roll(tiles[0], -WINDOW, 1)
        for f in range(1, 4):
            total = jnp.where(self.lanes >= PIECE * f, roll(tiles[f], PIECE * f - WINDOW, 1), total)
        self.young[p] = total
        self.free[p] = jnp.where(self.first_in, tiles[3], 0.0)

    def unpack_first(self, tiles, p):
        for f in range(3):
            self.res[1][p, f] = jnp.where(self.first_in, tiles[f], 0.0)

    def coefficients(self, planes):
        for level in range(1, LEVELS):
            step, spacing = 2 ** (level - 1), 2**level
            cells = (self.place >= 0) & (self.place <= 8 * LANES - 1 - spacing) & (self.rows < 8 - step)

            def fill_scale(p):
                total = self.young[p] + self.young[p + step]
                total = total + roll(total, -step, 0)
                total = total + roll(total, -step, 1)
                inside = cells & (p + (2 * OWN - COUNT) * self.half < 2 * OWN - step)
                self.scale[level - 1, p + PAD] = jnp.where(inside, (0.125 * spacing) * total, 0.0)

            def fill_gain(p):
                total = self.scale[level - 1, p + PAD] + self.scale[level - 1, p + PAD - step]
                total = total + roll(total, step, 0)
                total = total + roll(total, step, 1)
                self.gain[level - 1, p] = GAIN * self.free[p] / jnp.maximum(total, TINY)

            self.loop(fill_scale, planes)
            self.loop(fill_gain, planes)

    def put_modes(self, p, fields, step):
        modes = to_modes([[f] for f in fields], step, step)
        for k, key in enumerate(KEYS):
            self.mode[PAD + p, k] = modes[key][0]

    def smooth(self, level, planes):
        step = 2 ** (level - 1)

        def body(p):
            fields = []
            for f in range(3):
                if level == 1:
                    now = self.res[1][p, f]
                else:
                    above, reach = self.spread[level - 1], step // 2
                    sides = above[PAD + p - reach, f] + above[PAD + p + reach, f]
                    now = jnp.where(self.node_in, above[PAD + p, f] + 0.5 * sides, 0.0)
                    self.res[level][p, f] = now
                fields.append(self.gain[level - 1, p] * now)
            self.put_modes(p, fields, step)

        self.loop(body, planes)

    def cell(self, level, p):
        step = 2 ** (level - 1)
        low = {key: self.mode[PAD + p, k] for k, key in enumerate(KEYS)}
        high = {key: self.mode[PAD + p + step, k] for k, key in enumerate(KEYS)}
        to_low, to_high = cell(low, high, self.scale[level - 1, p + PAD])
        return to_low, to_high

    def sweep(self, level, planes, finish, before=False):
        step = 2 ** (level - 1)
        begin = planes[0] + (planes[1] - planes[0]) * self.half
        for p in range(step):
            if before:
                to_high = self.cell(level, begin - step + p)[1]
            for k, key in enumerate(KEYS):
                self.ahead[begin + p, k] = to_high[key] if before else self.zero

        def body(p):
            to_low, to_high = self.cell(level, p)
            modes = {key: [to_low[key] + self.ahead[p, k]] for k, key in enumerate(KEYS)}
            for k, key in enumerate(KEYS):
                self.ahead[p + step, k] = to_high[key]
            finish(p, [a[0] for a in from_modes(modes, step, step)])

        self.loop(body, planes)

    def down(self, points, sweeps, before):
        for level in range(1, LEVELS):
            step = 2 ** (level - 1)
            spread = self.spread[level]

            def restrict(p, applied):
                for f in range(3):
                    rest = self.res[level][p, f] - applied[f]
                    spread[PAD + p, f] = spread_plane([rest], step, step)[0]

            def correct(p, applied):
                for f in range(3):
                    now = self.res[level][p, f]
                    spread[PAD + p, f] = self.gain[level - 1, p] * (now + (now - applied[f]))

            self.smooth(level, points[level])
            self.sweep(level, sweeps[level], restrict if level < LEVELS - 1 else correct, before)


def head_kernel(meta_ref, own_ref, *refs):
    state, (young, free, first, mode, ahead) = refs[: len(STATE)], refs[len(STATE) :]
    run = Passes(meta_ref, young, free, first, mode, ahead, state)
    run.clear()
    for p in range(OWN, COUNT - HALO + PAD):
        young[p] = run.zero
        free[p] = run.zero
        for k in range(12):
            mode[PAD + p, k] = run.zero
    for p in range(OWN):
        tiles = [own_ref[p, f] for f in range(4)]
        run.unpack(tiles, p + HALO * run.half)
        run.unpack_first(tiles, p + HALO * run.half)
    run.coefficients((0, HALO, OWN, 16))
    run.down(HEAD_POINTS, HEAD_SWEEPS, False)


def tail_kernel(meta_ref, own_ref, side_ref, *refs):
    given, out_ref, refs = refs[: len(STATE)], refs[len(STATE)], refs[len(STATE) + 1 :]
    young, free, first, mode, ahead = refs[:5]
    state, (value, last) = refs[5 : 5 + len(STATE)], refs[5 + len(STATE) :]
    run = Passes(meta_ref, young, free, first, mode, ahead, state)
    run.clear()

    def take(n, carry):
        for u in range(8):
            p = 8 * n + u
            q = p + HALO * run.half
            run.unpack_first([own_ref[p, f] for f in range(3)], q)
            for level in range(3):
                state[2][level, q] = given[2][level, q]
                state[3][level, q + PAD] = given[3][level, q + PAD]
            for f in range(3):
                for n_res in range(2):
                    state[n_res][q, f] = given[n_res][q, f]
                for n_spread in range(4, 7):
                    state[n_spread][PAD + q, f] = given[n_spread][PAD + q, f]
        return carry

    lax.fori_loop(0, OWN // 8, take, 0)
    for n in range(8):
        p = n + (OWN - 8) * (1 - run.half)
        run.unpack([own_ref[p, f] for f in range(4)], p + HALO * run.half)
    for p in range(HALO):
        tiles = [side_ref[p, f] for f in range(4)]
        run.unpack(tiles, p + OWN * (1 - run.half))
        run.unpack_first(tiles, p + OWN * (1 - run.half))
    run.coefficients((28, 0, 22, 22))
    run.down(TAIL_POINTS, TAIL_SWEEPS, True)

    last[3, 0] = last[3, 1] = run.zero
    last[OWN + 4, 0] = last[OWN + 4, 1] = run.zero
    for level in range(LEVELS - 2, 0, -1):
        step = 2 ** (level - 1)
        coarse = run.spread[level + 1]

        def prolong(p):
            fields = []
            for f in range(3):
                sides = coarse[PAD + p - step, f] + coarse[PAD + p + step, f]
                along = coarse[PAD + p, f] + 0.5 * sides
                along = spread_plane([along], step, step)[0]
                smoothed = run.gain[level - 1, p] * run.res[level][p, f]
                fields.append(jnp.where(run.node_in, smoothed + 0.125 * along, 0.0))
                value[p, f] = fields[f]
            run.put_modes(p, fields, step)

        def correct(p, applied):
            fields = []
            for f in range(3):
                rest = run.res[level][p, f] - applied[f]
                fields.append(value[p, f] + run.gain[level - 1, p] * rest)
            if level > 1:
                for f in range(3):
                    run.spread[level][PAD + p, f] = fields[f]
                return
            place = p + 4 - HALO * run.half
            for t in range(2):
                third = roll(fields[2], BACK - 17 - (BACK // 2) * t, 1)
                last[place, t] = jnp.where(run.lanes < BACK, roll(fields[t], -17, 1), third)

        run.loop(prolong, POINTS_UP[level])
        run.sweep(level, SWEEPS_UP[level], correct)
    for d in range(8):
        for p in range(6):
            for t in range(2):
                out_ref[d, p, t] = last[4 * d + p + 3, t]


LAST_SCRATCH = (
    (SLAB + 4, 3, 2, 8, WIDE),
    (SLAB + 2, 12, 2, 8, WIDE),
    (12, 2, 8, WIDE),
    (12, 2, 8, WIDE),
    (SLAB + 2, 3, 2, 8, LANES),
    (SLAB + 4, 3, 2, 8, WIDE),
)


def last_kernel(own_ref, value_ref, scale_ref, gain_ref, in_ref, out_ref, coarse, mode, ahead, node, field, gather):
    lanes = lanes_of((8, LANES))
    for n in range(SLAB + 4):
        slot, parity = n // 2, n % 2
        for e in range(2):
            tiles = [[in_ref[e * 4 + parity * 2 + w, slot, t] for t in range(2)] for w in range(2)]
            for w in range(2):
                part = slice(w * LANES, (w + 1) * LANES)
                first, second = tiles[w]
                third = jnp.where(
                    lanes < BACK // 2, roll(first, -BACK, 1), roll(second, BACK // 2 - BACK, 1)
                )
                gather[n, 0, e, :, part] = first
                gather[n, 1, e, :, part] = second
                gather[n, 2, e, :, part] = third
    source = rows_of((WIDE, WIDE))
    target = lanes_of((WIDE, WIDE))
    y = 2 * (source % LANES) - 2 + source // LANES
    choose = ((source % LANES) < BACK) & (target == (y + WIDE) % WIDE)
    full = jnp.dot(
        gather[...].reshape((SLAB + 4) * 48, WIDE),
        choose.astype(F32),
        preferred_element_type=F32,
        precision=lax.Precision.HIGHEST,
    )
    full = full.reshape(SLAB + 4, 3, 2, 8, WIDE)
    for n in range(SLAB + 4):
        for i in range(3):
            planes = spread_plane([full[n, i, e] for e in range(2)], 1, 1)
            for e in range(2):
                coarse[n, i, e] = planes[e]

    def prolong(n, carry):
        fields = []
        for i in range(3):
            planes = []
            for e in range(2):
                along = coarse[n + 1, i, e] + 0.5 * (coarse[n, i, e] + coarse[n + 2, i, e])
                planes.append(value_ref[n, i, e] + 0.125 * along)
                field[n, i, e] = planes[e][:, :LANES]
            fields.append(planes)
        modes = to_modes(fields, 1, 1)
        for k, key in enumerate(KEYS):
            for e in range(2):
                mode[n, k, e] = modes[key][e]
        return carry

    fori(SLAB + 2, prolong, LAST_UNROLL)

    for k in range(12):
        for e in range(2):
            ahead[k, e] = jnp.zeros((8, WIDE), F32)

    for n in range(SLAB + 1):
        x = n - 1
        for e in range(2):
            for t in range(2):
                part = slice(t * LANES, (t + 1) * LANES)
                low = {key: mode[n, k, e, :, part] for k, key in enumerate(KEYS)}
                high = {key: mode[n + 1, k, e, :, part] for k, key in enumerate(KEYS)}
                to_low, to_high = cell(low, high, scale_ref[n, e, :, part])
                for k, key in enumerate(KEYS):
                    if x >= 0:
                        node[k, e, :, part] = to_low[key] + ahead[k, e, :, part]
                    ahead[k, e, :, part] = to_high[key]
        if x < 0:
            continue
        modes = {key: [node[k, e] for e in range(2)] for k, key in enumerate(KEYS)}
        applied = from_modes(modes, 1, 1)
        for i in range(3):
            for e in range(2):
                rest = own_ref[x, i, e] - applied[i][e][:, :LANES]
                total = field[n, i, e] + gain_ref[x, e] * rest
                out_ref[i, pl.ds(e * 8 + x, 8, stride=16), :] = own_ref[x, 4, e] * total


def shapes(*sizes):
    return [jax.ShapeDtypeStruct(size, F32) for size in sizes]


def scratch(*sizes):
    return [pltpu.VMEM(size, F32) for size in sizes]


def call(kernel, name, out, scratches, scalars, arrays, space=pltpu.VMEM, limit=VMEM_BYTES):
    specs = [pl.BlockSpec(memory_space=pltpu.SMEM)] * len(scalars)
    specs += [pl.BlockSpec(memory_space=space)] * len(arrays)
    return pl.pallas_call(
        kernel,
        out_shape=out,
        in_specs=specs,
        out_specs=[pl.BlockSpec(memory_space=pltpu.VMEM)] * len(out),
        scratch_shapes=scratches,
        compiler_params=pltpu.CompilerParams(vmem_limit_bytes=limit),
        name=name,
    )(*scalars, *arrays)


def on_device(right_side, density, fixed_mask):
    slab, line = lax.axis_index("gx"), lax.axis_index("gy")
    slabs, lines = lax.axis_size("gx"), lax.axis_size("gy")
    core = slab % 2
    half = slab // 8
    origin = LANES * line - REACH + core
    meta = jnp.stack([slab, line, core, half, origin]).astype(jnp.int32)
    groups = [list(range(8)), list(range(8, 16))]
    rows = 16 * SLAB

    own, first, last = call(
        edges_kernel,
        "edges",
        shapes((SLAB, 5, 2, 8, LANES), (SLAB, 2, 2, 8, LANES), (SLAB, 2, 2, 8, LANES)),
        [
            pltpu.VMEM((3, rows, LANES), F32),
            pltpu.VMEM((rows, LANES), jnp.int32),
            pltpu.VMEM((rows, LANES), jnp.int32),
            pltpu.SemaphoreType.DMA((3,)),
        ],
        [],
        [right_side.reshape(3, rows, LANES), density.reshape(rows, LANES), fixed_mask.reshape(rows, LANES)],
        pltpu.HBM,
        EDGES_BYTES,
    )
    after = lax.ppermute(first, "gy", [((j + 1) % lines, j) for j in range(lines)])
    before = lax.ppermute(last, "gy", [(j, (j + 1) % lines) for j in range(lines)])

    def columns(begin):
        parts = [lax.dynamic_slice_in_dim(a, begin, 3, axis=0) for a in (own, after, before)]
        return jnp.concatenate(parts, axis=1)

    pair = lax.ppermute(columns(5 * (1 - core)), "gx", [(i, i ^ 1) for i in range(slabs)])
    swaps = [(i, (i + 1) % slabs) for i in range(1, slabs, 2)]
    far = lax.ppermute(columns(5 * core), "gx", swaps + [(b, a) for a, b in swaps])

    fine_state = call(
        fine_head_kernel,
        "fine_head",
        shapes(*FINE_STATE),
        scratch((2, SLAB, 2, 8, WIDE)),
        [meta],
        [own, after, before],
    )
    packed, value, scale, gain = call(
        fine_kernel,
        "fine",
        shapes(
            (8, 4, 4, 8, LANES),
            (SLAB + 2, 3, 2, 8, WIDE),
            (SLAB + 1, 2, 8, WIDE),
            (SLAB, 2, 8, LANES),
        ),
        scratch(*FINE_SCRATCH),
        [meta],
        [*fine_state, pair, far],
    )
    packed = lax.all_to_all(packed, "gx", 0, 0, axis_index_groups=groups)
    packed = packed.reshape(OWN, 4, 8, LANES)
    side = lax.dynamic_slice_in_dim(packed, (OWN - HALO) * (1 - half), HALO, axis=0)
    side = lax.ppermute(side, "gx", [(i, i ^ 8) for i in range(slabs)])
    state = call(head_kernel, "head", shapes(*STATE), scratch(*HEAD_SCRATCH), [meta], [packed])
    (result,) = call(
        tail_kernel,
        "tail",
        shapes((8, 6, 2, 8, LANES)),
        scratch(*TAIL_SCRATCH),
        [meta],
        [packed, side, *state],
    )
    result = lax.all_to_all(result, "gx", 0, 0, axis_index_groups=groups)
    (correction,) = call(
        last_kernel,
        "last",
        shapes((3, rows, LANES)),
        scratch(*LAST_SCRATCH),
        [],
        [own, value, scale, gain, result],
    )
    return correction.reshape(right_side.shape)


def solution(mesh):
    in_specs = (P(None, None, "gx", "gy"), P(None, "gx", "gy"), P(None, "gx", "gy"))
    out_specs = P(None, None, "gx", "gy")
    return jax.shard_map(
        on_device, mesh=mesh, in_specs=in_specs, out_specs=out_specs, check_vma=False
    )
```

time: 79.2 us -> 74 us (0.934)
  waiting for transfers between devices: 26.1 us -> 18.6 us
  Pallas kernels: 18.2 us -> 22.2 us
  local copies, waits for them, and re-layouts: 2.75 us -> 1.1 us
    ppermute x1, waiting for transfers between devices: 6.53 us -> 0.99 us  [on_device(): side = lax.ppermute(side, 'gx', [(i, i ^ 8) for i in range(slabs)])]
    pallas_call x4 -> x6, Pallas kernels: 18.2 us -> 22.2 us  [call(): pl.pallas_call(kernel, out_shape=out, in_specs=specs, out_specs=[pl.Block...]
    unnamed x6 -> x2, local copies, waits for them, and re-layouts: 2.6 us -> 0.01 us
    ppermute x1, waiting for transfers between devices: 4.16 us -> 3 us  [on_device(): lax.ppermute(columns(5 * core), 'gx', swaps + [(b, a) for a, b in swaps])]
    dynamic_slice x3, local copies, waits for them, and re-layouts: 0.04 us -> 0.99 us  [columns(): lax.dynamic_slice_in_dim(a, begin, 3, axis=0)]
  transfers between devices with their start and end apart: 6 -> 6, of which waited for: 5 -> 5; matrix products, arithmetic and copies ran while one was open for 0% -> 1% of each run, Pallas kernels for 0% -> 9%
where the time goes in v4:
time: 74 us; the launch traced here: 73.8 us
  Pallas kernels  22.2 us (30%)
  starting transfers between devices  19.5 us (26%)
  waiting for transfers between devices  18.6 us (25%)
  blocking collectives  12.2 us (16%)
  local copies, waits for them, and re-layouts  1.1 us (1%)
    pallas_call x6, Pallas kernels, call(): pl.pallas_call(kernel, out_shape=out, in_specs=specs, out_specs=[pl.Block...  22.2 us
    all_to_all x1, blocking collectives, on_device(): result = lax.all_to_all(result, 'gx', 0, 0, axis_index_groups=groups)  12.2 us
    all_to_all x1, waiting for transfers between devices, on_device(): packed = lax.all_to_all(packed, 'gx', 0, 0, axis_index_groups=groups)  9.48 us
    all_to_all x1, starting transfers between devices, on_device(): packed = lax.all_to_all(packed, 'gx', 0, 0, axis_index_groups=groups)  7.76 us
    ppermute x1, starting transfers between devices, on_device(): lax.ppermute(first, 'gy', [((j + 1) % lines, j) for j in range(lines)])  5.67 us
    ppermute x1, waiting for transfers between devices, on_device(): lax.ppermute(last, 'gy', [(j, (j + 1) % lines) for j in range(lines)])  3.65 us
    ppermute x1, waiting for transfers between devices, on_device(): lax.ppermute(columns(5 * core), 'gx', swaps + [(b, a) for a, b in swaps])  3 us
    ppermute x1, starting transfers between devices, on_device(): side = lax.ppermute(side, 'gx', [(i, i ^ 8) for i in range(slabs)])  2.7 us
  transfers between devices with their start and end apart: 6, of which 5 were waited for; matrix products, arithmetic and copies ran while one was open for 1% of the time, Pallas kernels for 9%

profile of v4, /device:TPU:1, one launch (start us, length us, event | category | flops | bytes accessed | tf_op | source)
XLA Modules:
  0.0 73.8 jit_solution(9095342012365985474)
XLA Ops:
  0.0 1.9 %edges.1 = (f32[8,5,2,8,128]{4,3,2,1,0:T(8,128)}, f32[8,2,2,8,128]{4,3,2,1,0:T(8,128)}, f32[8,2,2,8,128]{4,3,2,1,0:T(8,128)}) custom-call(f32[3,128,128]{2,1,0:T(8,128)} %bitcast.13, s32[128,128]{1,0:T(8,128)} %bitcast.14, s32[128,128]{1,0:T(8,128)} %bitcast.15), custom_call_target="tpu_custom_call" | custom-call | tf_op jit(solution)/shard_map/edges/pallas_call | solution.py:749
  1.9 0.0 copy-start
  1.9 5.7 %collective-permute-start = (f32[8,2,2,8,128]{4,3,2,1,0:T(8,128)}, f32[8,2,2,8,128]{4,3,2,1,0:T(8,128)S(1)}, u32[]{:S(2)}, u32[]{:S(2)}) collective-permute-start(f32[8,2,2,8,128]{4,3,2,1,0:T(8,128)} %get-tuple-element.27), channel_id=1, source_target_pairs={{1,0},{2,1},{3,2},{4,3},{5,4},{6,5},{7,6},{0,7},{9,8},{10,9},{11,1... | collective-permute-start | bytes 393224 | tf_op jit(solution)/shard_map/ppermute | solution.py:785
  7.6 0.0 collective-permute-start.1
  7.6 1.0 %constant_dynamic-slice_fusion.3 = (f32[3,5,2,8,128]{4,3,2,1,0:T(8,128)S(1)}, f32[3,5,2,8,128]{4,3,2,1,0:T(8,128)S(1)}) fusion(f32[8,5,2,8,128]{4,3,2,1,0:T(8,128)} %get-tuple-element.26.own_ref, s32[]{:T(128)S(6)} %select_n.27, s32[]{:T(128)S(6)} %select_n.26), kind=kLoop, calls=%fused_computation.5 | loop fusion | bytes 491528 | tf_op jit(solution)/shard_map/dynamic_slice | solution.py:789
  8.6 1.5 %collective-permute-done.after_ref = f32[8,2,2,8,128]{4,3,2,1,0:T(8,128)S(1)} collective-permute-done((f32[8,2,2,8,128]{4,3,2,1,0:T(8,128)}, f32[8,2,2,8,128]{4,3,2,1,0:T(8,128)S(1)}, u32[]{:S(2)}, u32[]{:S(2)}) %collective-permute-start) | collective-permute-done | bytes 131104 | tf_op jit(solution)/shard_map/ppermute | solution.py:785
  10.1 3.6 %collective-permute-done.1.before_ref = f32[8,2,2,8,128]{4,3,2,1,0:T(8,128)S(1)} collective-permute-done((f32[8,2,2,8,128]{4,3,2,1,0:T(8,128)}, f32[8,2,2,8,128]{4,3,2,1,0:T(8,128)S(1)}, u32[]{:S(2)}, u32[]{:S(2)}) %collective-permute-start.1) | collective-permute-done | bytes 131104 | tf_op jit(solution)/shard_map/ppermute | solution.py:786
  13.8 2.2 %collective-permute-start.2 = (f32[3,9,2,8,128]{4,3,2,1,0:T(8,128)S(1)}, f32[3,9,2,8,128]{4,3,2,1,0:T(8,128)S(1)}, u32[]{:S(2)}, u32[]{:S(2)}) collective-permute-start(f32[3,9,2,8,128]{4,3,2,1,0:T(8,128)S(1)} %pad_maximum_fusion), channel_id=1, source_target_pairs={{0,8},{8,0},{16,24},{24,16},{32,40},{40,32},{48,56},{56,48},{64,72... | collective-permute-start | bytes 663560 | tf_op jit(solution)/shard_map/ppermute | solution.py:792
  16.0 1.2 %collective-permute-start.3 = (f32[3,9,2,8,128]{4,3,2,1,0:T(8,128)S(1)}, f32[3,9,2,8,128]{4,3,2,1,0:T(8,128)S(1)}, u32[]{:S(2)}, u32[]{:S(2)}) collective-permute-start(f32[3,9,2,8,128]{4,3,2,1,0:T(8,128)S(1)} %pad_maximum_fusion.1), channel_id=1, source_target_pairs={{8,16},{24,32},{40,48},{56,64},{72,80},{88,96},{104,112},{120,0},{... | collective-permute-start | bytes 663560 | tf_op jit(solution)/shard_map/ppermute | solution.py:794
  17.2 0.1 stack.23.meta_ref
  17.3 0.0 copy-done
  17.3 1.1 %fine_head.1 = (f32[8,2,8,256]{3,2,1,0:T(8,128)S(1)}, f32[8,3,2,8,256]{4,3,2,1,0:T(8,128)S(1)}, f32[8,12,2,8,256]{4,3,2,1,0:T(8,128)S(1)}, f32[8,3,2,8,256]{4,3,...) custom-call(s32[5]{0:T(128)S(1)} %stack.23.meta_ref, ...), custom_call_target="tpu_custom_call" | custom-call | tf_op jit(solution)/shard_map/fine_head/pallas_call | solution.py:749
  18.4 0.0 collective-permute-done.2.pair_ref
  18.4 3.0 %collective-permute-done.3.far_ref = f32[3,9,2,8,128]{4,3,2,1,0:T(8,128)S(1)} collective-permute-done((f32[3,9,2,8,128]{4,3,2,1,0:T(8,128)S(1)}, f32[3,9,2,8,128]{4,3,2,1,0:T(8,128)S(1)}, u32[]{:S(2)}, u32[]{:S(2)}) %collective-permute-start.3) | collective-permute-done | bytes 221216 | tf_op jit(solution)/shard_map/ppermute | solution.py:794
  21.4 3.3 %fine.1 = (f32[8,4,4,8,128]{4,3,2,1,0:T(8,128)}, f32[10,3,2,8,256]{4,3,2,1,0:T(8,128)S(1)}, f32[9,2,8,256]{3,2,1,0:T(8,128)S(1)}, f32[8,2,8,128]{3,2,1,0:T(8,128)S(1)}) custom-call(s32[5]{0:T(128)S(1)} %stack.23.meta_ref, f32[8,2,8,256]{3,2,1,0:T(8,128)S(1)} %get-tuple-element.29.own_scale, f32[8,3,2,8,256]{4,3,2,1,0:T(8,128)S(1)} %get-tuple-element.30.own_res, ...), custom_call_target="tpu_custom_call" | custom-call | tf_op jit(solution)/shard_map/fine/pallas_call | solution.py:749
  24.7 7.8 %all-to-all-start = ((f32[8,4,4,8,128]{4,3,2,1,0:T(8,128)}), f32[8,4,4,8,128]{4,3,2,1,0:T(8,128)S(1)}, u32[]{:S(2)}, u32[]{:S(2)}) async-start(f32[8,4,4,8,128]{4,3,2,1,0:T(8,128)} %get-tuple-element.39), calls=%async_computation | async-start | bytes 1048576 | tf_op jit(solution)/shard_map/all_to_all | solution.py:817
  32.4 9.5 %all-to-all-done = f32[8,4,4,8,128]{4,3,2,1,0:T(8,128)S(1)} async-done(((f32[8,4,4,8,128]{4,3,2,1,0:T(8,128)}), f32[8,4,4,8,128]{4,3,2,1,0:T(8,128)S(1)}, u32[]{:S(2)}, u32[]{:S(2)}) %all-to-all-start) | async-done | bytes 524320 | tf_op jit(solution)/shard_map/all_to_all | solution.py:817
  41.9 2.7 %collective-permute-start.4 = (f32[18,4,8,128]{3,2,1,0:T(8,128)S(1)}, f32[18,4,8,128]{3,2,1,0:T(8,128)S(1)}, u32[]{:S(2)}, u32[]{:S(2)}) collective-permute-start(f32[18,4,8,128]{3,2,1,0:T(8,128)S(1)} %constant_dynamic-slice_fusion), channel_id=1, source_target_pairs={{0,64},{8,72},{16,80},{24,88},{32,96},{40,104},{48,112},{56,120},{... | collective-permute-start | bytes 884744 | tf_op jit(solution)/shard_map/ppermute | solution.py:820
  44.6 5.5 %head.1 = (f32[50,3,8,128]{3,2,1,0:T(8,128)S(1)}, f32[50,3,8,128]{3,2,1,0:T(8,128)S(1)}, f32[3,50,8,128]{3,2,1,0:T(8,128)S(1)}, f32[3,54,8,128]{3,2,1,0:T(8,128)...) custom-call(s32[5]{0:T(128)S(1)} %stack.23.meta_ref, ...), custom_call_target="tpu_custom_call" | custom-call | tf_op jit(solution)/shard_map/head/pallas_call | solution.py:749
  50.2 1.0 %collective-permute-done.4.side_ref = f32[18,4,8,128]{3,2,1,0:T(8,128)S(1)} collective-permute-done((f32[18,4,8,128]{3,2,1,0:T(8,128)S(1)}, f32[18,4,8,128]{3,2,1,0:T(8,128)S(1)}, u32[]{:S(2)}, u32[]{:S(2)}) %collective-permute-start.4) | collective-permute-done | bytes 294944 | tf_op jit(solution)/shard_map/ppermute | solution.py:820
  51.2 7.8 %tail.1 = f32[8,6,2,8,128]{4,3,2,1,0:T(8,128)S(1)} custom-call(s32[5]{0:T(128)S(1)} %stack.23.meta_ref, f32[32,4,8,128]{3,2,1,0:T(8,128)S(1)} %bitcast.12, f32[18,4,8,128]{3,2,1,0:T(8,128)S(1)} %collective-permute-done.4.side_ref, f32[50,3,8,128]{3,2,1,0:T(8,128)S(1)} %get-tuple-element.40.refs_0_, f32[50,3,8,128]{3,2,1,0:T(8,128)S(1)} %get-tuple-element.41.refs_1_, ...), custom_call_target="tpu_custom_call" | custom-call | tf_op jit(solution)/shard_map/tail/pallas_call | solution.py:749
  59.0 12.2 %all_to_all.10.in_ref = f32[8,6,2,8,128]{4,3,2,1,0:T(8,128)S(1)} all-to-all(f32[8,6,2,8,128]{4,3,2,1,0:T(8,128)S(1)} %tail.1), channel_id=1, replica_groups={{0,8,16,24,32,40,48,56},{64,72,80,88,96,104,112,120},{1,9,17,25,33,41,4..., dimensions={0} | all-to-all | bytes 786432 | tf_op jit(solution)/shard_map/all_to_all | solution.py:830
  71.2 2.6 %last.1 = f32[3,128,128]{2,1,0:T(8,128)} custom-call(f32[8,5,2,8,128]{4,3,2,1,0:T(8,128)S(1)} %copy-done, f32[10,3,2,8,256]{4,3,2,1,0:T(8,128)S(1)} %get-tuple-element.36.value_ref, f32[9,2,8,256]{3,2,1,0:T(8,128)S(1)} %get-tuple-element.37.scale_ref, f32[8,2,8,128]{3,2,1,0:T(8,128)S(1)} %get-tuple-element.38.gain_ref, ...), custom_call_target="tpu_custom_call" | custom-call | tf_op jit(solution)/shard_map/last/pallas_call | solution.py:749
  (5 shorter events, 0.1 us)
Async XLA Ops:
  1.9 15.3 %copy-start = (f32[8,5,2,8,128]{4,3,2,1,0:T(8,128)S(1)}, f32[8,5,2,8,128]{4,3,2,1,0:T(8,128)}, u32[]{:S(2)}) copy-start(f32[8,5,2,8,128]{4,3,2,1,0:T(8,128)} %get-tuple-element.26.own_ref) | copy-start | bytes 983044
  1.9 8.1 %collective-permute-start = (f32[8,2,2,8,128]{4,3,2,1,0:T(8,128)}, f32[8,2,2,8,128]{4,3,2,1,0:T(8,128)S(1)}, u32[]{:S(2)}, u32[]{:S(2)}) collective-permute-start(f32[8,2,2,8,128]{4,3,2,1,0:T(8,128)} %get-tuple-element.27), channel_id=1, source_target_pairs={{1,0},{2,1},{3,2},{4,3},{5,4},{6,5},{7,6},{0,7},{9,8},{10,9},{11,1... | collective-permute-start | bytes 393224 | tf_op jit(solution)/shard_map/ppermute | solution.py:785
  7.6 6.1 %collective-permute-start.1 = (f32[8,2,2,8,128]{4,3,2,1,0:T(8,128)}, f32[8,2,2,8,128]{4,3,2,1,0:T(8,128)S(1)}, u32[]{:S(2)}, u32[]{:S(2)}) collective-permute-start(f32[8,2,2,8,128]{4,3,2,1,0:T(8,128)} %get-tuple-element.28), channel_id=1, source_target_pairs={{0,1},{1,2},{2,3},{3,4},{4,5},{5,6},{6,7},{7,0},{8,9},{9,10},{10,1... | collective-permute-start | bytes 393224 | tf_op jit(solution)/shard_map/ppermute | solution.py:786
  13.8 4.6 %collective-permute-start.2 = (f32[3,9,2,8,128]{4,3,2,1,0:T(8,128)S(1)}, f32[3,9,2,8,128]{4,3,2,1,0:T(8,128)S(1)}, u32[]{:S(2)}, u32[]{:S(2)}) collective-permute-start(f32[3,9,2,8,128]{4,3,2,1,0:T(8,128)S(1)} %pad_maximum_fusion), channel_id=1, source_target_pairs={{0,8},{8,0},{16,24},{24,16},{32,40},{40,32},{48,56},{56,48},{64,72... | collective-permute-start | bytes 663560 | tf_op jit(solution)/shard_map/ppermute | solution.py:792
  16.0 5.4 %collective-permute-start.3 = (f32[3,9,2,8,128]{4,3,2,1,0:T(8,128)S(1)}, f32[3,9,2,8,128]{4,3,2,1,0:T(8,128)S(1)}, u32[]{:S(2)}, u32[]{:S(2)}) collective-permute-start(f32[3,9,2,8,128]{4,3,2,1,0:T(8,128)S(1)} %pad_maximum_fusion.1), channel_id=1, source_target_pairs={{8,16},{24,32},{40,48},{56,64},{72,80},{88,96},{104,112},{120,0},{... | collective-permute-start | bytes 663560 | tf_op jit(solution)/shard_map/ppermute | solution.py:794
  24.7 17.2 %all-to-all-start = ((f32[8,4,4,8,128]{4,3,2,1,0:T(8,128)}), f32[8,4,4,8,128]{4,3,2,1,0:T(8,128)S(1)}, u32[]{:S(2)}, u32[]{:S(2)}) async-start(f32[8,4,4,8,128]{4,3,2,1,0:T(8,128)} %get-tuple-element.39), calls=%async_computation | async-start | bytes 1048576 | tf_op jit(solution)/shard_map/all_to_all | solution.py:817
  41.9 9.2 %collective-permute-start.4 = (f32[18,4,8,128]{3,2,1,0:T(8,128)S(1)}, f32[18,4,8,128]{3,2,1,0:T(8,128)S(1)}, u32[]{:S(2)}, u32[]{:S(2)}) collective-permute-start(f32[18,4,8,128]{3,2,1,0:T(8,128)S(1)} %constant_dynamic-slice_fusion), channel_id=1, source_target_pairs={{0,64},{8,72},{16,80},{24,88},{32,96},{40,104},{48,112},{56,120},{... | collective-permute-start | bytes 884744 | tf_op jit(solution)/shard_map/ppermute | solution.py:820

commit v5 on v4

--- a/solution.py
+++ b/solution.py
@@ -147,6 +147,8 @@
         above = [above[0], jnp.where(rows < 7, above[1], 0.0)]
         below = [jnp.where(rows >= 1, below[0], 0.0), below[1]]
     along = [p + 0.5 * (a + b) for p, a, b in zip(planes, above, below)]
+    if not spacing:
+        return along
     return [p + 0.5 * (roll(p, spacing, 1) + roll(p, -spacing, 1)) for p in along]
 
 
@@ -240,17 +242,35 @@
         return gains, res, values
 
 
-def choose_class():
+def near(offset):
+    apart = (offset + WIDE) % WIDE
+    return jnp.where(apart == 0, 1.0, 0.0) + jnp.where((apart == 1) | (apart == WIDE - 1), 0.5, 0.0)
+
+
+def choose_class(spread):
     source = rows_of((WIDE, WIDE))
     target = lanes_of((WIDE, WIDE))
     y = 2 * (target % LANES) - REACH + target // LANES
-    return (((target % LANES) < WINDOW) & (source == (y + WIDE) % WIDE)).astype(F32)
-
-
-def split_classes(rows_in):
-    return jnp.dot(
-        rows_in, choose_class(), preferred_element_type=F32, precision=lax.Precision.HIGHEST
-    )
+    offset = source - (y + WIDE) % WIDE
+    weights = near(offset) if spread else jnp.where(offset == 0, 1.0, 0.0)
+    return jnp.where((target % LANES) < WINDOW, weights, 0.0).astype(jnp.bfloat16)
+
+
+def choose_place():
+    source = rows_of((WIDE, WIDE))
+    target = lanes_of((WIDE, WIDE))
+    y = 2 * (source % LANES) - 2 + source // LANES
+    weights = near(target - (y + WIDE) % WIDE)
+    return jnp.where((source % LANES) < BACK, weights, 0.0).astype(jnp.bfloat16)
+
+
+def select(rows_in, choose):
+    total = 0.0
+    for _ in range(3):
+        term = rows_in.astype(jnp.bfloat16)
+        rows_in = rows_in - term.astype(F32)
+        total = total + jnp.dot(term, choose, preferred_element_type=F32)
+    return total
 
 
 def put_smoothed(x, found, res_ref, mode_ref, gain_ref, value_ref, n_res, n_mode, n_gain, n_value):
@@ -267,6 +287,16 @@
             gain_ref[n_gain, e] = gains[e][:, :LANES]
 
 
+def leave(at, x, node, res, left, n):
+    applied = from_modes({key: [node[k, e] for e in range(2)] for k, key in enumerate(KEYS)}, 1, 1)
+    keep = at.inside(at.node_in, x, SLAB)
+    for i in range(3):
+        planes = [jnp.where(keep, r - a, 0.0) for r, a in zip(res[i], applied[i])]
+        planes = spread_plane(planes, 1, 0)
+        for e in range(2):
+            left[n, i, e] = planes[e]
+
+
 FINE_STATE = (
     (SLAB, 2, 8, WIDE),
     (SLAB, 3, 2, 8, WIDE),
@@ -274,13 +304,15 @@
     (SLAB, 3, 2, 8, WIDE),
     (SLAB, 2, 8, LANES),
     (4, 2, 8, WIDE),
-    (2, SLAB, 2, 8, WIDE),
+    (4, SLAB, 2, 2, 8, LANES),
+    (SLAB, 3, 2, 8, WIDE),
+    (2, 12, 2, 8, WIDE),
 )
 
 
 def fine_head_kernel(
     meta_ref, own_ref, after_ref, before_ref,
-    scale, res, mode, value, gain, edge, split, gather,
+    scale, res, mode, value, gain, edge, pieces, left, border, choose, gather, node, ahead,
 ):
     at = Fine(meta_ref)
 
@@ -305,12 +337,41 @@
         fields += [None, [gather[0, x, e] for e in range(2)]]
         scales = [[scale[x - d, e] for e in range(2)] for d in range(2)]
         put_smoothed(x, at.smooth(x, scales, fields), res, mode, gain, value, x, x, x, x)
-    parts = split_classes(gather[...].reshape(2 * SLAB * 16, WIDE))
-    split[...] = parts.reshape(2, SLAB, 2, 8, WIDE)
+    parts = select(gather[...].reshape(2 * SLAB * 16, WIDE), choose_class(False))
+    parts = parts.reshape(2, SLAB, 2, 8, WIDE)
+    for x in range(SLAB):
+        for e in range(2):
+            for parity in range(2):
+                part = slice(parity * LANES, (parity + 1) * LANES)
+                for f in range(4):
+                    tile = roll(parts[1, x, e, :, part], WINDOW - PIECE * f, 1)
+                    if f == 3:
+                        tile = jnp.where(at.lanes < WINDOW, parts[0, x, e, :, part], tile)
+                    pieces[f, x, e, parity] = tile
+    choose[...] = choose_class(True)
+
+    for x in range(1, SLAB - 1):
+        for e in range(2):
+            for t in range(2):
+                part = slice(t * LANES, (t + 1) * LANES)
+                low = {key: mode[x, k, e, :, part] for k, key in enumerate(KEYS)}
+                high = {key: mode[x + 1, k, e, :, part] for k, key in enumerate(KEYS)}
+                to_low, to_high = cell(low, high, scale[x, e, :, part])
+                for k, key in enumerate(KEYS):
+                    if x == 1:
+                        border[0, k, e, :, part] = to_low[key]
+                    else:
+                        node[k, e, :, part] = to_low[key] + ahead[k, e, :, part]
+                    if x < SLAB - 2:
+                        ahead[k, e, :, part] = to_high[key]
+                    else:
+                        border[1, k, e, :, part] = to_high[key]
+        if x > 1:
+            leave(at, x, node, [[res[x, i, e] for e in range(2)] for i in range(3)], left, x)
 
 
 def fine_kernel(
-    meta_ref, own_scale, own_res, own_mode, own_value, own_gain, edge, split, pair_ref, far_ref,
+    meta_ref, own_scale, own_res, own_mode, edge, pieces, left, border, choose, pair_ref, far_ref,
     out_ref, value_ref, scale_ref, gain_ref,
     res, scale, mode, ahead, node, gather,
 ):
@@ -318,11 +379,13 @@
 
     def field(x, f, e):
         group, n = f // 3, f % 3
-        p = x + 3 if x < 0 else x - SLAB
+        if x == -3:
+            slots = (18, 19, 20)
+        else:
+            p = x + 2 if x < 0 else x - SLAB
+            slots = (5 * p + f, 10 + 2 * p + group, 14 + 2 * p + group)
         is_pair = (at.core == 1) if x < 0 else (at.core == 0)
-        parts = [
-            jnp.where(is_pair, pair_ref[p, s, e], far_ref[p, s, e]) for s in (f, 5 + group, 7 + group)
-        ]
+        parts = [jnp.where(is_pair, pair_ref[s, e], far_ref[s, e]) for s in slots]
         return at.widen(n, *parts)
 
     def scale_at(x, e):
@@ -348,57 +411,51 @@
             fields = [[field(x, i, e) if i != 3 else None for e in range(2)] for i in range(5)]
         scales = [[scale_at(x - d, e) for e in range(2)] for d in range(2)]
         found = at.smooth(x, scales, fields)
-        inner = -1 <= x <= SLAB
-        put_smoothed(
-            x, found, res, mode, gain_ref, value_ref, n, n, 0 if x == 0 else None, x + 1 if inner else None
-        )
-    for x in range(1, SLAB):
-        for e in range(2):
-            gain_ref[x, e] = own_gain[x, e]
-            for i in range(3):
-                value_ref[x + 1, i, e] = own_value[x, i, e]
-    for x in range(-1, SLAB):
-        for e in range(2):
-            scale_ref[x + 1, e] = scale_at(x, e)
-
-    for x in range(-2, SLAB + 1):
+        n_value = {-1: 0, 0: 1, SLAB: 2}.get(x)
+        put_smoothed(x, found, res, mode, gain_ref, value_ref, n, n, 0 if x == 0 else None, n_value)
+    for e in range(2):
+        scale_ref[e] = scale_at(-1, e)
+
+    for x in (-2, -1, 0, 1, SLAB - 1, SLAB):
         for e in range(2):
             for t in range(2):
                 part = slice(t * LANES, (t + 1) * LANES)
+                if x == 1:
+                    for k, key in enumerate(KEYS):
+                        node[k, e, :, part] = border[0, k, e, :, part] + ahead[k, e, :, part]
+                    continue
                 low = {key: mode_at(x, k, e, part) for k, key in enumerate(KEYS)}
                 high = {key: mode_at(x + 1, k, e, part) for k, key in enumerate(KEYS)}
                 to_low, to_high = cell(low, high, scale_at(x, e)[:, part])
                 for k, key in enumerate(KEYS):
-                    if x > -2:
+                    if x == SLAB - 1:
+                        node[k, e, :, part] = to_low[key] + border[1, k, e, :, part]
+                    elif x > -2:
                         node[k, e, :, part] = to_low[key] + ahead[k, e, :, part]
                     ahead[k, e, :, part] = to_high[key]
-        if x == -2:
-            continue
-        applied = from_modes({key: [node[k, e] for e in range(2)] for k, key in enumerate(KEYS)}, 1, 1)
-        keep = at.inside(at.node_in, x, SLAB)
-        for i in range(3):
-            planes = [jnp.where(keep, res_at(x, i, e) - applied[i][e], 0.0) for e in range(2)]
-            planes = spread_plane(planes, 1, 1)
-            for e in range(2):
-                gather[x + 1, i, e] = planes[e]
+        if x > -2:
+            now = [[res_at(x, i, e) for e in range(2)] for i in range(3)]
+            leave(at, x, node, now, gather, x + 1)
+
+    def left_at(x, i, e):
+        return left[x, i, e] if 2 <= x < SLAB - 1 else gather[x + 1, i, e]
+
     rows_in = [
-        gather[x + 1, i, e] + 0.5 * (gather[x, i, e] + gather[x + 2, i, e])
+        left_at(x, i, e) + 0.5 * (left_at(x - 1, i, e) + left_at(x + 1, i, e))
         for x in range(SLAB)
         for i in range(3)
         for e in range(2)
     ]
-    parts = split_classes(jnp.concatenate(rows_in, axis=0)).reshape(SLAB, 3, 2, 8, WIDE)
+    parts = select(jnp.concatenate(rows_in, axis=0), choose[...]).reshape(SLAB, 3, 2, 8, WIDE)
     for x in range(SLAB):
         for e in range(2):
             for parity in range(2):
                 part = slice(parity * LANES, (parity + 1) * LANES)
-                young = split[1, x, e, :, part]
-                mains = [parts[x, i, e, :, part] for i in range(3)] + [split[0, x, e, :, part]]
                 for f in range(4):
-                    piece = roll(young, WINDOW - PIECE * f, 1)
-                    out_ref[e * 4 + (x % 2) * 2 + parity, x // 2, f] = jnp.where(
-                        at.lanes < WINDOW, mains[f], piece
-                    )
+                    tile = pieces[f, x, e, parity]
+                    if f < 3:
+                        tile = jnp.where(at.lanes < WINDOW, parts[x, f, e, :, part], tile)
+                    out_ref[e * 4 + (x % 2) * 2 + parity, x // 2, f] = tile
 
 
 OWN = 32
@@ -412,22 +469,23 @@
 YOUNG = (COUNT + PAD, 8, LANES)
 FREE = (COUNT, 8, LANES)
 MODES = (2 * PAD + COUNT, 12, 8, LANES)
-STATE = (RES, RES, GAINS, SCALES, SPREAD, SPREAD, SPREAD)
-HEAD_SCRATCH = (YOUNG, FREE, RES, MODES, MODES)
-TAIL_SCRATCH = (YOUNG, FREE, RES, MODES, MODES, *STATE, RES, (OWN + 8, 2, 8, LANES))
+STATE = (RES, RES, GAINS, SCALES, SPREAD, SPREAD, SPREAD, YOUNG, FREE, RES)
+HEAD_SCRATCH = (MODES, MODES)
+TAIL_SCRATCH = (MODES, MODES, RES, (OWN + 8, 2, 8, LANES))
 HEAD_POINTS = {1: (0, 18, 32, 16), 2: (0, 20, 30, 15), 3: (0, 22, 28, 14)}
 HEAD_SWEEPS = {1: (0, 18, 32, 8), 2: (0, 20, 30, 10), 3: (0, 22, 28, 14)}
-TAIL_POINTS = {1: (28, 0, 22, 11), 2: (24, 0, 26, 13), 3: (16, 2, 32, 16)}
-TAIL_SWEEPS = {1: (30, 0, 20, 10), 2: (26, 2, 22, 11), 3: (20, 6, 24, 12)}
-POINTS_UP = {2: (0, 11, 39, 13), 1: (0, 14, 36, 12)}
-SWEEPS_UP = {2: (0, 11, 39, 13), 1: (0, 14, 36, 12)}
+TAIL_POINTS = {1: (29, 1, 20, 20), 2: (24, 2, 24, 24), 3: (16, 6, 28, 28)}
+TAIL_SWEEPS = {1: (30, 2, 18, 9), 2: (26, 4, 20, 10), 3: (20, 10, 20, 10)}
+POINTS_UP = {2: (0, 12, 38, 19), 1: (0, 16, 34, 17)}
+SWEEPS_UP = {2: (0, 12, 38, 19), 1: (0, 16, 34, 17)}
 
 
 class Passes:
-    def __init__(self, meta_ref, young, free, first, mode, ahead, state):
+    def __init__(self, meta_ref, mode, ahead, state):
         self.half, origin = meta_ref[3], meta_ref[4]
-        self.young, self.free, self.mode, self.ahead = young, free, mode, ahead
-        self.res = {1: first, 2: state[0], 3: state[1]}
+        self.mode, self.ahead = mode, ahead
+        self.young, self.free = state[7], state[8]
+        self.res = {1: state[9], 2: state[0], 3: state[1]}
         self.gain, self.scale = state[2], state[3]
         self.spread = {1: state[4], 2: state[5], 3: state[6]}
         shape = (8, LANES)
@@ -450,6 +508,12 @@
 
     def clear(self):
         for p in range(PAD):
+            for k in range(12):
+                self.mode[p, k] = self.zero
+                self.mode[PAD + COUNT + p, k] = self.zero
+
+    def clear_state(self):
+        for p in range(PAD):
             self.young[COUNT + p] = self.zero
             for level in range(3):
                 self.scale[level, p] = self.zero
@@ -457,9 +521,6 @@
                 for f in range(3):
                     spread[p, f] = self.zero
                     spread[PAD + COUNT + p, f] = self.zero
-            for k in range(12):
-                self.mode[p, k] = self.zero
-                self.mode[PAD + COUNT + p, k] = self.zero
 
     def unpack(self, tiles, p):
         total = roll(tiles[0], -WINDOW, 1)
@@ -467,31 +528,36 @@
             total = jnp.where(self.lanes >= PIECE * f, roll(tiles[f], PIECE * f - WINDOW, 1), total)
         self.young[p] = total
         self.free[p] = jnp.where(self.first_in, tiles[3], 0.0)
-
-    def unpack_first(self, tiles, p):
         for f in range(3):
             self.res[1][p, f] = jnp.where(self.first_in, tiles[f], 0.0)
 
     def coefficients(self, planes):
-        for level in range(1, LEVELS):
-            step, spacing = 2 ** (level - 1), 2**level
-            cells = (self.place >= 0) & (self.place <= 8 * LANES - 1 - spacing) & (self.rows < 8 - step)
-
-            def fill_scale(p):
+        levels = [(level, 2 ** (level - 1), 2**level) for level in range(1, LEVELS)]
+        place, rows = self.place, self.rows
+        cells = [
+            (place >= 0) & (place <= 8 * LANES - 1 - spacing) & (rows < 8 - step)
+            for _, step, spacing in levels
+        ]
+
+        def fill_scale(p):
+            x = p + (2 * OWN - COUNT) * self.half
+            for (level, step, spacing), mask in zip(levels, cells):
                 total = self.young[p] + self.young[p + step]
                 total = total + roll(total, -step, 0)
                 total = total + roll(total, -step, 1)
-                inside = cells & (p + (2 * OWN - COUNT) * self.half < 2 * OWN - step)
+                inside = mask & (x < 2 * OWN - step)
                 self.scale[level - 1, p + PAD] = jnp.where(inside, (0.125 * spacing) * total, 0.0)
 
-            def fill_gain(p):
+        def fill_gain(p):
+            free = GAIN * self.free[p]
+            for level, step, _ in levels:
                 total = self.scale[level - 1, p + PAD] + self.scale[level - 1, p + PAD - step]
                 total = total + roll(total, step, 0)
                 total = total + roll(total, step, 1)
-                self.gain[level - 1, p] = GAIN * self.free[p] / jnp.maximum(total, TINY)
-
-            self.loop(fill_scale, planes)
-            self.loop(fill_gain, planes)
+                self.gain[level - 1, p] = free / jnp.maximum(total, TINY)
+
+        self.loop(fill_scale, planes)
+        self.loop(fill_gain, planes)
 
     def put_modes(self, p, fields, step):
         modes = to_modes([[f] for f in fields], step, step)
@@ -561,52 +627,28 @@
 
 
 def head_kernel(meta_ref, own_ref, *refs):
-    state, (young, free, first, mode, ahead) = refs[: len(STATE)], refs[len(STATE) :]
-    run = Passes(meta_ref, young, free, first, mode, ahead, state)
+    state, (place_ref, mode, ahead) = refs[: len(STATE)], refs[len(STATE) :]
+    place_ref[...] = choose_place()
+    run = Passes(meta_ref, mode, ahead, state)
     run.clear()
-    for p in range(OWN, COUNT - HALO + PAD):
-        young[p] = run.zero
-        free[p] = run.zero
+    run.clear_state()
+    for p in range(OWN, OWN + PAD):
+        run.young[p] = run.zero
         for k in range(12):
             mode[PAD + p, k] = run.zero
     for p in range(OWN):
-        tiles = [own_ref[p, f] for f in range(4)]
-        run.unpack(tiles, p + HALO * run.half)
-        run.unpack_first(tiles, p + HALO * run.half)
-    run.coefficients((0, HALO, OWN, 16))
+        run.unpack([own_ref[p, f] for f in range(4)], p + HALO * run.half)
+    run.coefficients((0, HALO, OWN, 8))
     run.down(HEAD_POINTS, HEAD_SWEEPS, False)
 
 
-def tail_kernel(meta_ref, own_ref, side_ref, *refs):
-    given, out_ref, refs = refs[: len(STATE)], refs[len(STATE)], refs[len(STATE) + 1 :]
-    young, free, first, mode, ahead = refs[:5]
-    state, (value, last) = refs[5 : 5 + len(STATE)], refs[5 + len(STATE) :]
-    run = Passes(meta_ref, young, free, first, mode, ahead, state)
+def tail_kernel(meta_ref, side_ref, *refs):
+    refs = refs[len(STATE) :]
+    out_ref, state, (mode, ahead, value, last) = refs[0], refs[1 : 1 + len(STATE)], refs[1 + len(STATE) :]
+    run = Passes(meta_ref, mode, ahead, state)
     run.clear()
-
-    def take(n, carry):
-        for u in range(8):
-            p = 8 * n + u
-            q = p + HALO * run.half
-            run.unpack_first([own_ref[p, f] for f in range(3)], q)
-            for level in range(3):
-                state[2][level, q] = given[2][level, q]
-                state[3][level, q + PAD] = given[3][level, q + PAD]
-            for f in range(3):
-                for n_res in range(2):
-                    state[n_res][q, f] = given[n_res][q, f]
-                for n_spread in range(4, 7):
-                    state[n_spread][PAD + q, f] = given[n_spread][PAD + q, f]
-        return carry
-
-    lax.fori_loop(0, OWN // 8, take, 0)
-    for n in range(8):
-        p = n + (OWN - 8) * (1 - run.half)
-        run.unpack([own_ref[p, f] for f in range(4)], p + HALO * run.half)
     for p in range(HALO):
-        tiles = [side_ref[p, f] for f in range(4)]
-        run.unpack(tiles, p + OWN * (1 - run.half))
-        run.unpack_first(tiles, p + OWN * (1 - run.half))
+        run.unpack([side_ref[p, f] for f in range(4)], p + OWN * (1 - run.half))
     run.coefficients((28, 0, 22, 22))
     run.down(TAIL_POINTS, TAIL_SWEEPS, True)
 
@@ -659,7 +701,10 @@
 )
 
 
-def last_kernel(own_ref, value_ref, scale_ref, gain_ref, in_ref, out_ref, coarse, mode, ahead, node, field, gather):
+def last_kernel(
+    own_ref, own_value, own_scale, own_gain, edge_value, edge_scale, edge_gain, place_ref, in_ref, out_ref,
+    coarse, mode, ahead, node, field, gather,
+):
     lanes = lanes_of((8, LANES))
     for n in range(SLAB + 4):
         slot, parity = n // 2, n % 2
@@ -674,20 +719,11 @@
                 gather[n, 0, e, :, part] = first
                 gather[n, 1, e, :, part] = second
                 gather[n, 2, e, :, part] = third
-    source = rows_of((WIDE, WIDE))
-    target = lanes_of((WIDE, WIDE))
-    y = 2 * (source % LANES) - 2 + source // LANES
-    choose = ((source % LANES) < BACK) & (target == (y + WIDE) % WIDE)
-    full = jnp.dot(
-        gather[...].reshape((SLAB + 4) * 48, WIDE),
-        choose.astype(F32),
-        preferred_element_type=F32,
-        precision=lax.Precision.HIGHEST,
-    )
+    full = select(gather[...].reshape((SLAB + 4) * 48, WIDE), place_ref[...])
     full = full.reshape(SLAB + 4, 3, 2, 8, WIDE)
     for n in range(SLAB + 4):
         for i in range(3):
-            planes = spread_plane([full[n, i, e] for e in range(2)], 1, 1)
+            planes = spread_plane([full[n, i, e] for e in range(2)], 1, 0)
             for e in range(2):
                 coarse[n, i, e] = planes[e]
 
@@ -697,7 +733,8 @@
             planes = []
             for e in range(2):
                 along = coarse[n + 1, i, e] + 0.5 * (coarse[n, i, e] + coarse[n + 2, i, e])
-                planes.append(value_ref[n, i, e] + 0.125 * along)
+                first = own_value[n - 1, i, e] if 2 <= n <= SLAB else edge_value[n % (SLAB - 1), i, e]
+                planes.append(first + 0.125 * along)
                 field[n, i, e] = planes[e][:, :LANES]
             fields.append(planes)
         modes = to_modes(fields, 1, 1)
@@ -719,7 +756,7 @@
                 part = slice(t * LANES, (t + 1) * LANES)
                 low = {key: mode[n, k, e, :, part] for k, key in enumerate(KEYS)}
                 high = {key: mode[n + 1, k, e, :, part] for k, key in enumerate(KEYS)}
-                to_low, to_high = cell(low, high, scale_ref[n, e, :, part])
+                to_low, to_high = cell(low, high, (own_scale[x, e] if x >= 0 else edge_scale[e])[:, part])
                 for k, key in enumerate(KEYS):
                     if x >= 0:
                         node[k, e, :, part] = to_low[key] + ahead[k, e, :, part]
@@ -731,7 +768,7 @@
         for i in range(3):
             for e in range(2):
                 rest = own_ref[x, i, e] - applied[i][e][:, :LANES]
-                total = field[n, i, e] + gain_ref[x, e] * rest
+                total = field[n, i, e] + (own_gain[x, e] if x > 0 else edge_gain[0, e]) * rest
                 out_ref[i, pl.ds(e * 8 + x, 8, stride=16), :] = own_ref[x, 4, e] * total
 
 
@@ -743,7 +780,7 @@
     return [pltpu.VMEM(size, F32) for size in sizes]
 
 
-def call(kernel, name, out, scratches, scalars, arrays, space=pltpu.VMEM, limit=VMEM_BYTES):
+def call(kernel, name, out, scratches, scalars, arrays, space=pltpu.VMEM, limit=VMEM_BYTES, aliases={}):
     specs = [pl.BlockSpec(memory_space=pltpu.SMEM)] * len(scalars)
     specs += [pl.BlockSpec(memory_space=space)] * len(arrays)
     return pl.pallas_call(
@@ -752,6 +789,7 @@
         in_specs=specs,
         out_specs=[pl.BlockSpec(memory_space=pltpu.VMEM)] * len(out),
         scratch_shapes=scratches,
+        input_output_aliases=aliases,
         compiler_params=pltpu.CompilerParams(vmem_limit_bytes=limit),
         name=name,
     )(*scalars, *arrays)
@@ -785,48 +823,49 @@
     after = lax.ppermute(first, "gy", [((j + 1) % lines, j) for j in range(lines)])
     before = lax.ppermute(last, "gy", [(j, (j + 1) % lines) for j in range(lines)])
 
-    def columns(begin):
-        parts = [lax.dynamic_slice_in_dim(a, begin, 3, axis=0) for a in (own, after, before)]
-        return jnp.concatenate(parts, axis=1)
-
-    pair = lax.ppermute(columns(5 * (1 - core)), "gx", [(i, i ^ 1) for i in range(slabs)])
+    def columns(begin, scale_only):
+        parts = [lax.dynamic_slice_in_dim(a, begin, 2, axis=0) for a in (own, after, before)]
+        parts = [p.reshape(-1, 2, 8, LANES) for p in parts]
+        for array, f in ((own, 3), (after, 1), (before, 1)):
+            parts.append(lax.dynamic_slice_in_dim(array[:, f], scale_only, 1, axis=0))
+        return jnp.concatenate(parts, axis=0)
+
     swaps = [(i, (i + 1) % slabs) for i in range(1, slabs, 2)]
-    far = lax.ppermute(columns(5 * core), "gx", swaps + [(b, a) for a, b in swaps])
-
-    fine_state = call(
+    far = lax.ppermute(columns(6 * core, 5 * core), "gx", swaps + [(b, a) for a, b in swaps])
+    pair = lax.ppermute(columns(6 * (1 - core), 5 * (1 - core)), "gx", [(i, i ^ 1) for i in range(slabs)])
+    matrix = [jax.ShapeDtypeStruct((WIDE, WIDE), jnp.bfloat16)]
+    own_scale, own_res, own_mode, own_value, own_gain, *rest = call(
         fine_head_kernel,
         "fine_head",
-        shapes(*FINE_STATE),
-        scratch((2, SLAB, 2, 8, WIDE)),
+        shapes(*FINE_STATE) + matrix,
+        scratch((2, SLAB, 2, 8, WIDE), (12, 2, 8, WIDE), (12, 2, 8, WIDE)),
         [meta],
         [own, after, before],
     )
-    packed, value, scale, gain = call(
+    packed, *edges = call(
         fine_kernel,
         "fine",
-        shapes(
-            (8, 4, 4, 8, LANES),
-            (SLAB + 2, 3, 2, 8, WIDE),
-            (SLAB + 1, 2, 8, WIDE),
-            (SLAB, 2, 8, LANES),
-        ),
+        shapes((8, 4, 4, 8, LANES), (3, 3, 2, 8, WIDE), (2, 8, WIDE), (1, 2, 8, LANES)),
         scratch(*FINE_SCRATCH),
         [meta],
-        [*fine_state, pair, far],
+        [own_scale, own_res, own_mode, *rest, pair, far],
     )
     packed = lax.all_to_all(packed, "gx", 0, 0, axis_index_groups=groups)
     packed = packed.reshape(OWN, 4, 8, LANES)
     side = lax.dynamic_slice_in_dim(packed, (OWN - HALO) * (1 - half), HALO, axis=0)
     side = lax.ppermute(side, "gx", [(i, i ^ 8) for i in range(slabs)])
-    state = call(head_kernel, "head", shapes(*STATE), scratch(*HEAD_SCRATCH), [meta], [packed])
-    (result,) = call(
+    *state, place = call(
+        head_kernel, "head", shapes(*STATE) + matrix, scratch(*HEAD_SCRATCH), [meta], [packed]
+    )
+    result = call(
         tail_kernel,
         "tail",
-        shapes((8, 6, 2, 8, LANES)),
+        shapes((8, 6, 2, 8, LANES), *STATE),
         scratch(*TAIL_SCRATCH),
         [meta],
-        [packed, side, *state],
-    )
+        [side, *state],
+        aliases={2 + n: 1 + n for n in range(len(STATE))},
+    )[0]
     result = lax.all_to_all(result, "gx", 0, 0, axis_index_groups=groups)
     (correction,) = call(
         last_kernel,
@@ -834,7 +873,7 @@
         shapes((3, rows, LANES)),
         scratch(*LAST_SCRATCH),
         [],
-        [own, value, scale, gain, result],
+        [own, own_value, own_scale, own_gain, *edges, place, result],
     )
     return correction.reshape(right_side.shape)
 

time: 74 us -> 70.7 us (0.955)
  waiting for transfers between devices: 18.6 us -> 15.1 us
  Pallas kernels: 22.2 us -> 20.6 us
  local copies, waits for them, and re-layouts: 1.1 us -> 1.99 us
  starting transfers between devices: 19.5 us -> 20.3 us
    ppermute x2, waiting for transfers between devices: 3 us -> 0.01 us  [the longest x1 0.01 us: on_device(): lax.ppermute(columns(6 * core, 5 * core), 'gx', swaps + [(b, a) for a, b...]
    ppermute x2, starting transfers between devices: 3.38 us -> 5.29 us  [the longest x1 3.28 us: on_device(): lax.ppermute(columns(6 * core, 5 * core), 'gx', swaps + [(b, a) for a, b...]
    pallas_call x6, Pallas kernels: 22.2 us -> 20.6 us  [call(): pl.pallas_call(kernel, out_shape=out, in_specs=specs, out_specs=[pl.Block...]
    all_to_all x1, starting transfers between devices: 7.76 us -> 6.63 us  [on_device(): packed = lax.all_to_all(packed, 'gx', 0, 0, axis_index_groups=groups)]
    slice x0 -> x3, local copies, waits for them, and re-layouts: none -> 0.86 us  [columns(): parts.append(lax.dynamic_slice_in_dim(array[:, f], scale_only, 1, axis=0))]
    ppermute x1, waiting for transfers between devices: 1.5 us -> 0.65 us  [on_device(): lax.ppermute(first, 'gy', [((j + 1) % lines, j) for j in range(lines)])]
  transfers between devices with their start and end apart: 6 -> 6, of which waited for: 5 -> 4; matrix products, arithmetic and copies ran while one was open for 1% -> 3% of each run, Pallas kernels for 9% -> 10%
where the time goes in v5:
time: 70.7 us; the launch traced here: 70.3 us
  Pallas kernels  20.6 us (29%)
  starting transfers between devices  20.3 us (29%)
  waiting for transfers between devices  15.1 us (21%)
  blocking collectives  12.2 us (17%)
  local copies, waits for them, and re-layouts  1.99 us (3%)
    pallas_call x6, Pallas kernels, call(): pl.pallas_call(kernel, out_shape=out, in_specs=specs, out_specs=[pl.Block...  20.6 us
    all_to_all x1, blocking collectives, on_device(): result = lax.all_to_all(result, 'gx', 0, 0, axis_index_groups=groups)  12.2 us
    all_to_all x1, waiting for transfers between devices, on_device(): packed = lax.all_to_all(packed, 'gx', 0, 0, axis_index_groups=groups)  9.5 us
    all_to_all x1, starting transfers between devices, on_device(): packed = lax.all_to_all(packed, 'gx', 0, 0, axis_index_groups=groups)  6.63 us
    ppermute x1, starting transfers between devices, on_device(): lax.ppermute(first, 'gy', [((j + 1) % lines, j) for j in range(lines)])  5.67 us
    ppermute x1, waiting for transfers between devices, on_device(): lax.ppermute(last, 'gy', [(j, (j + 1) % lines) for j in range(lines)])  3.66 us
    ppermute x1, starting transfers between devices, on_device(): lax.ppermute(columns(6 * core, 5 * core), 'gx', swaps + [(b, a) for a, b...  3.28 us
    ppermute x1, starting transfers between devices, on_device(): side = lax.ppermute(side, 'gx', [(i, i ^ 8) for i in range(slabs)])  2.7 us
  transfers between devices with their start and end apart: 6, of which 4 were waited for; matrix products, arithmetic and copies ran while one was open for 3% of the time, Pallas kernels for 10%

profile of v5, /device:TPU:1, one launch (start us, length us, event | category | flops | bytes accessed | tf_op | source)
XLA Modules:
  0.0 70.3 jit_solution(16969922890215205814)
XLA Ops:
  0.0 1.9 %edges.1 = (f32[8,5,2,8,128]{4,3,2,1,0:T(8,128)}, f32[8,2,2,8,128]{4,3,2,1,0:T(8,128)}, f32[8,2,2,8,128]{4,3,2,1,0:T(8,128)}) custom-call(f32[3,128,128]{2,1,0:T(8,128)} %bitcast.32, s32[128,128]{1,0:T(8,128)} %bitcast.37, s32[128,128]{1,0:T(8,128)} %bitcast.38), custom_call_target="tpu_custom_call" | custom-call | tf_op jit(solution)/shard_map/edges/pallas_call | solution.py:786
  1.9 0.0 copy-start
  1.9 5.7 %collective-permute-start = (f32[8,2,2,8,128]{4,3,2,1,0:T(8,128)}, f32[8,2,2,8,128]{4,3,2,1,0:T(8,128)S(1)}, u32[]{:S(2)}, u32[]{:S(2)}) collective-permute-start(f32[8,2,2,8,128]{4,3,2,1,0:T(8,128)} %get-tuple-element.35), channel_id=1, source_target_pairs={{1,0},{2,1},{3,2},{4,3},{5,4},{6,5},{7,6},{0,7},{9,8},{10,9},{11,1... | collective-permute-start | bytes 393224 | tf_op jit(solution)/shard_map/ppermute | solution.py:823
  7.6 0.0 collective-permute-start.1
  7.6 0.9 %constant_dynamic-slice_fusion.3 = (f32[2,5,2,8,128]{4,3,2,1,0:T(8,128)S(1)}, f32[2,5,2,8,128]{4,3,2,1,0:T(8,128)S(1)}) fusion(f32[8,5,2,8,128]{4,3,2,1,0:T(8,128)} %get-tuple-element.34.own_ref, s32[]{:T(128)S(6)} %select_n.38, s32[]{:T(128)S(6)} %select_n.36), kind=kLoop, calls=%fused_computation.15 | loop fusion | bytes 327688 | tf_op jit(solution)/shard_map/dynamic_slice | solution.py:827
  8.6 0.9 %slice.12 = f32[8,1,2,8,128]{4,3,2,1,0:T(8,128)S(1)} slice(f32[8,5,2,8,128]{4,3,2,1,0:T(8,128)} %get-tuple-element.34.own_ref), slice={[0:8], [3:4], [0:2], [0:8], [0:128]} | slice | bytes 131072 | tf_op jit(solution)/shard_map/slice | solution.py:830
  9.4 0.6 collective-permute-done.after_ref
  10.1 3.7 %collective-permute-done.1.before_ref = f32[8,2,2,8,128]{4,3,2,1,0:T(8,128)S(1)} collective-permute-done((f32[8,2,2,8,128]{4,3,2,1,0:T(8,128)}, f32[8,2,2,8,128]{4,3,2,1,0:T(8,128)S(1)}, u32[]{:S(2)}, u32[]{:S(2)}) %collective-permute-start.1) | collective-permute-done | bytes 131104 | tf_op jit(solution)/shard_map/ppermute | solution.py:824
  13.9 3.3 %collective-permute-start.3 = (f32[21,2,8,128]{3,2,1,0:T(8,128)S(1)}, f32[21,2,8,128]{3,2,1,0:T(8,128)S(1)}, u32[]{:S(2)}, u32[]{:S(2)}) collective-permute-start(f32[21,2,8,128]{3,2,1,0:T(8,128)S(1)} %get-tuple-element.69), channel_id=1, source_target_pairs={{8,16},{24,32},{40,48},{56,64},{72,80},{88,96},{104,112},{120,0},{... | collective-permute-start | bytes 516104 | tf_op jit(solution)/shard_map/ppermute | solution.py:834
  17.2 2.0 %collective-permute-start.2 = (f32[21,2,8,128]{3,2,1,0:T(8,128)S(1)}, f32[21,2,8,128]{3,2,1,0:T(8,128)S(1)}, u32[]{:S(2)}, u32[]{:S(2)}) collective-permute-start(f32[21,2,8,128]{3,2,1,0:T(8,128)S(1)} %get-tuple-element.70), channel_id=1, source_target_pairs={{0,8},{8,0},{16,24},{24,16},{32,40},{40,32},{48,56},{56,48},{64,72... | collective-permute-start | bytes 516104 | tf_op jit(solution)/shard_map/ppermute | solution.py:835
  19.2 0.1 stack.23.meta_ref
  19.3 0.0 copy-done
  19.3 2.0 %fine_head.1 = (f32[8,2,8,256]{3,2,1,0:T(8,128)S(1)}, f32[8,3,2,8,256]{4,3,2,1,0:T(8,128)S(1)}, f32[8,12,2,8,256]{4,3,2,1,0:T(8,128)S(1)}, f32[8,3,2,8,256]{4,3,...) custom-call(s32[5]{0:T(128)S(1)} %stack.23.meta_ref, ...), custom_call_target="tpu_custom_call" | custom-call | tf_op jit(solution)/shard_map/fine_head/pallas_call | solution.py:786
  21.3 0.0 collective-permute-done.3.far_ref
  21.3 0.0 collective-permute-done.2.pair_ref
  21.3 2.5 %fine.1 = (f32[8,4,4,8,128]{4,3,2,1,0:T(8,128)}, f32[3,3,2,8,256]{4,3,2,1,0:T(8,128)S(1)}, f32[2,8,256]{2,1,0:T(8,128)S(1)}, f32[1,2,8,128]{3,2,1,0:T(8,128)S(1)}) custom-call(s32[5]{0:T(128)S(1)} %stack.23.meta_ref, f32[8,2,8,256]{3,2,1,0:T(8,128)S(1)} %get-tuple-element.38.own_scale, f32[8,3,2,8,256]{4,3,2,1,0:T(8,128)S(1)} %get-tuple-element.40.own_res, ...), custom_call_target="tpu_custom_call" | custom-call | tf_op jit(solution)/shard_map/fine/pallas_call | solution.py:786
  23.8 6.6 %all-to-all-start = ((f32[8,4,4,8,128]{4,3,2,1,0:T(8,128)}), f32[8,4,4,8,128]{4,3,2,1,0:T(8,128)S(1)}, u32[]{:S(2)}, u32[]{:S(2)}) async-start(f32[8,4,4,8,128]{4,3,2,1,0:T(8,128)} %get-tuple-element.50), calls=%async_computation | async-start | bytes 1048576 | tf_op jit(solution)/shard_map/all_to_all | solution.py:853
  30.4 9.5 %all-to-all-done = f32[8,4,4,8,128]{4,3,2,1,0:T(8,128)S(1)} async-done(((f32[8,4,4,8,128]{4,3,2,1,0:T(8,128)}), f32[8,4,4,8,128]{4,3,2,1,0:T(8,128)S(1)}, u32[]{:S(2)}, u32[]{:S(2)}) %all-to-all-start) | async-done | bytes 524320 | tf_op jit(solution)/shard_map/all_to_all | solution.py:853
  40.0 2.7 %collective-permute-start.4 = (f32[18,4,8,128]{3,2,1,0:T(8,128)S(1)}, f32[18,4,8,128]{3,2,1,0:T(8,128)S(1)}, u32[]{:S(2)}, u32[]{:S(2)}) collective-permute-start(f32[18,4,8,128]{3,2,1,0:T(8,128)S(1)} %constant_dynamic-slice_fusion), channel_id=1, source_target_pairs={{0,64},{8,72},{16,80},{24,88},{32,96},{40,104},{48,112},{56,120},{... | collective-permute-start | bytes 884744 | tf_op jit(solution)/shard_map/ppermute | solution.py:856
  42.7 5.3 %head.1 = (f32[50,3,8,128]{3,2,1,0:T(8,128)S(1)}, f32[50,3,8,128]{3,2,1,0:T(8,128)S(1)}, f32[3,50,8,128]{3,2,1,0:T(8,128)S(1)}, f32[3,54,8,128]{3,2,1,0:T(8,128)...) custom-call(s32[5]{0:T(128)S(1)} %stack.23.meta_ref, ...), custom_call_target="tpu_custom_call" | custom-call | tf_op jit(solution)/shard_map/head/pallas_call | solution.py:786
  48.0 1.2 %collective-permute-done.4.side_ref = f32[18,4,8,128]{3,2,1,0:T(8,128)S(1)} collective-permute-done((f32[18,4,8,128]{3,2,1,0:T(8,128)S(1)}, f32[18,4,8,128]{3,2,1,0:T(8,128)S(1)}, u32[]{:S(2)}, u32[]{:S(2)}) %collective-permute-start.4) | collective-permute-done | bytes 294944 | tf_op jit(solution)/shard_map/ppermute | solution.py:856
  49.2 6.7 %tail.1 = (f32[8,6,2,8,128]{4,3,2,1,0:T(8,128)S(1)}, f32[50,3,8,128]{3,2,1,0:T(8,128)S(1)}, f32[50,3,8,128]{3,2,1,0:T(8,128)S(1)}, f32[3,50,8,128]{3,2,1,0:T(8,1...) custom-call(s32[5]{0:T(128)S(1)} %stack.23.meta_ref, ...), custom_call_target="tpu_custom_call", output_to_operand_aliasing={{1}: (2, {}), {2}: (3, {}), {3}: (4, {}), {4}: (5, {}), {5}... | custom-call | tf_op jit(solution)/shard_map/tail/pallas_call | solution.py:786
  55.9 12.2 %all_to_all.10.in_ref = f32[8,6,2,8,128]{4,3,2,1,0:T(8,128)S(1)} all-to-all(f32[8,6,2,8,128]{4,3,2,1,0:T(8,128)S(1)} %get-tuple-element.62), channel_id=1, replica_groups={{0,8,16,24,32,40,48,56},{64,72,80,88,96,104,112,120},{1,9,17,25,33,41,4..., dimensions={0} | all-to-all | bytes 786432 | tf_op jit(solution)/shard_map/all_to_all | solution.py:869
  68.2 2.2 %last.1 = f32[3,128,128]{2,1,0:T(8,128)} custom-call(f32[8,5,2,8,128]{4,3,2,1,0:T(8,128)S(1)} %copy-done, f32[8,3,2,8,256]{4,3,2,1,0:T(8,128)S(1)} %get-tuple-element.37.own_value, f32[8,2,8,256]{3,2,1,0:T(8,128)S(1)} %get-tuple-element.38.own_scale, f32[8,2,8,128]{3,2,1,0:T(8,128)S(1)} %get-tuple-element.39.own_gain, ...), custom_call_target="tpu_custom_call" | custom-call | tf_op jit(solution)/shard_map/last/pallas_call | solution.py:786
  (13 shorter events, 0.1 us)
Async XLA Ops:
  1.9 17.3 %copy-start = (f32[8,5,2,8,128]{4,3,2,1,0:T(8,128)S(1)}, f32[8,5,2,8,128]{4,3,2,1,0:T(8,128)}, u32[]{:S(2)}) copy-start(f32[8,5,2,8,128]{4,3,2,1,0:T(8,128)} %get-tuple-element.34.own_ref) | copy-start | bytes 983044
  1.9 8.1 %collective-permute-start = (f32[8,2,2,8,128]{4,3,2,1,0:T(8,128)}, f32[8,2,2,8,128]{4,3,2,1,0:T(8,128)S(1)}, u32[]{:S(2)}, u32[]{:S(2)}) collective-permute-start(f32[8,2,2,8,128]{4,3,2,1,0:T(8,128)} %get-tuple-element.35), channel_id=1, source_target_pairs={{1,0},{2,1},{3,2},{4,3},{5,4},{6,5},{7,6},{0,7},{9,8},{10,9},{11,1... | collective-permute-start | bytes 393224 | tf_op jit(solution)/shard_map/ppermute | solution.py:823
  7.6 6.1 %collective-permute-start.1 = (f32[8,2,2,8,128]{4,3,2,1,0:T(8,128)}, f32[8,2,2,8,128]{4,3,2,1,0:T(8,128)S(1)}, u32[]{:S(2)}, u32[]{:S(2)}) collective-permute-start(f32[8,2,2,8,128]{4,3,2,1,0:T(8,128)} %get-tuple-element.36), channel_id=1, source_target_pairs={{0,1},{1,2},{2,3},{3,4},{4,5},{5,6},{6,7},{7,0},{8,9},{9,10},{10,1... | collective-permute-start | bytes 393224 | tf_op jit(solution)/shard_map/ppermute | solution.py:824
  13.9 7.4 %collective-permute-start.3 = (f32[21,2,8,128]{3,2,1,0:T(8,128)S(1)}, f32[21,2,8,128]{3,2,1,0:T(8,128)S(1)}, u32[]{:S(2)}, u32[]{:S(2)}) collective-permute-start(f32[21,2,8,128]{3,2,1,0:T(8,128)S(1)} %get-tuple-element.69), channel_id=1, source_target_pairs={{8,16},{24,32},{40,48},{56,64},{72,80},{88,96},{104,112},{120,0},{... | collective-permute-start | bytes 516104 | tf_op jit(solution)/shard_map/ppermute | solution.py:834
  17.2 4.1 %collective-permute-start.2 = (f32[21,2,8,128]{3,2,1,0:T(8,128)S(1)}, f32[21,2,8,128]{3,2,1,0:T(8,128)S(1)}, u32[]{:S(2)}, u32[]{:S(2)}) collective-permute-start(f32[21,2,8,128]{3,2,1,0:T(8,128)S(1)} %get-tuple-element.70), channel_id=1, source_target_pairs={{0,8},{8,0},{16,24},{24,16},{32,40},{40,32},{48,56},{56,48},{64,72... | collective-permute-start | bytes 516104 | tf_op jit(solution)/shard_map/ppermute | solution.py:835
  23.8 16.1 %all-to-all-start = ((f32[8,4,4,8,128]{4,3,2,1,0:T(8,128)}), f32[8,4,4,8,128]{4,3,2,1,0:T(8,128)S(1)}, u32[]{:S(2)}, u32[]{:S(2)}) async-start(f32[8,4,4,8,128]{4,3,2,1,0:T(8,128)} %get-tuple-element.50), calls=%async_computation | async-start | bytes 1048576 | tf_op jit(solution)/shard_map/all_to_all | solution.py:853
  40.0 9.2 %collective-permute-start.4 = (f32[18,4,8,128]{3,2,1,0:T(8,128)S(1)}, f32[18,4,8,128]{3,2,1,0:T(8,128)S(1)}, u32[]{:S(2)}, u32[]{:S(2)}) collective-permute-start(f32[18,4,8,128]{3,2,1,0:T(8,128)S(1)} %constant_dynamic-slice_fusion), channel_id=1, source_target_pairs={{0,64},{8,72},{16,80},{24,88},{32,96},{40,104},{48,112},{56,120},{... | collective-permute-start | bytes 884744 | tf_op jit(solution)/shard_map/ppermute | solution.py:856

commit v6 on v5

--- a/solution.py
+++ b/solution.py
@@ -469,25 +469,28 @@
 YOUNG = (COUNT + PAD, 8, LANES)
 FREE = (COUNT, 8, LANES)
 MODES = (2 * PAD + COUNT, 12, 8, LANES)
-STATE = (RES, RES, GAINS, SCALES, SPREAD, SPREAD, SPREAD, YOUNG, FREE, RES)
-HEAD_SCRATCH = (MODES, MODES)
-TAIL_SCRATCH = (MODES, MODES, RES, (OWN + 8, 2, 8, LANES))
-HEAD_POINTS = {1: (0, 18, 32, 16), 2: (0, 20, 30, 15), 3: (0, 22, 28, 14)}
-HEAD_SWEEPS = {1: (0, 18, 32, 8), 2: (0, 20, 30, 10), 3: (0, 22, 28, 14)}
+BACK_TILES = (OWN + 8, 2, 8, LANES)
+STATE = (RES, RES, GAINS, SCALES, SPREAD, SPREAD, SPREAD, YOUNG, FREE, RES, SPREAD, BACK_TILES)
+CLASS_SCRATCH = (MODES, MODES, RES)
+HEAD_POINTS = {1: (0, 18, 32, 32), 2: (0, 20, 30, 30), 3: (0, 22, 28, 28)}
+HEAD_SWEEPS = {1: (0, 18, 32, 16), 2: (0, 20, 30, 15), 3: (0, 22, 28, 14)}
 TAIL_POINTS = {1: (29, 1, 20, 20), 2: (24, 2, 24, 24), 3: (16, 6, 28, 28)}
 TAIL_SWEEPS = {1: (30, 2, 18, 9), 2: (26, 4, 20, 10), 3: (20, 10, 20, 10)}
-POINTS_UP = {2: (0, 12, 38, 19), 1: (0, 16, 34, 17)}
-SWEEPS_UP = {2: (0, 12, 38, 19), 1: (0, 16, 34, 17)}
+HEAD_POINTS_UP = {2: (0, 30, 20, 20), 1: (0, 34, 16, 16)}
+HEAD_SWEEPS_UP = {2: (0, 30, 20, 10), 1: (0, 34, 16, 16)}
+TAIL_POINTS_UP = {2: (15, 13, 22, 11), 1: (14, 16, 20, 10)}
+TAIL_SWEEPS_UP = {2: (17, 15, 18, 9), 1: (15, 17, 18, 9)}
 
 
 class Passes:
-    def __init__(self, meta_ref, mode, ahead, state):
+    def __init__(self, meta_ref, mode, ahead, value, state):
         self.half, origin = meta_ref[3], meta_ref[4]
-        self.mode, self.ahead = mode, ahead
+        self.mode, self.ahead, self.value = mode, ahead, value
         self.young, self.free = state[7], state[8]
         self.res = {1: state[9], 2: state[0], 3: state[1]}
         self.gain, self.scale = state[2], state[3]
         self.spread = {1: state[4], 2: state[5], 3: state[6]}
+        self.corrected, self.last = {2: state[10], 3: state[6]}, state[11]
         shape = (8, LANES)
         self.lanes, self.rows = lanes_of(shape), rows_of(shape)
         self.place = 2 * self.lanes + origin
@@ -517,10 +520,13 @@
             self.young[COUNT + p] = self.zero
             for level in range(3):
                 self.scale[level, p] = self.zero
-            for spread in self.spread.values():
+            for spread in (*self.spread.values(), self.corrected[2]):
                 for f in range(3):
                     spread[p, f] = self.zero
                     spread[PAD + COUNT + p, f] = self.zero
+        for t in range(2):
+            self.last[3, t] = self.zero
+            self.last[OWN + 4, t] = self.zero
 
     def unpack(self, tiles, p):
         total = roll(tiles[0], -WINDOW, 1)
@@ -626,69 +632,72 @@
             self.sweep(level, sweeps[level], restrict if level < LEVELS - 1 else correct, before)
 
 
+    def up(self, points, sweeps, before):
+        for level in range(LEVELS - 2, 0, -1):
+            step = 2 ** (level - 1)
+            coarse = self.corrected[level + 1]
+
+            def prolong(p):
+                fields = []
+                for f in range(3):
+                    sides = coarse[PAD + p - step, f] + coarse[PAD + p + step, f]
+                    along = coarse[PAD + p, f] + 0.5 * sides
+                    along = spread_plane([along], step, step)[0]
+                    smoothed = self.gain[level - 1, p] * self.res[level][p, f]
+                    fields.append(jnp.where(self.node_in, smoothed + 0.125 * along, 0.0))
+                    self.value[p, f] = fields[f]
+                self.put_modes(p, fields, step)
+
+            def correct(p, applied):
+                fields = []
+                for f in range(3):
+                    rest = self.res[level][p, f] - applied[f]
+                    fields.append(self.value[p, f] + self.gain[level - 1, p] * rest)
+                if level > 1:
+                    for f in range(3):
+                        self.corrected[level][PAD + p, f] = fields[f]
+                    return
+                place = p + 4 - HALO * self.half
+                for t in range(2):
+                    third = roll(fields[2], BACK - 17 - (BACK // 2) * t, 1)
+                    first = roll(fields[t], -17, 1)
+                    self.last[place, t] = jnp.where(self.lanes < BACK, first, third)
+
+            self.loop(prolong, points[level])
+            self.sweep(level, sweeps[level], correct, before)
+
+
 def head_kernel(meta_ref, own_ref, *refs):
-    state, (place_ref, mode, ahead) = refs[: len(STATE)], refs[len(STATE) :]
+    state, (place_ref, *scratches) = refs[: len(STATE)], refs[len(STATE) :]
     place_ref[...] = choose_place()
-    run = Passes(meta_ref, mode, ahead, state)
+    run = Passes(meta_ref, *scratches, state)
     run.clear()
     run.clear_state()
     for p in range(OWN, OWN + PAD):
         run.young[p] = run.zero
         for k in range(12):
-            mode[PAD + p, k] = run.zero
+            run.mode[PAD + p, k] = run.zero
     for p in range(OWN):
         run.unpack([own_ref[p, f] for f in range(4)], p + HALO * run.half)
-    run.coefficients((0, HALO, OWN, 8))
+    run.coefficients((0, HALO, OWN, 16))
     run.down(HEAD_POINTS, HEAD_SWEEPS, False)
+    run.up(HEAD_POINTS_UP, HEAD_SWEEPS_UP, False)
 
 
 def tail_kernel(meta_ref, side_ref, *refs):
     refs = refs[len(STATE) :]
-    out_ref, state, (mode, ahead, value, last) = refs[0], refs[1 : 1 + len(STATE)], refs[1 + len(STATE) :]
-    run = Passes(meta_ref, mode, ahead, state)
+    out_ref, state, scratches = refs[0], refs[1 : 1 + len(STATE)], refs[1 + len(STATE) :]
+    run = Passes(meta_ref, *scratches, state)
     run.clear()
     for p in range(HALO):
         run.unpack([side_ref[p, f] for f in range(4)], p + OWN * (1 - run.half))
     run.coefficients((28, 0, 22, 22))
     run.down(TAIL_POINTS, TAIL_SWEEPS, True)
-
-    last[3, 0] = last[3, 1] = run.zero
-    last[OWN + 4, 0] = last[OWN + 4, 1] = run.zero
-    for level in range(LEVELS - 2, 0, -1):
-        step = 2 ** (level - 1)
-        coarse = run.spread[level + 1]
-
-        def prolong(p):
-            fields = []
-            for f in range(3):
-                sides = coarse[PAD + p - step, f] + coarse[PAD + p + step, f]
-                along = coarse[PAD + p, f] + 0.5 * sides
-                along = spread_plane([along], step, step)[0]
-                smoothed = run.gain[level - 1, p] * run.res[level][p, f]
-                fields.append(jnp.where(run.node_in, smoothed + 0.125 * along, 0.0))
-                value[p, f] = fields[f]
-            run.put_modes(p, fields, step)
-
-        def correct(p, applied):
-            fields = []
-            for f in range(3):
-                rest = run.res[level][p, f] - applied[f]
-                fields.append(value[p, f] + run.gain[level - 1, p] * rest)
-            if level > 1:
-                for f in range(3):
-                    run.spread[level][PAD + p, f] = fields[f]
-                return
-            place = p + 4 - HALO * run.half
-            for t in range(2):
-                third = roll(fields[2], BACK - 17 - (BACK // 2) * t, 1)
-                last[place, t] = jnp.where(run.lanes < BACK, roll(fields[t], -17, 1), third)
-
-        run.loop(prolong, POINTS_UP[level])
-        run.sweep(level, SWEEPS_UP[level], correct)
+    run.up(TAIL_POINTS_UP, TAIL_SWEEPS_UP, True)
     for d in range(8):
         for p in range(6):
             for t in range(2):
-                out_ref[d, p, t] = last[4 * d + p + 3, t]
+                out_ref[d, p, t] = run.last[4 * d + p + 3, t]
 
 
 LAST_SCRATCH = (
@@ -855,13 +864,13 @@
     side = lax.dynamic_slice_in_dim(packed, (OWN - HALO) * (1 - half), HALO, axis=0)
     side = lax.ppermute(side, "gx", [(i, i ^ 8) for i in range(slabs)])
     *state, place = call(
-        head_kernel, "head", shapes(*STATE) + matrix, scratch(*HEAD_SCRATCH), [meta], [packed]
+        head_kernel, "head", shapes(*STATE) + matrix, scratch(*CLASS_SCRATCH), [meta], [packed]
     )
     result = call(
         tail_kernel,
         "tail",
         shapes((8, 6, 2, 8, LANES), *STATE),
-        scratch(*TAIL_SCRATCH),
+        scratch(*CLASS_SCRATCH),
         [meta],
         [side, *state],
         aliases={2 + n: 1 + n for n in range(len(STATE))},

time: 70.7 us -> 69.2 us (0.979)
  waiting for transfers between devices: 15.1 us -> 14.1 us
    ppermute x1, waiting for transfers between devices: 1.25 us -> 0.3 us  [on_device(): side = lax.ppermute(side, 'gx', [(i, i ^ 8) for i in range(slabs)])]
  transfers between devices with their start and end apart: 6 -> 6, of which waited for: 4 -> 4; matrix products, arithmetic and copies ran while one was open for 3% -> 3% of each run, Pallas kernels for 10% -> 12%
where the time goes in v6:
time: 69.2 us; the launch traced here: 68.9 us
  starting transfers between devices  20.3 us (29%)
  Pallas kernels  20.1 us (29%)
  waiting for transfers between devices  14.1 us (20%)
  blocking collectives  12.2 us (18%)
  local copies, waits for them, and re-layouts  1.99 us (3%)
    pallas_call x6, Pallas kernels, call(): pl.pallas_call(kernel, out_shape=out, in_specs=specs, out_specs=[pl.Block...  20.1 us
    all_to_all x1, blocking collectives, on_device(): result = lax.all_to_all(result, 'gx', 0, 0, axis_index_groups=groups)  12.2 us
    all_to_all x1, waiting for transfers between devices, on_device(): packed = lax.all_to_all(packed, 'gx', 0, 0, axis_index_groups=groups)  9.5 us
    all_to_all x1, starting transfers between devices, on_device(): packed = lax.all_to_all(packed, 'gx', 0, 0, axis_index_groups=groups)  6.63 us
    ppermute x1, starting transfers between devices, on_device(): lax.ppermute(first, 'gy', [((j + 1) % lines, j) for j in range(lines)])  5.67 us
    ppermute x1, waiting for transfers between devices, on_device(): lax.ppermute(last, 'gy', [(j, (j + 1) % lines) for j in range(lines)])  3.66 us
    ppermute x1, starting transfers between devices, on_device(): lax.ppermute(columns(6 * core, 5 * core), 'gx', swaps + [(b, a) for a, b...  3.28 us
    ppermute x1, starting transfers between devices, on_device(): side = lax.ppermute(side, 'gx', [(i, i ^ 8) for i in range(slabs)])  2.7 us
  transfers between devices with their start and end apart: 6, of which 4 were waited for; matrix products, arithmetic and copies ran while one was open for 3% of the time, Pallas kernels for 12%

profile of v6, /device:TPU:1, one launch (start us, length us, event | category | flops | bytes accessed | tf_op | source)
XLA Modules:
  0.0 68.9 jit_solution(5576760641606475630)
XLA Ops:
  0.0 1.9 %edges.1 = (f32[8,5,2,8,128]{4,3,2,1,0:T(8,128)}, f32[8,2,2,8,128]{4,3,2,1,0:T(8,128)}, f32[8,2,2,8,128]{4,3,2,1,0:T(8,128)}) custom-call(f32[3,128,128]{2,1,0:T(8,128)} %bitcast.32, s32[128,128]{1,0:T(8,128)} %bitcast.37, s32[128,128]{1,0:T(8,128)} %bitcast.38), custom_call_target="tpu_custom_call" | custom-call | tf_op jit(solution)/shard_map/edges/pallas_call | solution.py:795
  1.9 0.0 copy-start
  1.9 5.7 %collective-permute-start = (f32[8,2,2,8,128]{4,3,2,1,0:T(8,128)}, f32[8,2,2,8,128]{4,3,2,1,0:T(8,128)S(1)}, u32[]{:S(2)}, u32[]{:S(2)}) collective-permute-start(f32[8,2,2,8,128]{4,3,2,1,0:T(8,128)} %get-tuple-element.37), channel_id=1, source_target_pairs={{1,0},{2,1},{3,2},{4,3},{5,4},{6,5},{7,6},{0,7},{9,8},{10,9},{11,1... | collective-permute-start | bytes 393224 | tf_op jit(solution)/shard_map/ppermute | solution.py:832
  7.6 0.0 collective-permute-start.1
  7.6 0.9 %constant_dynamic-slice_fusion.3 = (f32[2,5,2,8,128]{4,3,2,1,0:T(8,128)S(1)}, f32[2,5,2,8,128]{4,3,2,1,0:T(8,128)S(1)}) fusion(f32[8,5,2,8,128]{4,3,2,1,0:T(8,128)} %get-tuple-element.36.own_ref, s32[]{:T(128)S(6)} %select_n.38, s32[]{:T(128)S(6)} %select_n.36), kind=kLoop, calls=%fused_computation.15 | loop fusion | bytes 327688 | tf_op jit(solution)/shard_map/dynamic_slice | solution.py:836
  8.6 0.9 %slice.12 = f32[8,1,2,8,128]{4,3,2,1,0:T(8,128)S(1)} slice(f32[8,5,2,8,128]{4,3,2,1,0:T(8,128)} %get-tuple-element.36.own_ref), slice={[0:8], [3:4], [0:2], [0:8], [0:128]} | slice | bytes 131072 | tf_op jit(solution)/shard_map/slice | solution.py:839
  9.4 0.6 collective-permute-done.after_ref
  10.1 3.7 %collective-permute-done.1.before_ref = f32[8,2,2,8,128]{4,3,2,1,0:T(8,128)S(1)} collective-permute-done((f32[8,2,2,8,128]{4,3,2,1,0:T(8,128)}, f32[8,2,2,8,128]{4,3,2,1,0:T(8,128)S(1)}, u32[]{:S(2)}, u32[]{:S(2)}) %collective-permute-start.1) | collective-permute-done | bytes 131104 | tf_op jit(solution)/shard_map/ppermute | solution.py:833
  13.9 3.3 %collective-permute-start.3 = (f32[21,2,8,128]{3,2,1,0:T(8,128)S(1)}, f32[21,2,8,128]{3,2,1,0:T(8,128)S(1)}, u32[]{:S(2)}, u32[]{:S(2)}) collective-permute-start(f32[21,2,8,128]{3,2,1,0:T(8,128)S(1)} %get-tuple-element.73), channel_id=1, source_target_pairs={{8,16},{24,32},{40,48},{56,64},{72,80},{88,96},{104,112},{120,0},{... | collective-permute-start | bytes 516104 | tf_op jit(solution)/shard_map/ppermute | solution.py:843
  17.2 2.0 %collective-permute-start.2 = (f32[21,2,8,128]{3,2,1,0:T(8,128)S(1)}, f32[21,2,8,128]{3,2,1,0:T(8,128)S(1)}, u32[]{:S(2)}, u32[]{:S(2)}) collective-permute-start(f32[21,2,8,128]{3,2,1,0:T(8,128)S(1)} %get-tuple-element.74), channel_id=1, source_target_pairs={{0,8},{8,0},{16,24},{24,16},{32,40},{40,32},{48,56},{56,48},{64,72... | collective-permute-start | bytes 516104 | tf_op jit(solution)/shard_map/ppermute | solution.py:844
  19.2 0.1 stack.23.meta_ref
  19.3 0.0 copy-done
  19.3 2.0 %fine_head.1 = (f32[8,2,8,256]{3,2,1,0:T(8,128)S(1)}, f32[8,3,2,8,256]{4,3,2,1,0:T(8,128)S(1)}, f32[8,12,2,8,256]{4,3,2,1,0:T(8,128)S(1)}, f32[8,3,2,8,256]{4,3,...) custom-call(s32[5]{0:T(128)S(1)} %stack.23.meta_ref, ...), custom_call_target="tpu_custom_call" | custom-call | tf_op jit(solution)/shard_map/fine_head/pallas_call | solution.py:795
  21.3 0.0 collective-permute-done.3.far_ref
  21.3 0.0 collective-permute-done.2.pair_ref
  21.3 2.5 %fine.1 = (f32[8,4,4,8,128]{4,3,2,1,0:T(8,128)}, f32[3,3,2,8,256]{4,3,2,1,0:T(8,128)S(1)}, f32[2,8,256]{2,1,0:T(8,128)S(1)}, f32[1,2,8,128]{3,2,1,0:T(8,128)S(1)}) custom-call(s32[5]{0:T(128)S(1)} %stack.23.meta_ref, f32[8,2,8,256]{3,2,1,0:T(8,128)S(1)} %get-tuple-element.40.own_scale, f32[8,3,2,8,256]{4,3,2,1,0:T(8,128)S(1)} %get-tuple-element.42.own_res, ...), custom_call_target="tpu_custom_call" | custom-call | tf_op jit(solution)/shard_map/fine/pallas_call | solution.py:795
  23.8 6.6 %all-to-all-start = ((f32[8,4,4,8,128]{4,3,2,1,0:T(8,128)}), f32[8,4,4,8,128]{4,3,2,1,0:T(8,128)S(1)}, u32[]{:S(2)}, u32[]{:S(2)}) async-start(f32[8,4,4,8,128]{4,3,2,1,0:T(8,128)} %get-tuple-element.52), calls=%async_computation | async-start | bytes 1048576 | tf_op jit(solution)/shard_map/all_to_all | solution.py:862
  30.4 9.5 %all-to-all-done = f32[8,4,4,8,128]{4,3,2,1,0:T(8,128)S(1)} async-done(((f32[8,4,4,8,128]{4,3,2,1,0:T(8,128)}), f32[8,4,4,8,128]{4,3,2,1,0:T(8,128)S(1)}, u32[]{:S(2)}, u32[]{:S(2)}) %all-to-all-start) | async-done | bytes 524320 | tf_op jit(solution)/shard_map/all_to_all | solution.py:862
  40.0 2.7 %collective-permute-start.4 = (f32[18,4,8,128]{3,2,1,0:T(8,128)S(1)}, f32[18,4,8,128]{3,2,1,0:T(8,128)S(1)}, u32[]{:S(2)}, u32[]{:S(2)}) collective-permute-start(f32[18,4,8,128]{3,2,1,0:T(8,128)S(1)} %constant_dynamic-slice_fusion), channel_id=1, source_target_pairs={{0,64},{8,72},{16,80},{24,88},{32,96},{40,104},{48,112},{56,120},{... | collective-permute-start | bytes 884744 | tf_op jit(solution)/shard_map/ppermute | solution.py:865
  42.7 6.2 %head.1 = (f32[50,3,8,128]{3,2,1,0:T(8,128)S(1)}, f32[50,3,8,128]{3,2,1,0:T(8,128)S(1)}, f32[3,50,8,128]{3,2,1,0:T(8,128)S(1)}, f32[3,54,8,128]{3,2,1,0:T(8,128)...) custom-call(s32[5]{0:T(128)S(1)} %stack.23.meta_ref, ...), custom_call_target="tpu_custom_call" | custom-call | tf_op jit(solution)/shard_map/head/pallas_call | solution.py:795
  48.9 0.3 collective-permute-done.4.side_ref
  49.2 5.3 %tail.1 = (f32[8,6,2,8,128]{4,3,2,1,0:T(8,128)S(1)}, f32[50,3,8,128]{3,2,1,0:T(8,128)S(1)}, f32[50,3,8,128]{3,2,1,0:T(8,128)S(1)}, f32[3,50,8,128]{3,2,1,0:T(8,1...) custom-call(s32[5]{0:T(128)S(1)} %stack.23.meta_ref, ...), custom_call_target="tpu_custom_call", output_to_operand_aliasing={{1}: (2, {}), {2}: (3, {}), {3}: (4, {}), {4}: (5, {}), {5}... | custom-call | tf_op jit(solution)/shard_map/tail/pallas_call | solution.py:795
  54.5 12.2 %all_to_all.10.in_ref = f32[8,6,2,8,128]{4,3,2,1,0:T(8,128)S(1)} all-to-all(f32[8,6,2,8,128]{4,3,2,1,0:T(8,128)S(1)} %get-tuple-element.66), channel_id=1, replica_groups={{0,8,16,24,32,40,48,56},{64,72,80,88,96,104,112,120},{1,9,17,25,33,41,4..., dimensions={0} | all-to-all | bytes 786432 | tf_op jit(solution)/shard_map/all_to_all | solution.py:878
  66.7 2.2 %last.1 = f32[3,128,128]{2,1,0:T(8,128)} custom-call(f32[8,5,2,8,128]{4,3,2,1,0:T(8,128)S(1)} %copy-done, f32[8,3,2,8,256]{4,3,2,1,0:T(8,128)S(1)} %get-tuple-element.39.own_value, f32[8,2,8,256]{3,2,1,0:T(8,128)S(1)} %get-tuple-element.40.own_scale, f32[8,2,8,128]{3,2,1,0:T(8,128)S(1)} %get-tuple-element.41.own_gain, ...), custom_call_target="tpu_custom_call" | custom-call | tf_op jit(solution)/shard_map/last/pallas_call | solution.py:795
  (13 shorter events, 0.1 us)
Async XLA Ops:
  1.9 17.3 %copy-start = (f32[8,5,2,8,128]{4,3,2,1,0:T(8,128)S(1)}, f32[8,5,2,8,128]{4,3,2,1,0:T(8,128)}, u32[]{:S(2)}) copy-start(f32[8,5,2,8,128]{4,3,2,1,0:T(8,128)} %get-tuple-element.36.own_ref) | copy-start | bytes 983044
  1.9 8.1 %collective-permute-start = (f32[8,2,2,8,128]{4,3,2,1,0:T(8,128)}, f32[8,2,2,8,128]{4,3,2,1,0:T(8,128)S(1)}, u32[]{:S(2)}, u32[]{:S(2)}) collective-permute-start(f32[8,2,2,8,128]{4,3,2,1,0:T(8,128)} %get-tuple-element.37), channel_id=1, source_target_pairs={{1,0},{2,1},{3,2},{4,3},{5,4},{6,5},{7,6},{0,7},{9,8},{10,9},{11,1... | collective-permute-start | bytes 393224 | tf_op jit(solution)/shard_map/ppermute | solution.py:832
  7.6 6.1 %collective-permute-start.1 = (f32[8,2,2,8,128]{4,3,2,1,0:T(8,128)}, f32[8,2,2,8,128]{4,3,2,1,0:T(8,128)S(1)}, u32[]{:S(2)}, u32[]{:S(2)}) collective-permute-start(f32[8,2,2,8,128]{4,3,2,1,0:T(8,128)} %get-tuple-element.38), channel_id=1, source_target_pairs={{0,1},{1,2},{2,3},{3,4},{4,5},{5,6},{6,7},{7,0},{8,9},{9,10},{10,1... | collective-permute-start | bytes 393224 | tf_op jit(solution)/shard_map/ppermute | solution.py:833
  13.9 7.4 %collective-permute-start.3 = (f32[21,2,8,128]{3,2,1,0:T(8,128)S(1)}, f32[21,2,8,128]{3,2,1,0:T(8,128)S(1)}, u32[]{:S(2)}, u32[]{:S(2)}) collective-permute-start(f32[21,2,8,128]{3,2,1,0:T(8,128)S(1)} %get-tuple-element.73), channel_id=1, source_target_pairs={{8,16},{24,32},{40,48},{56,64},{72,80},{88,96},{104,112},{120,0},{... | collective-permute-start | bytes 516104 | tf_op jit(solution)/shard_map/ppermute | solution.py:843
  17.2 4.1 %collective-permute-start.2 = (f32[21,2,8,128]{3,2,1,0:T(8,128)S(1)}, f32[21,2,8,128]{3,2,1,0:T(8,128)S(1)}, u32[]{:S(2)}, u32[]{:S(2)}) collective-permute-start(f32[21,2,8,128]{3,2,1,0:T(8,128)S(1)} %get-tuple-element.74), channel_id=1, source_target_pairs={{0,8},{8,0},{16,24},{24,16},{32,40},{40,32},{48,56},{56,48},{64,72... | collective-permute-start | bytes 516104 | tf_op jit(solution)/shard_map/ppermute | solution.py:844
  23.8 16.1 %all-to-all-start = ((f32[8,4,4,8,128]{4,3,2,1,0:T(8,128)}), f32[8,4,4,8,128]{4,3,2,1,0:T(8,128)S(1)}, u32[]{:S(2)}, u32[]{:S(2)}) async-start(f32[8,4,4,8,128]{4,3,2,1,0:T(8,128)} %get-tuple-element.52), calls=%async_computation | async-start | bytes 1048576 | tf_op jit(solution)/shard_map/all_to_all | solution.py:862
  40.0 9.2 %collective-permute-start.4 = (f32[18,4,8,128]{3,2,1,0:T(8,128)S(1)}, f32[18,4,8,128]{3,2,1,0:T(8,128)S(1)}, u32[]{:S(2)}, u32[]{:S(2)}) collective-permute-start(f32[18,4,8,128]{3,2,1,0:T(8,128)S(1)} %constant_dynamic-slice_fusion), channel_id=1, source_target_pairs={{0,64},{8,72},{16,80},{24,88},{32,96},{40,104},{48,112},{56,120},{... | collective-permute-start | bytes 884744 | tf_op jit(solution)/shard_map/ppermute | solution.py:865

commit v7 on v6

--- a/solution.py
+++ b/solution.py
@@ -19,7 +19,7 @@
 SLAB = 8
 LANES = 128
 LAST_UNROLL = 10
-EDGE = 40
+EDGE = 36
 REACH = 36
 WINDOW = 100
 PIECE = WINDOW // 4
@@ -173,16 +173,21 @@
             fields = [free * right_ref[i, rows, :] for i in range(3)] + [UNIT * young, free]
             for f, value in enumerate(fields):
                 own_ref[x, f, e] = value
-            for group in range(2):
-                members = fields[3 * group : 3 * group + 3]
-                first = last = None
-                for n, value in enumerate(members):
-                    begin = roll(value, EDGE * n, 1)
-                    end = roll(value, EDGE * n - (LANES - EDGE), 1)
-                    first = begin if n == 0 else jnp.where(lanes < EDGE * n, first, begin)
-                    last = end if n == 0 else jnp.where(lanes < EDGE * n, last, end)
-                first_ref[x, group, e] = first
-                last_ref[x, group, e] = last
+    third = EDGE * 3
+    rest = LANES - third
+    for pair in range(SLAB // 2):
+        for e in range(2):
+            even, odd = ([own_ref[2 * pair + n, f, e] for f in range(5)] for n in range(2))
+            for target, start, more in ((first_ref, 0, 0), (last_ref, LANES - EDGE, 1)):
+                spare = [roll(even[3], third - start + more - rest * n, 1) for n in range(2)]
+                rows_of_slots = [even[:3] + [spare[0]], odd[:3] + [spare[1]], [even[4], odd[4], odd[3]]]
+                for t, slots in enumerate(rows_of_slots):
+                    tile = None
+                    for n, value in enumerate(slots):
+                        if n < 3:
+                            value = roll(value, EDGE * n - start + (more if (t, n) == (2, 2) else 0), 1)
+                        tile = value if n == 0 else jnp.where(lanes < EDGE * n, tile, value)
+                    target[pair, t, e] = tile
 
 
 WIDE = 2 * LANES
@@ -219,9 +224,22 @@
             return mask & jnp.logical_not(self.last_slab)
         return mask
 
-    def widen(self, n, mid, hi, lo):
-        hi = roll(hi, -EDGE * n, 1)
-        lo = roll(lo, (LANES - EDGE) - EDGE * n, 1)
+    def widen(self, odd, f, mid, after, before):
+        if f == 3 and not odd:
+            rest = LANES - 3 * EDGE
+            turn = LANES - EDGE - 1 - 3 * EDGE
+            hi = jnp.where(
+                self.lanes < rest, roll(after(0), -3 * EDGE, 1), roll(after(1), rest - 3 * EDGE, 1)
+            )
+            lo = jnp.where(
+                self.lanes < LANES - EDGE - 1 + rest,
+                roll(before(0), turn, 1),
+                roll(before(1), turn + rest, 1),
+            )
+        else:
+            t, n = (odd, f) if f < 3 else (2, 2 if f == 3 else odd)
+            hi = roll(after(t), -EDGE * n, 1)
+            lo = roll(before(t), LANES - EDGE - int(f == 3) - EDGE * n, 1)
         return jnp.concatenate([mid, jnp.where(self.lanes < 64, hi, lo)], axis=1)
 
     def cells(self, x, e, young):
@@ -317,8 +335,13 @@
     at = Fine(meta_ref)
 
     def field(x, f, e):
-        group, n = f // 3, f % 3
-        return at.widen(n, own_ref[x, f, e], after_ref[x, group, e], before_ref[x, group, e])
+        return at.widen(
+            x % 2,
+            f,
+            own_ref[x, f, e],
+            lambda t: after_ref[x // 2, t, e],
+            lambda t: before_ref[x // 2, t, e],
+        )
 
     for x in range(SLAB):
         for e in range(2):
@@ -378,15 +401,15 @@
     at = Fine(meta_ref)
 
     def field(x, f, e):
-        group, n = f // 3, f % 3
+        is_pair = (at.core == 1) if x < 0 else (at.core == 0)
+
+        def take(slot):
+            return jnp.where(is_pair, pair_ref[slot, e], far_ref[slot, e])
+
         if x == -3:
-            slots = (18, 19, 20)
-        else:
-            p = x + 2 if x < 0 else x - SLAB
-            slots = (5 * p + f, 10 + 2 * p + group, 14 + 2 * p + group)
-        is_pair = (at.core == 1) if x < 0 else (at.core == 0)
-        parts = [jnp.where(is_pair, pair_ref[s, e], far_ref[s, e]) for s in slots]
-        return at.widen(n, *parts)
+            return at.widen(1, f, take(16), lambda t: take(17), lambda t: take(18))
+        mid = take(5 * (x % 2) + f)
+        return at.widen(x % 2, f, mid, lambda t: take(10 + t), lambda t: take(13 + t))
 
     def scale_at(x, e):
         return own_scale[x, e] if 0 <= x < SLAB else scale[x + 3 if x < 0 else x - SLAB + 3, e]
@@ -817,7 +840,7 @@
     own, first, last = call(
         edges_kernel,
         "edges",
-        shapes((SLAB, 5, 2, 8, LANES), (SLAB, 2, 2, 8, LANES), (SLAB, 2, 2, 8, LANES)),
+        shapes((SLAB, 5, 2, 8, LANES), (SLAB // 2, 3, 2, 8, LANES), (SLAB // 2, 3, 2, 8, LANES)),
         [
             pltpu.VMEM((3, rows, LANES), F32),
             pltpu.VMEM((rows, LANES), jnp.int32),
@@ -832,16 +855,18 @@
     after = lax.ppermute(first, "gy", [((j + 1) % lines, j) for j in range(lines)])
     before = lax.ppermute(last, "gy", [(j, (j + 1) % lines) for j in range(lines)])
 
-    def columns(begin, scale_only):
-        parts = [lax.dynamic_slice_in_dim(a, begin, 2, axis=0) for a in (own, after, before)]
-        parts = [p.reshape(-1, 2, 8, LANES) for p in parts]
-        for array, f in ((own, 3), (after, 1), (before, 1)):
-            parts.append(lax.dynamic_slice_in_dim(array[:, f], scale_only, 1, axis=0))
+    def columns(right):
+        parts = [
+            lax.dynamic_slice_in_dim(a, n * right, size, axis=0).reshape(-1, 2, 8, LANES)
+            for a, n, size in ((own, 6, 2), (after, 3, 1), (before, 3, 1))
+        ]
+        for array, f, n in ((own, 3, 5), (after, 2, 2), (before, 2, 2)):
+            parts.append(lax.dynamic_slice_in_dim(array[:, f], n * right, 1, axis=0))
         return jnp.concatenate(parts, axis=0)
 
     swaps = [(i, (i + 1) % slabs) for i in range(1, slabs, 2)]
-    far = lax.ppermute(columns(6 * core, 5 * core), "gx", swaps + [(b, a) for a, b in swaps])
-    pair = lax.ppermute(columns(6 * (1 - core), 5 * (1 - core)), "gx", [(i, i ^ 1) for i in range(slabs)])
+    far = lax.ppermute(columns(core), "gx", swaps + [(b, a) for a, b in swaps])
+    pair = lax.ppermute(columns(1 - core), "gx", [(i, i ^ 1) for i in range(slabs)])
     matrix = [jax.ShapeDtypeStruct((WIDE, WIDE), jnp.bfloat16)]
     own_scale, own_res, own_mode, own_value, own_gain, *rest = call(
         fine_head_kernel,

time: 69.2 us -> 68.6 us (level)
  no operation moved by 1% of the time
where the time goes in v7:
time: 68.6 us; the launch traced here: 68.3 us
  Pallas kernels  20.1 us (29%)
  starting transfers between devices  20.1 us (29%)
  waiting for transfers between devices  13.8 us (20%)
  blocking collectives  12.2 us (18%)
  local copies, waits for them, and re-layouts  1.95 us (3%)
    pallas_call x6, Pallas kernels, call(): pl.pallas_call(kernel, out_shape=out, in_specs=specs, out_specs=[pl.Block...  20.1 us
    all_to_all x1, blocking collectives, on_device(): result = lax.all_to_all(result, 'gx', 0, 0, axis_index_groups=groups)  12.2 us
    all_to_all x1, waiting for transfers between devices, on_device(): packed = lax.all_to_all(packed, 'gx', 0, 0, axis_index_groups=groups)  9.5 us
    all_to_all x1, starting transfers between devices, on_device(): packed = lax.all_to_all(packed, 'gx', 0, 0, axis_index_groups=groups)  6.43 us
    ppermute x1, starting transfers between devices, on_device(): lax.ppermute(first, 'gy', [((j + 1) % lines, j) for j in range(lines)])  5.67 us
    ppermute x1, waiting for transfers between devices, on_device(): lax.ppermute(last, 'gy', [(j, (j + 1) % lines) for j in range(lines)])  3.82 us
    ppermute x1, starting transfers between devices, on_device(): far = lax.ppermute(columns(core), 'gx', swaps + [(b, a) for a, b in swaps])  3.28 us
    ppermute x1, starting transfers between devices, on_device(): side = lax.ppermute(side, 'gx', [(i, i ^ 8) for i in range(slabs)])  2.7 us
  transfers between devices with their start and end apart: 6, of which 4 were waited for; matrix products, arithmetic and copies ran while one was open for 3% of the time, Pallas kernels for 12%

profile of v7, /device:TPU:1, one launch (start us, length us, event | category | flops | bytes accessed | tf_op | source)
XLA Modules:
  0.0 68.3 jit_solution(8650931488313170340)
XLA Ops:
  0.0 1.9 %edges.1 = (f32[8,5,2,8,128]{4,3,2,1,0:T(8,128)}, f32[4,3,2,8,128]{4,3,2,1,0:T(8,128)}, f32[4,3,2,8,128]{4,3,2,1,0:T(8,128)}) custom-call(f32[3,128,128]{2,1,0:T(8,128)} %bitcast.36, s32[128,128]{1,0:T(8,128)} %bitcast.37, s32[128,128]{1,0:T(8,128)} %bitcast.38), custom_call_target="tpu_custom_call" | custom-call | tf_op jit(solution)/shard_map/edges/pallas_call | solution.py:818
  1.9 0.0 copy-start
  1.9 5.7 %collective-permute-start = (f32[4,3,2,8,128]{4,3,2,1,0:T(8,128)}, f32[4,3,2,8,128]{4,3,2,1,0:T(8,128)S(1)}, u32[]{:S(2)}, u32[]{:S(2)}) collective-permute-start(f32[4,3,2,8,128]{4,3,2,1,0:T(8,128)} %get-tuple-element.37), channel_id=1, source_target_pairs={{1,0},{2,1},{3,2},{4,3},{5,4},{6,5},{7,6},{0,7},{9,8},{10,9},{11,1... | collective-permute-start | bytes 294920 | tf_op jit(solution)/shard_map/ppermute | solution.py:855
  7.6 0.0 collective-permute-start.1
  7.6 0.8 %slice.12 = f32[8,1,2,8,128]{4,3,2,1,0:T(8,128)S(1)} slice(f32[8,5,2,8,128]{4,3,2,1,0:T(8,128)} %get-tuple-element.36.own_ref), slice={[0:8], [3:4], [0:2], [0:8], [0:128]} | slice | bytes 131072 | tf_op jit(solution)/shard_map/slice | solution.py:864
  8.4 0.9 %constant_dynamic-slice_fusion.1 = (f32[2,5,2,8,128]{4,3,2,1,0:T(8,128)S(1)}, f32[2,5,2,8,128]{4,3,2,1,0:T(8,128)S(1)}) fusion(f32[8,5,2,8,128]{4,3,2,1,0:T(8,128)} %get-tuple-element.36.own_ref, s32[]{:T(128)S(6)} %select_n.48, s32[]{:T(128)S(6)} %select_n.44), kind=kLoop, calls=%fused_computation.13 | loop fusion | bytes 327688 | tf_op jit(solution)/shard_map/dynamic_slice | solution.py:860
  9.4 0.1 collective-permute-done.after_ref
  9.5 3.8 %collective-permute-done.1.before_ref = f32[4,3,2,8,128]{4,3,2,1,0:T(8,128)S(1)} collective-permute-done((f32[4,3,2,8,128]{4,3,2,1,0:T(8,128)}, f32[4,3,2,8,128]{4,3,2,1,0:T(8,128)S(1)}, u32[]{:S(2)}, u32[]{:S(2)}) %collective-permute-start.1) | collective-permute-done | bytes 98336 | tf_op jit(solution)/shard_map/ppermute | solution.py:856
  13.4 3.3 %collective-permute-start.3 = (f32[19,2,8,128]{3,2,1,0:T(8,128)S(1)}, f32[19,2,8,128]{3,2,1,0:T(8,128)S(1)}, u32[]{:S(2)}, u32[]{:S(2)}) collective-permute-start(f32[19,2,8,128]{3,2,1,0:T(8,128)S(1)} %get-tuple-element.75), channel_id=1, source_target_pairs={{8,16},{24,32},{40,48},{56,64},{72,80},{88,96},{104,112},{120,0},{... | collective-permute-start | bytes 466952 | tf_op jit(solution)/shard_map/ppermute | solution.py:868
  16.7 2.0 %collective-permute-start.2 = (f32[19,2,8,128]{3,2,1,0:T(8,128)S(1)}, f32[19,2,8,128]{3,2,1,0:T(8,128)S(1)}, u32[]{:S(2)}, u32[]{:S(2)}) collective-permute-start(f32[19,2,8,128]{3,2,1,0:T(8,128)S(1)} %get-tuple-element.76), channel_id=1, source_target_pairs={{0,8},{8,0},{16,24},{24,16},{32,40},{40,32},{48,56},{56,48},{64,72... | collective-permute-start | bytes 466952 | tf_op jit(solution)/shard_map/ppermute | solution.py:869
  18.7 0.1 stack.23.meta_ref
  18.8 0.0 copy-done
  18.8 2.0 %fine_head.1 = (f32[8,2,8,256]{3,2,1,0:T(8,128)S(1)}, f32[8,3,2,8,256]{4,3,2,1,0:T(8,128)S(1)}, f32[8,12,2,8,256]{4,3,2,1,0:T(8,128)S(1)}, f32[8,3,2,8,256]{4,3,...) custom-call(s32[5]{0:T(128)S(1)} %stack.23.meta_ref, ...), custom_call_target="tpu_custom_call" | custom-call | tf_op jit(solution)/shard_map/fine_head/pallas_call | solution.py:818
  20.8 0.0 collective-permute-done.3.far_ref
  20.8 0.0 collective-permute-done.2.pair_ref
  20.9 2.5 %fine.1 = (f32[8,4,4,8,128]{4,3,2,1,0:T(8,128)}, f32[3,3,2,8,256]{4,3,2,1,0:T(8,128)S(1)}, f32[2,8,256]{2,1,0:T(8,128)S(1)}, f32[1,2,8,128]{3,2,1,0:T(8,128)S(1)}) custom-call(s32[5]{0:T(128)S(1)} %stack.23.meta_ref, f32[8,2,8,256]{3,2,1,0:T(8,128)S(1)} %get-tuple-element.40.own_scale, f32[8,3,2,8,256]{4,3,2,1,0:T(8,128)S(1)} %get-tuple-element.42.own_res, ...), custom_call_target="tpu_custom_call" | custom-call | tf_op jit(solution)/shard_map/fine/pallas_call | solution.py:818
  23.4 6.4 %all-to-all-start = ((f32[8,4,4,8,128]{4,3,2,1,0:T(8,128)}), f32[8,4,4,8,128]{4,3,2,1,0:T(8,128)S(1)}, u32[]{:S(2)}, u32[]{:S(2)}) async-start(f32[8,4,4,8,128]{4,3,2,1,0:T(8,128)} %get-tuple-element.52), calls=%async_computation | async-start | bytes 1048576 | tf_op jit(solution)/shard_map/all_to_all | solution.py:887
  29.8 9.5 %all-to-all-done = f32[8,4,4,8,128]{4,3,2,1,0:T(8,128)S(1)} async-done(((f32[8,4,4,8,128]{4,3,2,1,0:T(8,128)}), f32[8,4,4,8,128]{4,3,2,1,0:T(8,128)S(1)}, u32[]{:S(2)}, u32[]{:S(2)}) %all-to-all-start) | async-done | bytes 524320 | tf_op jit(solution)/shard_map/all_to_all | solution.py:887
  39.4 2.7 %collective-permute-start.4 = (f32[18,4,8,128]{3,2,1,0:T(8,128)S(1)}, f32[18,4,8,128]{3,2,1,0:T(8,128)S(1)}, u32[]{:S(2)}, u32[]{:S(2)}) collective-permute-start(f32[18,4,8,128]{3,2,1,0:T(8,128)S(1)} %constant_dynamic-slice_fusion), channel_id=1, source_target_pairs={{0,64},{8,72},{16,80},{24,88},{32,96},{40,104},{48,112},{56,120},{... | collective-permute-start | bytes 884744 | tf_op jit(solution)/shard_map/ppermute | solution.py:890
  42.1 6.2 %head.1 = (f32[50,3,8,128]{3,2,1,0:T(8,128)S(1)}, f32[50,3,8,128]{3,2,1,0:T(8,128)S(1)}, f32[3,50,8,128]{3,2,1,0:T(8,128)S(1)}, f32[3,54,8,128]{3,2,1,0:T(8,128)...) custom-call(s32[5]{0:T(128)S(1)} %stack.23.meta_ref, ...), custom_call_target="tpu_custom_call" | custom-call | tf_op jit(solution)/shard_map/head/pallas_call | solution.py:818
  48.3 0.3 collective-permute-done.4.side_ref
  48.6 5.3 %tail.1 = (f32[8,6,2,8,128]{4,3,2,1,0:T(8,128)S(1)}, f32[50,3,8,128]{3,2,1,0:T(8,128)S(1)}, f32[50,3,8,128]{3,2,1,0:T(8,128)S(1)}, f32[3,50,8,128]{3,2,1,0:T(8,1...) custom-call(s32[5]{0:T(128)S(1)} %stack.23.meta_ref, ...), custom_call_target="tpu_custom_call", output_to_operand_aliasing={{1}: (2, {}), {2}: (3, {}), {3}: (4, {}), {4}: (5, {}), {5}... | custom-call | tf_op jit(solution)/shard_map/tail/pallas_call | solution.py:818
  53.9 12.2 %all_to_all.10.in_ref = f32[8,6,2,8,128]{4,3,2,1,0:T(8,128)S(1)} all-to-all(f32[8,6,2,8,128]{4,3,2,1,0:T(8,128)S(1)} %get-tuple-element.66), channel_id=1, replica_groups={{0,8,16,24,32,40,48,56},{64,72,80,88,96,104,112,120},{1,9,17,25,33,41,4..., dimensions={0} | all-to-all | bytes 786432 | tf_op jit(solution)/shard_map/all_to_all | solution.py:903
  66.1 2.1 %last.1 = f32[3,128,128]{2,1,0:T(8,128)} custom-call(f32[8,5,2,8,128]{4,3,2,1,0:T(8,128)S(1)} %copy-done, f32[8,3,2,8,256]{4,3,2,1,0:T(8,128)S(1)} %get-tuple-element.39.own_value, f32[8,2,8,256]{3,2,1,0:T(8,128)S(1)} %get-tuple-element.40.own_scale, f32[8,2,8,128]{3,2,1,0:T(8,128)S(1)} %get-tuple-element.41.own_gain, ...), custom_call_target="tpu_custom_call" | custom-call | tf_op jit(solution)/shard_map/last/pallas_call | solution.py:818
  (9 shorter events, 0.1 us)
Async XLA Ops:
  1.9 16.9 %copy-start = (f32[8,5,2,8,128]{4,3,2,1,0:T(8,128)S(1)}, f32[8,5,2,8,128]{4,3,2,1,0:T(8,128)}, u32[]{:S(2)}) copy-start(f32[8,5,2,8,128]{4,3,2,1,0:T(8,128)} %get-tuple-element.36.own_ref) | copy-start | bytes 983044
  1.9 7.6 %collective-permute-start = (f32[4,3,2,8,128]{4,3,2,1,0:T(8,128)}, f32[4,3,2,8,128]{4,3,2,1,0:T(8,128)S(1)}, u32[]{:S(2)}, u32[]{:S(2)}) collective-permute-start(f32[4,3,2,8,128]{4,3,2,1,0:T(8,128)} %get-tuple-element.37), channel_id=1, source_target_pairs={{1,0},{2,1},{3,2},{4,3},{5,4},{6,5},{7,6},{0,7},{9,8},{10,9},{11,1... | collective-permute-start | bytes 294920 | tf_op jit(solution)/shard_map/ppermute | solution.py:855
  7.6 5.8 %collective-permute-start.1 = (f32[4,3,2,8,128]{4,3,2,1,0:T(8,128)}, f32[4,3,2,8,128]{4,3,2,1,0:T(8,128)S(1)}, u32[]{:S(2)}, u32[]{:S(2)}) collective-permute-start(f32[4,3,2,8,128]{4,3,2,1,0:T(8,128)} %get-tuple-element.38), channel_id=1, source_target_pairs={{0,1},{1,2},{2,3},{3,4},{4,5},{5,6},{6,7},{7,0},{8,9},{9,10},{10,1... | collective-permute-start | bytes 294920 | tf_op jit(solution)/shard_map/ppermute | solution.py:856
  13.4 7.4 %collective-permute-start.3 = (f32[19,2,8,128]{3,2,1,0:T(8,128)S(1)}, f32[19,2,8,128]{3,2,1,0:T(8,128)S(1)}, u32[]{:S(2)}, u32[]{:S(2)}) collective-permute-start(f32[19,2,8,128]{3,2,1,0:T(8,128)S(1)} %get-tuple-element.75), channel_id=1, source_target_pairs={{8,16},{24,32},{40,48},{56,64},{72,80},{88,96},{104,112},{120,0},{... | collective-permute-start | bytes 466952 | tf_op jit(solution)/shard_map/ppermute | solution.py:868
  16.7 4.1 %collective-permute-start.2 = (f32[19,2,8,128]{3,2,1,0:T(8,128)S(1)}, f32[19,2,8,128]{3,2,1,0:T(8,128)S(1)}, u32[]{:S(2)}, u32[]{:S(2)}) collective-permute-start(f32[19,2,8,128]{3,2,1,0:T(8,128)S(1)} %get-tuple-element.76), channel_id=1, source_target_pairs={{0,8},{8,0},{16,24},{24,16},{32,40},{40,32},{48,56},{56,48},{64,72... | collective-permute-start | bytes 466952 | tf_op jit(solution)/shard_map/ppermute | solution.py:869
  23.4 15.9 %all-to-all-start = ((f32[8,4,4,8,128]{4,3,2,1,0:T(8,128)}), f32[8,4,4,8,128]{4,3,2,1,0:T(8,128)S(1)}, u32[]{:S(2)}, u32[]{:S(2)}) async-start(f32[8,4,4,8,128]{4,3,2,1,0:T(8,128)} %get-tuple-element.52), calls=%async_computation | async-start | bytes 1048576 | tf_op jit(solution)/shard_map/all_to_all | solution.py:887
  39.4 9.2 %collective-permute-start.4 = (f32[18,4,8,128]{3,2,1,0:T(8,128)S(1)}, f32[18,4,8,128]{3,2,1,0:T(8,128)S(1)}, u32[]{:S(2)}, u32[]{:S(2)}) collective-permute-start(f32[18,4,8,128]{3,2,1,0:T(8,128)S(1)} %constant_dynamic-slice_fusion), channel_id=1, source_target_pairs={{0,64},{8,72},{16,80},{24,88},{32,96},{40,104},{48,112},{56,120},{... | collective-permute-start | bytes 884744 | tf_op jit(solution)/shard_map/ppermute | solution.py:890

commit v8 on v7

--- a/solution.py
+++ b/solution.py
@@ -282,9 +282,9 @@
     return jnp.where((source % LANES) < BACK, weights, 0.0).astype(jnp.bfloat16)
 
 
-def select(rows_in, choose):
+def select(rows_in, choose, terms):
     total = 0.0
-    for _ in range(3):
+    for _ in range(terms):
         term = rows_in.astype(jnp.bfloat16)
         rows_in = rows_in - term.astype(F32)
         total = total + jnp.dot(term, choose, preferred_element_type=F32)
@@ -360,7 +360,7 @@
         fields += [None, [gather[0, x, e] for e in range(2)]]
         scales = [[scale[x - d, e] for e in range(2)] for d in range(2)]
         put_smoothed(x, at.smooth(x, scales, fields), res, mode, gain, value, x, x, x, x)
-    parts = select(gather[...].reshape(2 * SLAB * 16, WIDE), choose_class(False))
+    parts = select(gather[...].reshape(2 * SLAB * 16, WIDE), choose_class(False), 3)
     parts = parts.reshape(2, SLAB, 2, 8, WIDE)
     for x in range(SLAB):
         for e in range(2):
@@ -469,7 +469,7 @@
         for i in range(3)
         for e in range(2)
     ]
-    parts = select(jnp.concatenate(rows_in, axis=0), choose[...]).reshape(SLAB, 3, 2, 8, WIDE)
+    parts = select(jnp.concatenate(rows_in, axis=0), choose[...], 2).reshape(SLAB, 3, 2, 8, WIDE)
     for x in range(SLAB):
         for e in range(2):
             for parity in range(2):
@@ -751,7 +751,7 @@
                 gather[n, 0, e, :, part] = first
                 gather[n, 1, e, :, part] = second
                 gather[n, 2, e, :, part] = third
-    full = select(gather[...].reshape((SLAB + 4) * 48, WIDE), place_ref[...])
+    full = select(gather[...].reshape((SLAB + 4) * 48, WIDE), place_ref[...], 2)
     full = full.reshape(SLAB + 4, 3, 2, 8, WIDE)
     for n in range(SLAB + 4):
         for i in range(3):

time: 68.6 us -> 68.4 us (level)
  no operation moved by 1% of the time
where the time goes in v8:
time: 68.4 us; the launch traced here: 68.1 us
  starting transfers between devices  20.1 us (29%)
  Pallas kernels  20 us (29%)
  waiting for transfers between devices  13.8 us (20%)
  blocking collectives  12.2 us (18%)
  local copies, waits for them, and re-layouts  1.95 us (3%)
    pallas_call x6, Pallas kernels, call(): pl.pallas_call(kernel, out_shape=out, in_specs=specs, out_specs=[pl.Block...  20 us
    all_to_all x1, blocking collectives, on_device(): result = lax.all_to_all(result, 'gx', 0, 0, axis_index_groups=groups)  12.2 us
    all_to_all x1, waiting for transfers between devices, on_device(): packed = lax.all_to_all(packed, 'gx', 0, 0, axis_index_groups=groups)  9.5 us
    all_to_all x1, starting transfers between devices, on_device(): packed = lax.all_to_all(packed, 'gx', 0, 0, axis_index_groups=groups)  6.43 us
    ppermute x1, starting transfers between devices, on_device(): lax.ppermute(first, 'gy', [((j + 1) % lines, j) for j in range(lines)])  5.67 us
    ppermute x1, waiting for transfers between devices, on_device(): lax.ppermute(last, 'gy', [(j, (j + 1) % lines) for j in range(lines)])  3.82 us
    ppermute x1, starting transfers between devices, on_device(): far = lax.ppermute(columns(core), 'gx', swaps + [(b, a) for a, b in swaps])  3.28 us
    ppermute x1, starting transfers between devices, on_device(): side = lax.ppermute(side, 'gx', [(i, i ^ 8) for i in range(slabs)])  2.7 us
  transfers between devices with their start and end apart: 6, of which 4 were waited for; matrix products, arithmetic and copies ran while one was open for 3% of the time, Pallas kernels for 12%

profile of v8, /device:TPU:1, one launch (start us, length us, event | category | flops | bytes accessed | tf_op | source)
XLA Modules:
  0.0 68.1 jit_solution(16717574050896543607)
XLA Ops:
  0.0 1.9 %edges.1 = (f32[8,5,2,8,128]{4,3,2,1,0:T(8,128)}, f32[4,3,2,8,128]{4,3,2,1,0:T(8,128)}, f32[4,3,2,8,128]{4,3,2,1,0:T(8,128)}) custom-call(f32[3,128,128]{2,1,0:T(8,128)} %bitcast.36, s32[128,128]{1,0:T(8,128)} %bitcast.37, s32[128,128]{1,0:T(8,128)} %bitcast.38), custom_call_target="tpu_custom_call" | custom-call | tf_op jit(solution)/shard_map/edges/pallas_call | solution.py:818
  1.9 0.0 copy-start
  1.9 5.7 %collective-permute-start = (f32[4,3,2,8,128]{4,3,2,1,0:T(8,128)}, f32[4,3,2,8,128]{4,3,2,1,0:T(8,128)S(1)}, u32[]{:S(2)}, u32[]{:S(2)}) collective-permute-start(f32[4,3,2,8,128]{4,3,2,1,0:T(8,128)} %get-tuple-element.37), channel_id=1, source_target_pairs={{1,0},{2,1},{3,2},{4,3},{5,4},{6,5},{7,6},{0,7},{9,8},{10,9},{11,1... | collective-permute-start | bytes 294920 | tf_op jit(solution)/shard_map/ppermute | solution.py:855
  7.6 0.0 collective-permute-start.1
  7.6 0.8 %slice.12 = f32[8,1,2,8,128]{4,3,2,1,0:T(8,128)S(1)} slice(f32[8,5,2,8,128]{4,3,2,1,0:T(8,128)} %get-tuple-element.36.own_ref), slice={[0:8], [3:4], [0:2], [0:8], [0:128]} | slice | bytes 131072 | tf_op jit(solution)/shard_map/slice | solution.py:864
  8.4 0.9 %constant_dynamic-slice_fusion.1 = (f32[2,5,2,8,128]{4,3,2,1,0:T(8,128)S(1)}, f32[2,5,2,8,128]{4,3,2,1,0:T(8,128)S(1)}) fusion(f32[8,5,2,8,128]{4,3,2,1,0:T(8,128)} %get-tuple-element.36.own_ref, s32[]{:T(128)S(6)} %select_n.48, s32[]{:T(128)S(6)} %select_n.44), kind=kLoop, calls=%fused_computation.13 | loop fusion | bytes 327688 | tf_op jit(solution)/shard_map/dynamic_slice | solution.py:860
  9.4 0.1 collective-permute-done.after_ref
  9.5 3.8 %collective-permute-done.1.before_ref = f32[4,3,2,8,128]{4,3,2,1,0:T(8,128)S(1)} collective-permute-done((f32[4,3,2,8,128]{4,3,2,1,0:T(8,128)}, f32[4,3,2,8,128]{4,3,2,1,0:T(8,128)S(1)}, u32[]{:S(2)}, u32[]{:S(2)}) %collective-permute-start.1) | collective-permute-done | bytes 98336 | tf_op jit(solution)/shard_map/ppermute | solution.py:856
  13.4 3.3 %collective-permute-start.3 = (f32[19,2,8,128]{3,2,1,0:T(8,128)S(1)}, f32[19,2,8,128]{3,2,1,0:T(8,128)S(1)}, u32[]{:S(2)}, u32[]{:S(2)}) collective-permute-start(f32[19,2,8,128]{3,2,1,0:T(8,128)S(1)} %get-tuple-element.75), channel_id=1, source_target_pairs={{8,16},{24,32},{40,48},{56,64},{72,80},{88,96},{104,112},{120,0},{... | collective-permute-start | bytes 466952 | tf_op jit(solution)/shard_map/ppermute | solution.py:868
  16.7 2.0 %collective-permute-start.2 = (f32[19,2,8,128]{3,2,1,0:T(8,128)S(1)}, f32[19,2,8,128]{3,2,1,0:T(8,128)S(1)}, u32[]{:S(2)}, u32[]{:S(2)}) collective-permute-start(f32[19,2,8,128]{3,2,1,0:T(8,128)S(1)} %get-tuple-element.76), channel_id=1, source_target_pairs={{0,8},{8,0},{16,24},{24,16},{32,40},{40,32},{48,56},{56,48},{64,72... | collective-permute-start | bytes 466952 | tf_op jit(solution)/shard_map/ppermute | solution.py:869
  18.7 0.1 stack.23.meta_ref
  18.8 0.0 copy-done
  18.8 2.0 %fine_head.1 = (f32[8,2,8,256]{3,2,1,0:T(8,128)S(1)}, f32[8,3,2,8,256]{4,3,2,1,0:T(8,128)S(1)}, f32[8,12,2,8,256]{4,3,2,1,0:T(8,128)S(1)}, f32[8,3,2,8,256]{4,3,...) custom-call(s32[5]{0:T(128)S(1)} %stack.23.meta_ref, ...), custom_call_target="tpu_custom_call" | custom-call | tf_op jit(solution)/shard_map/fine_head/pallas_call | solution.py:818
  20.8 0.0 collective-permute-done.3.far_ref
  20.8 0.0 collective-permute-done.2.pair_ref
  20.9 2.5 %fine.1 = (f32[8,4,4,8,128]{4,3,2,1,0:T(8,128)}, f32[3,3,2,8,256]{4,3,2,1,0:T(8,128)S(1)}, f32[2,8,256]{2,1,0:T(8,128)S(1)}, f32[1,2,8,128]{3,2,1,0:T(8,128)S(1)}) custom-call(s32[5]{0:T(128)S(1)} %stack.23.meta_ref, f32[8,2,8,256]{3,2,1,0:T(8,128)S(1)} %get-tuple-element.40.own_scale, f32[8,3,2,8,256]{4,3,2,1,0:T(8,128)S(1)} %get-tuple-element.42.own_res, ...), custom_call_target="tpu_custom_call" | custom-call | tf_op jit(solution)/shard_map/fine/pallas_call | solution.py:818
  23.3 6.4 %all-to-all-start = ((f32[8,4,4,8,128]{4,3,2,1,0:T(8,128)}), f32[8,4,4,8,128]{4,3,2,1,0:T(8,128)S(1)}, u32[]{:S(2)}, u32[]{:S(2)}) async-start(f32[8,4,4,8,128]{4,3,2,1,0:T(8,128)} %get-tuple-element.52), calls=%async_computation | async-start | bytes 1048576 | tf_op jit(solution)/shard_map/all_to_all | solution.py:887
  29.8 9.5 %all-to-all-done = f32[8,4,4,8,128]{4,3,2,1,0:T(8,128)S(1)} async-done(((f32[8,4,4,8,128]{4,3,2,1,0:T(8,128)}), f32[8,4,4,8,128]{4,3,2,1,0:T(8,128)S(1)}, u32[]{:S(2)}, u32[]{:S(2)}) %all-to-all-start) | async-done | bytes 524320 | tf_op jit(solution)/shard_map/all_to_all | solution.py:887
  39.3 2.7 %collective-permute-start.4 = (f32[18,4,8,128]{3,2,1,0:T(8,128)S(1)}, f32[18,4,8,128]{3,2,1,0:T(8,128)S(1)}, u32[]{:S(2)}, u32[]{:S(2)}) collective-permute-start(f32[18,4,8,128]{3,2,1,0:T(8,128)S(1)} %constant_dynamic-slice_fusion), channel_id=1, source_target_pairs={{0,64},{8,72},{16,80},{24,88},{32,96},{40,104},{48,112},{56,120},{... | collective-permute-start | bytes 884744 | tf_op jit(solution)/shard_map/ppermute | solution.py:890
  42.0 6.2 %head.1 = (f32[50,3,8,128]{3,2,1,0:T(8,128)S(1)}, f32[50,3,8,128]{3,2,1,0:T(8,128)S(1)}, f32[3,50,8,128]{3,2,1,0:T(8,128)S(1)}, f32[3,54,8,128]{3,2,1,0:T(8,128)...) custom-call(s32[5]{0:T(128)S(1)} %stack.23.meta_ref, ...), custom_call_target="tpu_custom_call" | custom-call | tf_op jit(solution)/shard_map/head/pallas_call | solution.py:818
  48.2 0.3 collective-permute-done.4.side_ref
  48.5 5.3 %tail.1 = (f32[8,6,2,8,128]{4,3,2,1,0:T(8,128)S(1)}, f32[50,3,8,128]{3,2,1,0:T(8,128)S(1)}, f32[50,3,8,128]{3,2,1,0:T(8,128)S(1)}, f32[3,50,8,128]{3,2,1,0:T(8,1...) custom-call(s32[5]{0:T(128)S(1)} %stack.23.meta_ref, ...), custom_call_target="tpu_custom_call", output_to_operand_aliasing={{1}: (2, {}), {2}: (3, {}), {3}: (4, {}), {4}: (5, {}), {5}... | custom-call | tf_op jit(solution)/shard_map/tail/pallas_call | solution.py:818
  53.8 12.2 %all_to_all.10.in_ref = f32[8,6,2,8,128]{4,3,2,1,0:T(8,128)S(1)} all-to-all(f32[8,6,2,8,128]{4,3,2,1,0:T(8,128)S(1)} %get-tuple-element.66), channel_id=1, replica_groups={{0,8,16,24,32,40,48,56},{64,72,80,88,96,104,112,120},{1,9,17,25,33,41,4..., dimensions={0} | all-to-all | bytes 786432 | tf_op jit(solution)/shard_map/all_to_all | solution.py:903
  66.0 2.1 %last.1 = f32[3,128,128]{2,1,0:T(8,128)} custom-call(f32[8,5,2,8,128]{4,3,2,1,0:T(8,128)S(1)} %copy-done, f32[8,3,2,8,256]{4,3,2,1,0:T(8,128)S(1)} %get-tuple-element.39.own_value, f32[8,2,8,256]{3,2,1,0:T(8,128)S(1)} %get-tuple-element.40.own_scale, f32[8,2,8,128]{3,2,1,0:T(8,128)S(1)} %get-tuple-element.41.own_gain, ...), custom_call_target="tpu_custom_call" | custom-call | tf_op jit(solution)/shard_map/last/pallas_call | solution.py:818
  (9 shorter events, 0.1 us)
Async XLA Ops:
  1.9 16.9 %copy-start = (f32[8,5,2,8,128]{4,3,2,1,0:T(8,128)S(1)}, f32[8,5,2,8,128]{4,3,2,1,0:T(8,128)}, u32[]{:S(2)}) copy-start(f32[8,5,2,8,128]{4,3,2,1,0:T(8,128)} %get-tuple-element.36.own_ref) | copy-start | bytes 983044
  1.9 7.6 %collective-permute-start = (f32[4,3,2,8,128]{4,3,2,1,0:T(8,128)}, f32[4,3,2,8,128]{4,3,2,1,0:T(8,128)S(1)}, u32[]{:S(2)}, u32[]{:S(2)}) collective-permute-start(f32[4,3,2,8,128]{4,3,2,1,0:T(8,128)} %get-tuple-element.37), channel_id=1, source_target_pairs={{1,0},{2,1},{3,2},{4,3},{5,4},{6,5},{7,6},{0,7},{9,8},{10,9},{11,1... | collective-permute-start | bytes 294920 | tf_op jit(solution)/shard_map/ppermute | solution.py:855
  7.6 5.8 %collective-permute-start.1 = (f32[4,3,2,8,128]{4,3,2,1,0:T(8,128)}, f32[4,3,2,8,128]{4,3,2,1,0:T(8,128)S(1)}, u32[]{:S(2)}, u32[]{:S(2)}) collective-permute-start(f32[4,3,2,8,128]{4,3,2,1,0:T(8,128)} %get-tuple-element.38), channel_id=1, source_target_pairs={{0,1},{1,2},{2,3},{3,4},{4,5},{5,6},{6,7},{7,0},{8,9},{9,10},{10,1... | collective-permute-start | bytes 294920 | tf_op jit(solution)/shard_map/ppermute | solution.py:856
  13.4 7.4 %collective-permute-start.3 = (f32[19,2,8,128]{3,2,1,0:T(8,128)S(1)}, f32[19,2,8,128]{3,2,1,0:T(8,128)S(1)}, u32[]{:S(2)}, u32[]{:S(2)}) collective-permute-start(f32[19,2,8,128]{3,2,1,0:T(8,128)S(1)} %get-tuple-element.75), channel_id=1, source_target_pairs={{8,16},{24,32},{40,48},{56,64},{72,80},{88,96},{104,112},{120,0},{... | collective-permute-start | bytes 466952 | tf_op jit(solution)/shard_map/ppermute | solution.py:868
  16.7 4.1 %collective-permute-start.2 = (f32[19,2,8,128]{3,2,1,0:T(8,128)S(1)}, f32[19,2,8,128]{3,2,1,0:T(8,128)S(1)}, u32[]{:S(2)}, u32[]{:S(2)}) collective-permute-start(f32[19,2,8,128]{3,2,1,0:T(8,128)S(1)} %get-tuple-element.76), channel_id=1, source_target_pairs={{0,8},{8,0},{16,24},{24,16},{32,40},{40,32},{48,56},{56,48},{64,72... | collective-permute-start | bytes 466952 | tf_op jit(solution)/shard_map/ppermute | solution.py:869
  23.3 15.9 %all-to-all-start = ((f32[8,4,4,8,128]{4,3,2,1,0:T(8,128)}), f32[8,4,4,8,128]{4,3,2,1,0:T(8,128)S(1)}, u32[]{:S(2)}, u32[]{:S(2)}) async-start(f32[8,4,4,8,128]{4,3,2,1,0:T(8,128)} %get-tuple-element.52), calls=%async_computation | async-start | bytes 1048576 | tf_op jit(solution)/shard_map/all_to_all | solution.py:887
  39.3 9.2 %collective-permute-start.4 = (f32[18,4,8,128]{3,2,1,0:T(8,128)S(1)}, f32[18,4,8,128]{3,2,1,0:T(8,128)S(1)}, u32[]{:S(2)}, u32[]{:S(2)}) collective-permute-start(f32[18,4,8,128]{3,2,1,0:T(8,128)S(1)} %constant_dynamic-slice_fusion), channel_id=1, source_target_pairs={{0,64},{8,72},{16,80},{24,88},{32,96},{40,104},{48,112},{56,120},{... | collective-permute-start | bytes 884744 | tf_op jit(solution)/shard_map/ppermute | solution.py:890
